TPU v7x, 32 devices: a whole 2x2x4 slice. The times are simulated.
32 devices in a mesh: fsdp: 4 (over y, x), frame: 8 (over z, core).
Axes of the slice: x: 2, y: 2, z: 4, core: 2. Of those that a mesh axis runs over, the one named last changes fastest.
Arguments:
- queries: bfloat16 [8, 512, 1024], P('frame', 'fsdp'), may hold values from -5 to 5
- key_rows: bfloat16 [8, 512, 1024], P('frame', 'fsdp'), may hold values from -5 to 5
- value_rows: bfloat16 [8, 512, 1024], P('frame', 'fsdp'), may hold values from -6 to 6
- out_weight: bfloat16 [1024, 2048], P(('fsdp', 'frame')), may hold values from -0.75 to 0.75
- conv_weight: bfloat16 [31, 2048], replicated, may hold values from -1 to 1
- grad_out: bfloat16 [8, 512, 2048], P('frame', 'fsdp'), may hold values from -6 to 6
Outputs:
- block_out: bfloat16 [8, 512, 2048], P('frame', 'fsdp')
- grad_queries: bfloat16 [8, 512, 1024], P('frame', 'fsdp')
- grad_keys: bfloat16 [8, 512, 1024], P('frame', 'fsdp')
- grad_values: bfloat16 [8, 512, 1024], P('frame', 'fsdp')
- weight_grad: float32 [1024, 2048], P(('fsdp', 'frame'))
- conv_grad: float32 [31, 2048], replicated
All inputs are finite; a program needn't handle non-finite values.
Results may differ from a plain program's by a relative error of at most 0.014.
Values may be sent and summed in bfloat16 or wider, within the bound.
No kernel may reach another device: no remote copies, remote signals or barrier semaphores. Data moves between devices by JAX's collectives and lax.ppermute only.
A program may use at most 128 MiB of HBM per device.

v0:
```python
import math

import jax
import jax.numpy as jnp
from jax import lax
from jax.sharding import PartitionSpec as P

HDIM = 128
KERNEL = 31
INNER = 1024


def with_halo(cells, sides, width):
    for axis, dim in sides:
        count = lax.axis_size(axis)
        ends = count - 1
        head = lax.slice_in_dim(cells, 0, width, axis=dim)
        tail = lax.slice_in_dim(cells, cells.shape[dim] - width, cells.shape[dim], axis=dim)
        cells = jnp.concatenate(
            [
                lax.ppermute(tail, axis, [(i, (i + 1) % count) for i in range(ends)]),
                cells,
                lax.ppermute(head, axis, [((i + 1) % count, i) for i in range(ends)]),
            ],
            axis=dim,
        )
    return cells


def head_scores(queries, key_rows):
    return jnp.einsum("qd,kd->qk", queries, key_rows, preferred_element_type=jnp.float32) * (
        1.0 / math.sqrt(HDIM)
    )


def forward_head(queries, key_rows, value_rows):
    scores = head_scores(queries, key_rows)
    row_max = jnp.max(scores, axis=1)
    exponent = jnp.exp(scores - row_max[:, None])
    row_sum = jnp.sum(exponent, axis=1)
    rounded = (exponent / row_sum[:, None]).astype(jnp.bfloat16)
    attended = jnp.dot(rounded, value_rows, preferred_element_type=jnp.float32).astype(jnp.bfloat16)
    return (attended, row_max, row_sum)


def score_grads(queries, key_rows, value_rows, upstream, row_max, row_sum, row_dot):
    scores = head_scores(queries, key_rows)
    weights = jnp.exp(scores - row_max[:, None]) / row_sum[:, None]
    grad_probs = jnp.einsum("qd,kd->qk", upstream, value_rows, preferred_element_type=jnp.float32)
    row_dot = jnp.sum(weights * grad_probs, axis=1)
    grad_scores = (weights * (grad_probs - row_dot[:, None])).astype(jnp.bfloat16)
    return (weights, grad_scores, row_dot)


def query_grad(grad_scores, key_rows):
    product = jnp.dot(grad_scores, key_rows, preferred_element_type=jnp.float32)
    return (product * (1.0 / math.sqrt(HDIM))).astype(jnp.bfloat16)


def key_grads(queries, weights, grad_scores, upstream):
    grad_key = jnp.einsum("qk,qd->kd", grad_scores, queries, preferred_element_type=jnp.float32) * (
        1.0 / math.sqrt(HDIM)
    )
    grad_value = jnp.einsum(
        "qk,qd->kd", weights.astype(jnp.bfloat16), upstream, preferred_element_type=jnp.float32
    )
    return (grad_key, grad_value)


def block_length():
    return 512


def head_forward_blocks(queries, key_rows, value_rows):
    length = queries.shape[0]
    block_rows = block_length()
    q_blocks = queries.reshape(length // block_rows, block_rows, HDIM)
    attended, row_max, row_sum = lax.map(
        lambda q_block: forward_head(q_block, key_rows, value_rows), q_blocks
    )
    return (attended.reshape(length, HDIM), row_max.reshape(length), row_sum.reshape(length))


def head_backward_blocks(queries, key_rows, value_rows, upstream, row_max, row_sum):
    length = queries.shape[0]
    block_rows = block_length()
    count_blocks = length // block_rows

    def advance(running, inputs):
        q_block, g_block, max_block, sum_block = inputs
        weights, grad_scores, row_dot = score_grads(
            q_block, key_rows, value_rows, g_block, max_block, sum_block, None
        )
        grad_key, grad_value = key_grads(q_block, weights, grad_scores, g_block)
        return ((running[0] + grad_key, running[1] + grad_value), query_grad(grad_scores, key_rows))

    empty_sum = jnp.zeros((key_rows.shape[0], HDIM), jnp.float32)
    inputs = (
        queries.reshape(count_blocks, block_rows, HDIM),
        upstream.reshape(count_blocks, block_rows, HDIM),
        row_max.reshape(count_blocks, block_rows),
        row_sum.reshape(count_blocks, block_rows),
    )
    key_sums, grad_query = lax.scan(advance, (empty_sum, empty_sum), inputs)
    return (
        grad_query.reshape(length, HDIM),
        key_sums[0].astype(jnp.bfloat16),
        key_sums[1].astype(jnp.bfloat16),
    )


def depthwise(signal, taps):
    channels = signal.shape[1]
    result = lax.conv_general_dilated(
        signal[None],
        taps[:, None, :],
        (1,),
        "VALID",
        dimension_numbers=("NWC", "WIO", "NWC"),
        feature_group_count=channels,
        precision=lax.Precision.HIGHEST,
        preferred_element_type=jnp.float32,
    )
    return result[0]


def shards(queries, key_rows, value_rows, out_weight, conv_weight, grad_out):
    local_rows = queries.shape[1]
    half_width = KERNEL // 2
    own_queries = queries[0]
    own_keys = key_rows[0]
    own_values = value_rows[0]
    upstream = grad_out[0].astype(jnp.float32)
    full_weight = lax.all_gather(out_weight, ("fsdp", "frame"), axis=0, tiled=True)
    groups = lax.axis_size("fsdp")
    group_width = INNER // groups
    local_heads = group_width // HDIM
    exchanged = (
        lax.all_to_all(
            own_queries.reshape(local_rows, groups, group_width),
            "fsdp",
            split_axis=1,
            concat_axis=0,
            tiled=True,
        ),
        lax.all_to_all(
            own_keys.reshape(local_rows, groups, group_width),
            "fsdp",
            split_axis=1,
            concat_axis=0,
            tiled=True,
        ),
        lax.all_to_all(
            own_values.reshape(local_rows, groups, group_width),
            "fsdp",
            split_axis=1,
            concat_axis=0,
            tiled=True,
        ),
    )
    span_rows = exchanged[0].shape[0]
    head_queries = exchanged[0].reshape(span_rows, group_width)
    head_keys = exchanged[1].reshape(span_rows, group_width)
    head_values = exchanged[2].reshape(span_rows, group_width)
    pieces = []
    maxima = []
    row_sums = []
    for head_index in range(local_heads):
        columns = slice(head_index * HDIM, (head_index + 1) * HDIM)
        attended, row_max, row_sum = head_forward_blocks(
            head_queries[:, columns], head_keys[:, columns], head_values[:, columns]
        )
        pieces.append(attended)
        maxima.append(row_max)
        row_sums.append(row_sum)
    head_attention = jnp.concatenate(pieces, axis=1)
    attention = lax.all_to_all(
        head_attention.reshape(span_rows, 1, group_width),
        "fsdp",
        split_axis=0,
        concat_axis=1,
        tiled=True,
    ).reshape(local_rows, INNER)
    projected = jnp.dot(attention, full_weight, preferred_element_type=jnp.float32).astype(
        jnp.bfloat16
    )
    padded = with_halo(projected[None], (("fsdp", 1),), half_width)[0].astype(jnp.float32)
    conv_taps = conv_weight.astype(jnp.float32)
    conv_value = depthwise(padded, conv_taps)
    sigmoid_conv = jax.nn.sigmoid(conv_value)
    block_out = (padded[half_width : half_width + local_rows] + conv_value * sigmoid_conv).astype(
        jnp.bfloat16
    )
    grad_conv = (upstream * sigmoid_conv * (1.0 + conv_value * (1.0 - sigmoid_conv))).astype(
        jnp.bfloat16
    )
    grad_padded = with_halo(grad_conv[None], (("fsdp", 1),), half_width)[0].astype(jnp.float32)
    grad_projected = (upstream + depthwise(grad_padded, conv_taps[::-1])).astype(jnp.bfloat16)
    conv_terms = depthwise(padded, grad_conv.astype(jnp.float32))
    total_frames = local_rows * groups * lax.axis_size("frame")
    grad_scale = 1.0 / math.sqrt(total_frames)
    conv_grad = lax.psum(conv_terms, ("fsdp", "frame")) * grad_scale
    weight_grad = (
        lax.psum_scatter(
            jnp.einsum("ri,rd->id", attention, grad_projected, preferred_element_type=jnp.float32),
            ("fsdp", "frame"),
            scatter_dimension=0,
            tiled=True,
        )
        * grad_scale
    )
    grad_attention = jnp.einsum(
        "rd,id->ri", grad_projected, full_weight, preferred_element_type=jnp.float32
    ).astype(jnp.bfloat16)
    head_grads = lax.all_to_all(
        grad_attention.reshape(local_rows, groups, group_width),
        "fsdp",
        split_axis=1,
        concat_axis=0,
        tiled=True,
    ).reshape(span_rows, group_width)
    query_list = []
    key_list = []
    value_list = []
    for head_index in range(local_heads):
        columns = slice(head_index * HDIM, (head_index + 1) * HDIM)
        grad_query, grad_key, grad_value = head_backward_blocks(
            head_queries[:, columns],
            head_keys[:, columns],
            head_values[:, columns],
            head_grads[:, columns],
            maxima[head_index],
            row_sums[head_index],
        )
        query_list.append(grad_query)
        key_list.append(grad_key)
        value_list.append(grad_value)
    returned = (
        lax.all_to_all(
            jnp.concatenate(query_list, axis=1).reshape(span_rows, 1, group_width),
            "fsdp",
            split_axis=0,
            concat_axis=1,
            tiled=True,
        ),
        lax.all_to_all(
            jnp.concatenate(key_list, axis=1).reshape(span_rows, 1, group_width),
            "fsdp",
            split_axis=0,
            concat_axis=1,
            tiled=True,
        ),
        lax.all_to_all(
            jnp.concatenate(value_list, axis=1).reshape(span_rows, 1, group_width),
            "fsdp",
            split_axis=0,
            concat_axis=1,
            tiled=True,
        ),
    )
    grad_queries = returned[0].reshape(local_rows, INNER)
    grad_keys = returned[1].reshape(local_rows, INNER)
    grad_values = returned[2].reshape(local_rows, INNER)
    return (
        block_out[None],
        grad_queries[None],
        grad_keys[None],
        grad_values[None],
        weight_grad,
        conv_grad,
    )


def solution(mesh):
    return jax.shard_map(
        shards,
        mesh=mesh,
        in_specs=(
            P("frame", "fsdp", None),
            P("frame", "fsdp", None),
            P("frame", "fsdp", None),
            P(("fsdp", "frame"), None),
            P(),
            P("frame", "fsdp", None),
        ),
        out_specs=(
            P("frame", "fsdp", None),
            P("frame", "fsdp", None),
            P("frame", "fsdp", None),
            P("frame", "fsdp", None),
            P(("fsdp", "frame"), None),
            P(),
        ),
        check_vma=False,
    )
```

profile of v0, /device:TPU:0, one launch (start us, length us, event | category | flops | bytes accessed | tf_op | source)
XLA Modules:
  0.0 402.2 jit_solution(11246321883372407034)
XLA Ops:
  9.7 5.2 %all-to-all-start = ((bf16[128,4,256]{0,2,1:T(8,128)(2,1)}), bf16[128,4,256]{0,2,1:T(8,128)(2,1)S(1)}, u32[]{:S(2)}, u32[]{:S(2)}) async-start(bf16[128,4,256]{0,2,1:T(8,128)(2,1)} %bitcast), calls=%async_computation | async-start | bytes 524288 | tf_op jit(solution)/shard_map/all_to_all | solution.py:139
  15.7 4.5 %all-to-all-done = bf16[128,4,256]{0,2,1:T(8,128)(2,1)S(1)} async-done(((bf16[128,4,256]{0,2,1:T(8,128)(2,1)}), bf16[128,4,256]{0,2,1:T(8,128)(2,1)S(1)}, u32[]{:S(2)}, u32[]{:S(2)}) %all-to-all-start) | async-done | bytes 262176 | tf_op jit(solution)/shard_map/all_to_all | solution.py:139
  20.2 3.4 all-to-all-start.1
  24.5 4.5 %all-to-all-done.1 = bf16[128,4,256]{0,2,1:T(8,128)(2,1)S(1)} async-done(((bf16[128,4,256]{0,2,1:T(8,128)(2,1)}), bf16[128,4,256]{0,2,1:T(8,128)(2,1)S(1)}, u32[]{:S(2)}, u32[]{:S(2)}) %all-to-all-start.1) | async-done | bytes 262176 | tf_op jit(solution)/shard_map/all_to_all | solution.py:146
  29.0 3.4 all-to-all-start.2
  32.8 5.0 %all-to-all-done.2 = bf16[128,4,256]{0,2,1:T(8,128)(2,1)S(1)} async-done(((bf16[128,4,256]{0,2,1:T(8,128)(2,1)}), bf16[128,4,256]{0,2,1:T(8,128)(2,1)S(1)}, u32[]{:S(2)}, u32[]{:S(2)}) %all-to-all-start.2) | async-done | bytes 262176 | tf_op jit(solution)/shard_map/all_to_all | solution.py:153
  41.2 8.1 %all_to_all.120 = bf16[4,2,16384]{2,1,0:T(2,128)(2,1)S(1)} all-to-all(bf16[4,2,16384]{2,1,0:T(2,128)(2,1)S(1)} %reshape.170), channel_id=1, replica_groups=mesh['fsdp'=4,'frame'=8] {'fsdp'}, dimensions={0} | all-to-all | bytes 524288 | tf_op jit(solution)/shard_map/all_to_all | solution.py:177
  51.5 24.9 %all-gather.2.cloned.1.call-done = bf16[1024,2048]{1,0:T(8,128)(2,1)} async-done(((bf16[32,2048]{1,0:T(8,128)(2,1)}), bf16[1024,2048]{1,0:T(8,128)(2,1)}) %all-gather.2.cloned.1.call-update) | async-done | bytes 4194320 | tf_op jit(solution)/shard_map/all_gather | solution.py:134
  76.4 3.0 convolution_convert_fusion
  80.0 3.8 collective-permute-start
  85.1 5.0 %rev.3 = f32[31,2048]{1,0:T(8,128)} reverse(bf16[31,2048]{1,0:T(8,128)(2,1)S(1)} %copy-done.9), dimensions={0} | reverse | bytes 380928 | tf_op jit(solution)/shard_map/rev | solution.py:198
  91.3 8.1 %multiply_convert_fusion.2 = (bf16[1,128,2048]{2,0,1:T(2,128)(2,1)S(1)}, f32[1,128,2048]{2,0,1:T(1,128)S(1)}) fusion(bf16[1,128,2048]{2,1,0:T(8,128)(2,1)S(1)} %copy-done.11, bf16[31,1,2048]{2,0,1:T(8,128)(2,1)S(1)} %bitcast.144, bf16[1,158,2048]{2,1,0:T(8,128)(2,1)S(1)} %pad_maximum_fusion), kind=kOutput, calls=%fused_computation.44 | convolution fusion | flops 18874368 | bytes 2871296 | tf_op jit(solution)/shard_map/conv_general_dilated | solution.py:114
  100.6 5.1 %collective-permute-start.2 = (bf16[1,15,2048]{2,0,1:T(2,128)(2,1)}, bf16[1,15,2048]{2,0,1:T(2,128)(2,1)}, u32[]{:S(2)}, u32[]{:S(2)}) collective-permute-start(bf16[1,15,2048]{2,0,1:T(2,128)(2,1)} %get-tuple-element.84), channel_id=1, source_target_pairs={{0,8},{8,16},{16,24},{1,9},{9,17},{17,25},{2,10},{10,18},{18,26},{... | collective-permute-start | bytes 184328 | tf_op jit(solution)/shard_map/ppermute | solution.py:21
  107.0 7.4 %fusion.19 = f32[1,31,2048]{2,0,1:T(1,128)S(1)} fusion(f32[1,128,2048]{2,0,1:T(1,128)S(1)} %get-tuple-element.103, bf16[1,158,2048]{2,1,0:T(8,128)(2,1)S(1)} %pad_maximum_fusion, bf16[1,128,2048]{2,1,0:T(8,128)(2,1)S(1)} %copy-done.11), kind=kOutput, calls=%fused_computation.38 | convolution fusion | flops 18874368 | bytes 2473984 | tf_op jit(solution)/shard_map/conv_general_dilated | solution.py:114
  115.3 6.9 %fusion = bf16[1,128,2048]{2,0,1:T(2,128)(2,1)S(1)} fusion(bf16[1,15,2048]{2,0,1:T(2,128)(2,1)} %collective-permute-done.3, bf16[1,128,2048]{2,0,1:T(2,128)(2,1)} %copy-done.10, bf16[1,15,2048]{2,0,1:T(2,128)(2,1)} %collective-permute-done.2, bf16[1,128,2048]{2,1,0:T(8,128)(2,1)} %param.11, f32[31,1,2048]{2,0,1:T(8,128)} %bitcast.135), kind=kOutput, calls=%fused_computation.2 | convolution fusion | flops 100245504 | bytes 1949696 | tf_op jit(solution)/shard_map/conv_general_dilated | solution.py:114
  123.2 4.5 %fusion.30 = f32[1024,2048]{1,0:T(8,128)} fusion(bf16[128,1024]{0,1:T(8,128)(2,1)S(1)} %bitcast.114, bf16[1,128,2048]{2,0,1:T(2,128)(2,1)S(1)} %fusion), kind=kOutput, calls=%fused_computation.56 | convolution fusion | flops 536870912 | bytes 9175040 | tf_op jit(solution)/shard_map/ri,rd->id/dot_general | solution.py:205
  127.8 4.1 %convolution_convert_fusion.1 = bf16[128,1024]{1,0:T(8,128)(2,1)S(1)} fusion(bf16[1024,2048]{1,0:T(8,128)(2,1)} %all-gather.2.cloned.1.call-done, bf16[1,128,2048]{2,0,1:T(2,128)(2,1)} %copy-done), kind=kOutput, calls=%fused_computation.10 | convolution fusion | flops 537001984 | bytes 4980736 | tf_op jit(solution)/shard_map/rd,id->ri/dot_general | solution.py:212
  132.6 4.7 %all-to-all-start.4 = ((bf16[128,4,256]{2,0,1:T(8,128)(2,1)}), bf16[128,4,256]{2,0,1:T(8,128)(2,1)S(1)}, u32[]{:S(2)}, u32[]{:S(2)}) async-start(bf16[128,4,256]{2,0,1:T(8,128)(2,1)} %bitcast.109), calls=%async_computation.4 | async-start | bytes 524288 | tf_op jit(solution)/shard_map/all_to_all | solution.py:215
  145.5 3.6 all-to-all-start.7
  154.3 4.0 all-to-all-start.5
  160.3 3.3 all-to-all-done.5
  163.7 3.4 all-to-all-start.6
  167.1 73.9 %all-reduce.2.cloned.1.call-done = f32[31,2048]{1,0:T(8,128)} async-done(((f32[31,2048]{1,0:T(8,128)}), f32[31,2048]{1,0:T(8,128)}) %all-reduce.2.cloned.1.call-update) | async-done | bytes 253968 | tf_op jit(solution)/shard_map/psum | solution.py:202
  246.7 147.3 %reduce-scatter.2.cloned.1.call-done = f32[32,2048]{1,0:T(8,128)} async-done(((f32[1024,2048]{1,0:T(8,128)}), f32[32,2048]{1,0:T(8,128)}) %reduce-scatter.2.cloned.1.call-update) | async-done | bytes 262160 | tf_op jit(solution)/shard_map/reduce_scatter | solution.py:204
  (101 shorter events, 40.9 us)
Async XLA Ops:
  7.2 7.7 %copy-start.2 = (bf16[1,128,1024]{2,1,0:T(8,128)(2,1)S(1)}, bf16[1,128,1024]{2,1,0:T(8,128)(2,1)}, u32[]{:S(2)}) copy-start(bf16[1,128,1024]{2,1,0:T(8,128)(2,1)} %param.7) | copy-start | bytes 786436
  7.2 16.5 %copy-start.3 = (bf16[1,128,1024]{2,1,0:T(8,128)(2,1)S(1)}, bf16[1,128,1024]{2,1,0:T(8,128)(2,1)}, u32[]{:S(2)}) copy-start(bf16[1,128,1024]{2,1,0:T(8,128)(2,1)} %param.8) | copy-start | bytes 786436
  7.2 69.2 %all-gather.2.cloned.1.call-start = ((), (), s32[]{:S(2)}) async-start(), calls=%async_computation.9 | async-start | bytes 4325376 | tf_op jit(solution)/shard_map/all_gather | solution.py:134
  9.7 10.5 %all-to-all-start = ((bf16[128,4,256]{0,2,1:T(8,128)(2,1)}), bf16[128,4,256]{0,2,1:T(8,128)(2,1)S(1)}, u32[]{:S(2)}, u32[]{:S(2)}) async-start(bf16[128,4,256]{0,2,1:T(8,128)(2,1)} %bitcast), calls=%async_computation | async-start | bytes 524288 | tf_op jit(solution)/shard_map/all_to_all | solution.py:139
  20.2 8.8 %all-to-all-start.1 = ((bf16[128,4,256]{0,2,1:T(8,128)(2,1)}), bf16[128,4,256]{0,2,1:T(8,128)(2,1)S(1)}, u32[]{:S(2)}, u32[]{:S(2)}) async-start(bf16[128,4,256]{0,2,1:T(8,128)(2,1)} %bitcast.4), calls=%async_computation.1 | async-start | bytes 524288 | tf_op jit(solution)/shard_map/all_to_all | solution.py:146
  29.0 8.8 %all-to-all-start.2 = ((bf16[128,4,256]{0,2,1:T(8,128)(2,1)}), bf16[128,4,256]{0,2,1:T(8,128)(2,1)S(1)}, u32[]{:S(2)}, u32[]{:S(2)}) async-start(bf16[128,4,256]{0,2,1:T(8,128)(2,1)} %bitcast.8), calls=%async_computation.2 | async-start | bytes 524288 | tf_op jit(solution)/shard_map/all_to_all | solution.py:153
  32.4 208.5 %all-reduce.2.cloned.1.call-start = ((), (), s32[]{:S(2)}) async-start(), calls=%async_computation.11 | async-start | bytes 524288 | tf_op jit(solution)/shard_map/psum | solution.py:202
  37.9 1.4 copy-start.4
  76.4 8.7 %copy-start.9 = (bf16[31,2048]{1,0:T(8,128)(2,1)S(1)}, bf16[31,2048]{1,0:T(8,128)(2,1)}, u32[]{:S(2)}) copy-start(bf16[31,2048]{1,0:T(8,128)(2,1)} %param.10) | copy-start | bytes 380932
  80.0 10.1 %collective-permute-start = (bf16[1,15,2048]{2,1,0:T(8,128)(2,1)}, bf16[1,15,2048]{2,1,0:T(8,128)(2,1)}, u32[]{:S(2)}, u32[]{:S(2)}) collective-permute-start(bf16[1,15,2048]{2,1,0:T(8,128)(2,1)} %get-tuple-element.96), channel_id=1, source_target_pairs={{0,8},{8,16},{16,24},{1,9},{9,17},{17,25},{2,10},{10,18},{18,26},{... | collective-permute-start | bytes 184328 | tf_op jit(solution)/shard_map/ppermute | solution.py:21
  83.8 6.5 %collective-permute-start.1 = (bf16[1,15,2048]{2,1,0:T(8,128)(2,1)}, bf16[1,15,2048]{2,1,0:T(8,128)(2,1)}, u32[]{:S(2)}, u32[]{:S(2)}) collective-permute-start(bf16[1,15,2048]{2,1,0:T(8,128)(2,1)} %get-tuple-element.97), channel_id=1, source_target_pairs={{8,0},{16,8},{24,16},{9,1},{17,9},{25,17},{10,2},{18,10},{26,18},{... | collective-permute-start | bytes 184328 | tf_op jit(solution)/shard_map/ppermute | solution.py:23
  90.1 1.2 copy-start.11
  99.5 7.5 %copy-start.10 = (bf16[1,128,2048]{2,0,1:T(2,128)(2,1)}, bf16[1,128,2048]{2,0,1:T(2,128)(2,1)S(1)}, u32[]{:S(2)}) copy-start(bf16[1,128,2048]{2,0,1:T(2,128)(2,1)S(1)} %get-tuple-element.102) | copy-start | bytes 1572868
  99.5 15.0 %copy-start.1 = (f32[1,128,2048]{2,0,1:T(1,128)}, f32[1,128,2048]{2,0,1:T(1,128)S(1)}, u32[]{:S(2)}) copy-start(f32[1,128,2048]{2,0,1:T(1,128)S(1)} %get-tuple-element.103) | copy-start | bytes 3145732
  100.6 14.7 %collective-permute-start.2 = (bf16[1,15,2048]{2,0,1:T(2,128)(2,1)}, bf16[1,15,2048]{2,0,1:T(2,128)(2,1)}, u32[]{:S(2)}, u32[]{:S(2)}) collective-permute-start(bf16[1,15,2048]{2,0,1:T(2,128)(2,1)} %get-tuple-element.84), channel_id=1, source_target_pairs={{0,8},{8,16},{16,24},{1,9},{9,17},{17,25},{2,10},{10,18},{18,26},{... | collective-permute-start | bytes 184328 | tf_op jit(solution)/shard_map/ppermute | solution.py:21
  105.7 9.6 %collective-permute-start.3 = (bf16[1,15,2048]{2,0,1:T(2,128)(2,1)S(1)}, bf16[1,15,2048]{2,0,1:T(2,128)(2,1)}, u32[]{:S(2)}, u32[]{:S(2)}) collective-permute-start(bf16[1,15,2048]{2,0,1:T(2,128)(2,1)S(1)} %get-tuple-element.85), channel_id=1, source_target_pairs={{8,0},{16,8},{24,16},{9,1},{17,9},{25,17},{10,2},{18,10},{26,18},{... | collective-permute-start | bytes 184328 | tf_op jit(solution)/shard_map/ppermute | solution.py:23
  115.3 278.7 %reduce-scatter.2.cloned.1.call-start = ((), (), s32[]{:S(2)}) async-start(), calls=%async_computation.10 | async-start | bytes 8650752 | tf_op jit(solution)/shard_map/reduce_scatter | solution.py:204
  122.2 1.0 copy-start
  132.6 10.1 %all-to-all-start.4 = ((bf16[128,4,256]{2,0,1:T(8,128)(2,1)}), bf16[128,4,256]{2,0,1:T(8,128)(2,1)S(1)}, u32[]{:S(2)}, u32[]{:S(2)}) async-start(bf16[128,4,256]{2,0,1:T(8,128)(2,1)} %bitcast.109), calls=%async_computation.4 | async-start | bytes 524288 | tf_op jit(solution)/shard_map/all_to_all | solution.py:215
  143.7 5.4 %copy-start.5 = (bf16[4,128,1,256]{3,1,0,2:T(8,128)(2,1)S(1)}, bf16[4,128,1,256]{3,1,0,2:T(8,128)(2,1)}, u32[]{:S(2)}) copy-start(bf16[4,128,1,256]{3,1,0,2:T(8,128)(2,1)} %copy-done.4) | copy-start | bytes 786436
  145.5 8.8 %all-to-all-start.7 = ((bf16[4,2,16384]{2,1,0:T(2,128)(2,1)}), bf16[4,2,16384]{2,1,0:T(2,128)(2,1)S(1)}, u32[]{:S(2)}, u32[]{:S(2)}) async-start(bf16[4,2,16384]{2,1,0:T(2,128)(2,1)} %reshape.176), calls=%async_computation.7 | async-start | bytes 524288 | tf_op jit(solution)/shard_map/all_to_all | solution.py:253
  150.3 1.0 copy-start.8
  154.3 9.4 %all-to-all-start.5 = ((bf16[4,2,16384]{2,1,0:T(2,128)(2,1)}), bf16[4,2,16384]{2,1,0:T(2,128)(2,1)S(1)}, u32[]{:S(2)}, u32[]{:S(2)}) async-start(bf16[4,2,16384]{2,1,0:T(2,128)(2,1)} %reshape.172), calls=%async_computation.5 | async-start | bytes 524288 | tf_op jit(solution)/shard_map/all_to_all | solution.py:239
  163.7 81.7 %all-to-all-start.6 = ((bf16[4,2,16384]{2,1,0:T(2,128)(2,1)}), bf16[4,2,16384]{2,1,0:T(2,128)(2,1)S(1)}, u32[]{:S(2)}, u32[]{:S(2)}) async-start(bf16[4,2,16384]{2,1,0:T(2,128)(2,1)} %reshape.174), calls=%async_computation.6 | async-start | bytes 524288 | tf_op jit(solution)/shard_map/all_to_all | solution.py:246
  (2 other events, 1.7 us)
Sparse Core Ops, SparseCore 0:
  11.0 65.3 all-gather.1
  115.4 125.5 all-reduce.1
  243.3 150.6 reduce-scatter.1
where the time goes:
time: 403 us; the launch traced here: 402 us
  waiting for transfers between devices  267 us (66%)
  starting transfers between devices  39.2 us (10%)
  matrix products  38.7 us (10%)
  local copies, waits for them, and re-layouts  23.6 us (6%)
  between operations  14.3 us (4%)
  other arithmetic  11.2 us (3%)
  blocking collectives  8.11 us (2%)
    reduce_scatter x1, waiting for transfers between devices, shards(): lax.psum_scatter(jnp.einsum('ri,rd->id', attention, grad_projected, prefe...  147 us
    psum x1, waiting for transfers between devices, shards(): conv_grad = lax.psum(conv_terms, ('fsdp', 'frame')) * grad_scale  73.9 us
    all_gather x1, waiting for transfers between devices, shards(): lax.all_gather(out_weight, ('fsdp', 'frame'), axis=0, tiled=True)  24.9 us
    conv_general_dilated x3, matrix products, depthwise(): lax.conv_general_dilated(signal[None], taps[:, None, :], (1,), 'VALID', d...  22.5 us
    unnamed x47, local copies, waits for them, and re-layouts  13.5 us
    ppermute x2, starting transfers between devices, with_halo(): lax.ppermute(tail, axis, [(i, (i + 1) % count) for i in range(ends)])  8.83 us
    all_to_all x1, blocking collectives, shards(): lax.all_to_all(head_attention.reshape(span_rows, 1, group_width), 'fsdp',...  8.11 us
  transfers between devices with their start and end apart: 14, of which 9 were waited for; matrix products, arithmetic and copies ran while one was open for 14% of the time, Pallas kernels for 0%

commit v1 on v0

v1 whole, which is shorter than its diff:
```python
import functools
import math

import jax
import jax.numpy as jnp
from jax import lax
from jax.experimental import pallas as pl
from jax.experimental.pallas import tpu as pltpu
from jax.sharding import PartitionSpec as P

HDIM = 128
KERNEL = 31
HALF = KERNEL // 2
LANES = 128
TILE = 64
TAPS = 32
F32 = jnp.float32
BF16 = jnp.bfloat16
ROOT = 1.0 / math.sqrt(HDIM)


def swap(cells, axis, mask):
    count = lax.axis_size(axis)
    return lax.ppermute(cells, axis, [(i, i ^ mask) for i in range(count)])


def call(body, outs, *operands, scratch=(), flops=0, loose=0):
    vmem = pl.BlockSpec(memory_space=pltpu.VMEM)
    in_specs = [vmem] * (len(operands) - loose) + [pl.BlockSpec(memory_space=pl.ANY)] * loose
    moved = sum(x.size * x.dtype.itemsize for x in operands[: len(operands) - loose])
    moved += sum(math.prod(s) * jnp.dtype(t).itemsize for s, t in outs)
    return pl.pallas_call(
        body,
        out_shape=[jax.ShapeDtypeStruct(s, t) for s, t in outs],
        in_specs=in_specs,
        out_specs=[vmem] * len(outs),
        scratch_shapes=list(scratch),
        cost_estimate=pl.CostEstimate(flops=flops, bytes_accessed=moved, transcendentals=0),
        compiler_params=pltpu.CompilerParams(vmem_limit_bytes=40 * 1024 * 1024),
    )(*operands)


def block(index, size, unit):
    return pl.ds(pl.multiple_of(index * size, unit), size)


def product(left, right, left_dim, right_dim):
    return lax.dot_general(
        left, right, (((left_dim,), (right_dim,)), ((), ())), preferred_element_type=F32
    )


def tree_sum(terms):
    while len(terms) > 1:
        terms = [terms[i] + terms[i + 1] for i in range(0, len(terms), 2)]
    return terms[0]


def pack_rows(groups, *refs):
    queries, keys, values = refs[:3]
    outs = refs[3:]
    me = lax.axis_index("fsdp")
    width = queries.shape[1] // groups
    for k in range(groups):
        columns = block(me ^ k, width, LANES)
        for at, source in enumerate((queries, keys, values)):
            outs[k][:, at * width : (at + 1) * width] = source[:, columns]


def pack_columns(groups, *refs):
    source = refs[0]
    outs = refs[-groups:]
    me = lax.axis_index("fsdp")
    width = source.shape[1] // groups
    for k in range(groups):
        outs[k][...] = source[:, block(me ^ k, width, LANES)]


def attend(groups, *refs):
    pieces = refs[:groups]
    rows_ref, out = refs[groups:]
    me = lax.axis_index("fsdp")
    local = pieces[0].shape[0]
    width = out.shape[1]
    for k in range(groups):
        rows_ref[block(me ^ k, local, local), :] = pieces[k][...]
    for head in range(width // HDIM):
        at = head * HDIM
        queries = rows_ref[:, at : at + HDIM]
        keys = rows_ref[:, width + at : width + at + HDIM]
        values = rows_ref[:, 2 * width + at : 2 * width + at + HDIM]
        scores = product(queries, keys, 1, 1) * ROOT
        exponent = jnp.exp(scores - jnp.max(scores, axis=1, keepdims=True))
        probs = exponent * (1.0 / jnp.sum(exponent, axis=1, keepdims=True))
        out[:, at : at + HDIM] = product(probs.astype(BF16), values, 1, 0).astype(BF16)


def join_weight(groups, count, *refs):
    pieces = refs[:count]
    out = refs[count]
    me = lax.axis_index("frame")
    rows = pieces[0].shape[0] // groups
    width = rows * count
    for n in range(count):
        for k in range(groups):
            start = pl.multiple_of(k * width + (me ^ n) * rows, rows)
            out[pl.ds(start, rows), :] = pieces[n][k * rows : (k + 1) * rows, :]


def shifted(padded, start, tile):
    for residue in range(8):
        taps = range(residue, KERNEL, 8)
        reach = 8 * (len(taps) - 1)
        rows = padded[start + 1 + residue : start + 1 + residue + tile + reach, :]
        yield taps, rows


def convolve(groups, *refs):
    attention = refs[:groups]
    weight, taps_ref = refs[groups : groups + 2]
    projected_ref, slope_ref = refs[groups + 2 : groups + 4]
    outs = refs[groups + 4 : 2 * groups + 4]
    padded, taps, result = refs[2 * groups + 4 :]
    me = lax.axis_index("fsdp")
    frames, depth = attention[0].shape
    channels = weight.shape[1]
    local = frames // groups
    padded[0:16, :] = jnp.zeros((16, LANES), F32)
    padded[frames + 16 : frames + 32, :] = jnp.zeros((16, LANES), F32)

    def lane_block(c, carry):
        columns = block(c, LANES, LANES)
        total = product(attention[0][...], weight[0:depth, columns], 1, 0)
        for k in range(1, groups):
            total += product(attention[k][...], weight[k * depth : (k + 1) * depth, columns], 1, 0)
        rounded = total.astype(BF16)
        projected_ref[:, columns] = rounded
        padded[16 : frames + 16, :] = rounded.astype(F32)
        taps[0:KERNEL, :] = taps_ref[:, block(me * (channels // LANES) + c, LANES, LANES)].astype(F32)
        for start in range(0, frames, TILE):
            conv = jnp.zeros((TILE, LANES), F32)
            for indices, rows in shifted(padded, start, TILE):
                for at, j in enumerate(indices):
                    conv += taps[j : j + 1, :] * rows[8 * at : 8 * at + TILE, :]
            gate = 1.0 / (1.0 + jnp.exp(-conv))
            own = padded[start + 16 : start + 16 + TILE, :]
            result[start : start + TILE, :] = own + conv * gate
            slope_ref[start : start + TILE, columns] = gate * (1.0 + conv * (1.0 - gate))
        for k in range(groups):
            outs[k][:, columns] = result[block(me ^ k, local, local), :].astype(BF16)
        return carry

    lax.fori_loop(0, channels // LANES, lane_block, 0)


def convolve_back(groups, *refs):
    upstream = refs[:groups]
    projected_ref, slope_ref, weight, taps_ref = refs[groups : groups + 4]
    grad_ref, tap_ref = refs[groups + 4 : groups + 6]
    outs = refs[groups + 6 : 2 * groups + 6]
    padded, taps, above, sums = refs[2 * groups + 6 :]
    me = lax.axis_index("fsdp")
    frames, channels = projected_ref.shape
    local = frames // groups
    depth = weight.shape[0] // groups
    padded[0:16, :] = jnp.zeros((16, LANES), F32)
    padded[frames + 16 : frames + 32, :] = jnp.zeros((16, LANES), F32)

    def lane_block(c, carry):
        columns = block(c, LANES, LANES)
        for k in range(groups):
            above[block(me ^ k, local, local), :] = upstream[k][:, columns].astype(F32)
        taps[0:KERNEL, :] = taps_ref[:, block(me * (channels // LANES) + c, LANES, LANES)].astype(F32)
        padded[16 : frames + 16, :] = (above[...] * slope_ref[:, columns]).astype(BF16).astype(F32)
        sums[...] = jnp.zeros(sums.shape, F32)
        for start in range(0, frames, TILE):
            total = above[start : start + TILE, :]
            own = projected_ref[start : start + TILE, columns].astype(F32)
            for indices, rows in shifted(padded, start, TILE):
                for at, j in enumerate(indices):
                    part = rows[8 * at : 8 * at + TILE, :]
                    tap = KERNEL - 1 - j
                    total += taps[tap : tap + 1, :] * part
                    terms = own * part
                    sums[8 * tap : 8 * tap + 8, :] += tree_sum(
                        [terms[8 * i : 8 * i + 8, :] for i in range(TILE // 8)]
                    )
            grad_ref[start : start + TILE, columns] = total.astype(BF16)
        tap_ref[:, columns] = jnp.sum(sums[...].reshape(TAPS, 8, LANES), axis=1)
        return carry

    lax.fori_loop(0, channels // LANES, lane_block, 0)
    grads = grad_ref[...]
    for k in range(groups):
        outs[k][...] = product(grads, weight[k * depth : (k + 1) * depth, :], 1, 1).astype(BF16)


def weight_terms(groups, count, rows, *refs):
    attention = refs[:groups]
    grads, tap_ref = refs[groups : groups + 2]
    outs = refs[groups + 2 : groups + 4]
    terms = refs[groups + 4]
    me = lax.axis_index("frame")
    gathered = groups * rows
    half = count // 2
    for k in range(groups):
        terms[...] = product(attention[k][...], grads[...], 0, 0)
        for m in range(half):
            for core in range(2):
                there = pl.ds(pl.multiple_of((me ^ (2 * m + core)) * rows, rows), rows)
                at = m * gathered + k * rows
                outs[core][at : at + rows, :] = terms[there, :].astype(BF16)
    for core in range(2):
        outs[core][half * gathered :, :] = tap_ref[...].astype(BF16)


def plain_terms(groups, *refs):
    attention = refs[:groups]
    grads, out = refs[groups:]
    depth = attention[0].shape[1]
    for k in range(groups):
        out[k * depth : (k + 1) * depth, :] = product(attention[k][...], grads[...], 0, 0).astype(BF16)


def add_core(gathered, *refs):
    mine, other = refs[:2]
    outs = refs[2:]
    taps = len(outs) * gathered
    shared = (mine[taps:, :].astype(F32) + other[taps:, :].astype(F32)).astype(BF16)
    for m, out in enumerate(outs):
        rows = slice(m * gathered, (m + 1) * gathered)
        out[0:gathered, :] = (mine[rows, :].astype(F32) + other[rows, :].astype(F32)).astype(BF16)
        out[gathered:, :] = shared


def add_spans(pieces, rows, *refs):
    outs = refs[pieces:]
    total = tree_sum([ref[...].astype(F32) for ref in refs[:pieces]])
    gathered = len(outs) * rows
    for k, out in enumerate(outs):
        out[0:TAPS, :] = total[gathered:, :].astype(BF16)
        out[TAPS:, :] = total[k * rows : (k + 1) * rows, :].astype(BF16)


def join_sums(groups, scale, *refs):
    pieces = refs[:groups]
    weight_ref, tap_ref = refs[groups:]
    me = lax.axis_index("fsdp")
    width = pieces[0].shape[1]
    for k in range(groups):
        columns = block(me ^ k, width, LANES)
        tap_ref[:, columns] = pieces[k][0:KERNEL, :].astype(F32) * scale
        weight_ref[:, columns] = pieces[k][TAPS:, :].astype(F32) * scale


def attend_back(groups, *refs):
    rows_ref = refs[0]
    upstream = refs[1 : groups + 1]
    outs = refs[groups + 1 : 2 * groups + 1]
    grads, result = refs[2 * groups + 1 :]
    me = lax.axis_index("fsdp")
    width = upstream[0].shape[1]
    local = outs[0].shape[0]
    grads[...] = tree_sum([ref[...].astype(F32) for ref in upstream]).astype(BF16)
    for head in range(width // HDIM):
        at = head * HDIM
        queries = rows_ref[:, at : at + HDIM]
        keys = rows_ref[:, width + at : width + at + HDIM]
        values = rows_ref[:, 2 * width + at : 2 * width + at + HDIM]
        above = grads[:, at : at + HDIM]
        scores = product(queries, keys, 1, 1) * ROOT
        exponent = jnp.exp(scores - jnp.max(scores, axis=1, keepdims=True))
        weights = exponent * (1.0 / jnp.sum(exponent, axis=1, keepdims=True))
        slopes = product(above, values, 1, 1)
        row_dot = jnp.sum(weights * slopes, axis=1, keepdims=True)
        grad_scores = (weights * (slopes - row_dot)).astype(BF16)
        result[:, at : at + HDIM] = (product(grad_scores, keys, 1, 0) * ROOT).astype(BF16)
        result[:, width + at : width + at + HDIM] = (
            product(grad_scores, queries, 0, 0) * ROOT
        ).astype(BF16)
        result[:, 2 * width + at : 2 * width + at + HDIM] = product(
            weights.astype(BF16), above, 0, 0
        ).astype(BF16)
    for k in range(groups):
        outs[k][...] = result[block(me ^ k, local, local), :]


def join_rows(groups, *refs):
    pieces = refs[:groups]
    outs = refs[groups:]
    me = lax.axis_index("fsdp")
    width = pieces[0].shape[1] // len(outs)
    for k in range(groups):
        columns = block(me ^ k, width, LANES)
        for at, out in enumerate(outs):
            out[0, :, columns] = pieces[k][:, at * width : (at + 1) * width]


def gather_weight(out_weight, groups, count):
    rows, model = out_weight.shape
    channels = model // groups
    direct = rows % 16 == 0
    if direct:
        sent = call(functools.partial(pack_columns, groups), [((rows, channels), BF16)] * groups, out_weight)
    else:
        me = lax.axis_index("fsdp")
        sent = [
            lax.dynamic_slice_in_dim(out_weight, (me ^ k) * channels, channels, axis=1)
            for k in range(groups)
        ]
    mine = jnp.concatenate(
        [sent[0]] + [swap(sent[k], "fsdp", k) for k in range(1, groups)], axis=0
    )
    across = [mine] + [swap(mine, "frame", 2 * m) for m in range(1, count // 2)]
    pieces = []
    for piece in across:
        pieces += [piece, swap(piece, "frame", 1)]
    if direct:
        return call(
            functools.partial(join_weight, groups, count),
            [((groups * count * rows, channels), BF16)],
            *pieces,
        )[0]
    me = lax.axis_index("frame")
    ordered = jnp.take(jnp.stack(pieces), me ^ jnp.arange(count), axis=0)
    ordered = ordered.reshape(count, groups, rows, channels).transpose(1, 0, 2, 3)
    return ordered.reshape(groups * count * rows, channels)


def reduce_sums(attention, grads, tap_terms, groups, count, rows, scale):
    channels = grads.shape[1]
    depth = attention[0].shape[1]
    half = count // 2
    gathered = groups * rows
    flops = 2 * grads.shape[0] * depth * groups * channels
    if rows % 16 == 0:
        mine, other = call(
            functools.partial(weight_terms, groups, count, rows),
            [((half * gathered + TAPS, channels), BF16)] * 2,
            *attention,
            grads,
            tap_terms,
            scratch=[pltpu.VMEM((depth, channels), F32)],
            flops=flops,
        )
    else:
        (terms,) = call(
            functools.partial(plain_terms, groups),
            [((groups * depth, channels), BF16)],
            *attention,
            grads,
            flops=flops,
        )
        me = lax.axis_index("frame")
        terms = jnp.take(
            terms.reshape(groups, count, rows, channels), me ^ jnp.arange(count), axis=1
        )
        terms = terms.reshape(groups, half, 2, rows, channels).transpose(2, 1, 0, 3, 4)
        terms = terms.reshape(2, half * gathered, channels)
        mine, other = [
            jnp.concatenate([terms[core], tap_terms.astype(BF16)], axis=0) for core in range(2)
        ]
    sent = call(
        functools.partial(add_core, gathered),
        [((gathered + TAPS, channels), BF16)] * half,
        mine,
        swap(other, "frame", 1),
    )
    pieces = [sent[0]] + [swap(sent[m], "frame", 2 * m) for m in range(1, half)]
    sent = call(
        functools.partial(add_spans, half, rows),
        [((TAPS + rows, channels), BF16)] * groups,
        *pieces,
    )
    pieces = [sent[0]] + [swap(sent[k], "fsdp", k) for k in range(1, groups)]
    return call(
        functools.partial(join_sums, groups, scale),
        [((rows, groups * channels), F32), ((KERNEL, groups * channels), F32)],
        *pieces,
    )


def shards(queries, key_rows, value_rows, out_weight, conv_weight, grad_out):
    local, inner = queries.shape[1:]
    model = grad_out.shape[2]
    groups = lax.axis_size("fsdp")
    count = lax.axis_size("frame")
    frames = local * groups
    width = inner // groups
    channels = model // groups
    scale = 1.0 / math.sqrt(frames * count)
    weight = gather_weight(out_weight, groups, count)

    sent = call(
        functools.partial(pack_rows, groups),
        [((local, 3 * width), BF16)] * groups,
        queries[0],
        key_rows[0],
        value_rows[0],
    )
    pieces = [sent[0]] + [swap(sent[k], "fsdp", k) for k in range(1, groups)]
    rows, own = call(
        functools.partial(attend, groups),
        [((frames, 3 * width), BF16), ((frames, width), BF16)],
        *pieces,
        flops=4 * frames * frames * width,
    )
    attention = [own] + [swap(own, "fsdp", k) for k in range(1, groups)]

    sent = call(
        functools.partial(pack_columns, groups),
        [((local, channels), BF16)] * groups,
        grad_out[0],
        attention[1],
        loose=1,
    )
    upstream = [sent[0]] + [swap(sent[k], "fsdp", k) for k in range(1, groups)]

    outs = call(
        functools.partial(convolve, groups),
        [((frames, channels), BF16), ((frames, channels), F32)] + [((local, channels), BF16)] * groups,
        *attention,
        weight,
        conv_weight,
        scratch=[
            pltpu.VMEM((frames + 32, LANES), F32),
            pltpu.VMEM((TAPS, LANES), F32),
            pltpu.VMEM((frames, LANES), F32),
        ],
        flops=2 * frames * inner * channels,
    )
    projected, slope = outs[:2]
    sent = outs[2:]
    pieces = [sent[0]] + [swap(sent[k], "fsdp", k) for k in range(1, groups)]
    (block_out,) = call(functools.partial(join_rows, groups), [((1, local, model), BF16)], *pieces)

    outs = call(
        functools.partial(convolve_back, groups),
        [((frames, channels), BF16), ((TAPS, channels), F32)] + [((frames, width), BF16)] * groups,
        *upstream,
        projected,
        slope,
        weight,
        conv_weight,
        scratch=[
            pltpu.VMEM((frames + 32, LANES), F32),
            pltpu.VMEM((TAPS, LANES), F32),
            pltpu.VMEM((frames, LANES), F32),
            pltpu.VMEM((8 * TAPS, LANES), F32),
        ],
        flops=2 * frames * inner * channels,
    )
    grads, tap_terms = outs[:2]
    sent = outs[2:]
    above = [sent[0]] + [swap(sent[k], "fsdp", k) for k in range(1, groups)]
    weight_grad, conv_grad = reduce_sums(
        attention, grads, tap_terms, groups, count, out_weight.shape[0], scale
    )
    sent = call(
        functools.partial(attend_back, groups),
        [((local, 3 * width), BF16)] * groups,
        rows,
        *above,
        scratch=[pltpu.VMEM((frames, width), BF16), pltpu.VMEM((frames, 3 * width), BF16)],
        flops=10 * frames * frames * width,
    )
    pieces = [sent[0]] + [swap(sent[k], "fsdp", k) for k in range(1, groups)]
    grad_queries, grad_keys, grad_values = call(
        functools.partial(join_rows, groups), [((1, local, inner), BF16)] * 3, *pieces
    )
    return (block_out, grad_queries, grad_keys, grad_values, weight_grad, conv_grad)


def solution(mesh):
    return jax.shard_map(
        shards,
        mesh=mesh,
        in_specs=(
            P("frame", "fsdp", None),
            P("frame", "fsdp", None),
            P("frame", "fsdp", None),
            P(("fsdp", "frame"), None),
            P(),
            P("frame", "fsdp", None),
        ),
        out_specs=(
            P("frame", "fsdp", None),
            P("frame", "fsdp", None),
            P("frame", "fsdp", None),
            P("frame", "fsdp", None),
            P(("fsdp", "frame"), None),
            P(),
        ),
        check_vma=False,
    )
```

time: 403 us -> 99.8 us (0.25)
  waiting for transfers between devices: 267 us -> 37 us
  matrix products: 38.7 us -> 0 us
  local copies, waits for them, and re-layouts: 23.6 us -> 3.77 us
  Pallas kernels: 0 us -> 17.7 us
  between operations: 14.3 us -> 0.79 us
  other arithmetic: 11.2 us -> 0 us
  blocking collectives: 8.11 us -> 0 us
    reduce_scatter x1 -> x0, waiting for transfers between devices: 147 us -> none  [shards(): lax.psum_scatter(jnp.einsum('ri,rd->id', attention, grad_projected, prefe...]
    psum x1 -> x0, waiting for transfers between devices: 73.9 us -> none  [shards(): conv_grad = lax.psum(conv_terms, ('fsdp', 'frame')) * grad_scale]
    ppermute x4 -> x35, waiting for transfers between devices: 0.15 us -> 37 us  [swap(): return lax.ppermute(cells, axis, [(i, i ^ mask) for i in range(count)])]
    ppermute x4 -> x35, starting transfers between devices: 11.4 us -> 40.3 us  [swap(): return lax.ppermute(cells, axis, [(i, i ^ mask) for i in range(count)])]
    all_to_all x7 -> x0, starting transfers between devices: 27.7 us -> none  [the longest x1 5.16 us: shards(): lax.all_to_all(own_queries.reshape(local_rows, groups, group_width), 'fsd...]
    all_gather x1 -> x0, waiting for transfers between devices: 24.9 us -> none  [shards(): lax.all_gather(out_weight, ('fsdp', 'frame'), axis=0, tiled=True)]
    conv_general_dilated x3 -> x0, matrix products: 22.5 us -> none  [depthwise(): lax.conv_general_dilated(signal[None], taps[:, None, :], (1,), 'VALID', d...]
    all_to_all x7 -> x0, waiting for transfers between devices: 20.2 us -> none  [the longest x1 4.99 us: shards(): lax.all_to_all(own_values.reshape(local_rows, groups, group_width), 'fsdp...]
  transfers between devices with their start and end apart: 14 -> 35, of which waited for: 9 -> 12; matrix products, arithmetic and copies ran while one was open for 14% -> 0% of each run, Pallas kernels for 0% -> 11%
where the time goes in v1:
time: 99.8 us; the launch traced here: 99.6 us
  starting transfers between devices  40.3 us (40%)
  waiting for transfers between devices  37 us (37%)
  Pallas kernels  17.7 us (18%)
  local copies, waits for them, and re-layouts  3.77 us (4%)
    ppermute x35, starting transfers between devices, swap(): return lax.ppermute(cells, axis, [(i, i ^ mask) for i in range(count)])  40.3 us
    ppermute x35, waiting for transfers between devices, swap(): return lax.ppermute(cells, axis, [(i, i ^ mask) for i in range(count)])  37 us
    pallas_call x14, Pallas kernels, call(): pl.pallas_call(body, out_shape=[jax.ShapeDtypeStruct(s, t) for s, t in ou...  17.7 us
    unnamed x15, local copies, waits for them, and re-layouts  3.76 us
  transfers between devices with their start and end apart: 35, of which 12 were waited for; matrix products, arithmetic and copies ran while one was open for 0% of the time, Pallas kernels for 11%

profile of v1, /device:TPU:0, one launch (start us, length us, event | category | flops | bytes accessed | tf_op | source)
XLA Modules:
  0.0 99.6 jit_solution(11112259184601771635)
XLA Ops:
  1.5 3.0 %collective-permute-start.6 = (bf16[32,512]{1,0:T(8,128)(2,1)S(1)}, bf16[32,512]{1,0:T(8,128)(2,1)S(1)}, u32[]{:S(2)}, u32[]{:S(2)}) collective-permute-start(bf16[32,512]{1,0:T(8,128)(2,1)S(1)} %get-tuple-element.57), channel_id=1, source_target_pairs={{0,8},{8,0},{16,24},{24,16},{1,9},{9,1},{17,25},{25,17},{2,10},{10... | collective-permute-start | bytes 98312 | tf_op jit(solution)/shard_map/ppermute | solution.py:24
  4.6 1.5 %collective-permute-start.7 = (bf16[32,512]{1,0:T(8,128)(2,1)S(1)}, bf16[32,512]{1,0:T(8,128)(2,1)S(1)}, u32[]{:S(2)}, u32[]{:S(2)}) collective-permute-start(bf16[32,512]{1,0:T(8,128)(2,1)S(1)} %get-tuple-element.58), channel_id=1, source_target_pairs={{0,16},{8,24},{16,0},{24,8},{1,17},{9,25},{17,1},{25,9},{2,18},{10... | collective-permute-start | bytes 98312 | tf_op jit(solution)/shard_map/ppermute | solution.py:24
  9.1 2.0 %collective-permute-start = (bf16[128,768]{1,0:T(8,128)(2,1)S(1)}, bf16[128,768]{1,0:T(8,128)(2,1)S(1)}, u32[]{:S(2)}, u32[]{:S(2)}) collective-permute-start(bf16[128,768]{1,0:T(8,128)(2,1)S(1)} %get-tuple-element.52), channel_id=1, source_target_pairs={{0,8},{8,0},{16,24},{24,16},{1,9},{9,1},{17,25},{25,17},{2,10},{10... | collective-permute-start | bytes 589832 | tf_op jit(solution)/shard_map/ppermute | solution.py:24
  11.1 1.5 %collective-permute-start.1 = (bf16[128,768]{1,0:T(8,128)(2,1)S(1)}, bf16[128,768]{1,0:T(8,128)(2,1)S(1)}, u32[]{:S(2)}, u32[]{:S(2)}) collective-permute-start(bf16[128,768]{1,0:T(8,128)(2,1)S(1)} %get-tuple-element.53), channel_id=1, source_target_pairs={{0,16},{8,24},{16,0},{24,8},{1,17},{9,25},{17,1},{25,9},{2,18},{10... | collective-permute-start | bytes 589832 | tf_op jit(solution)/shard_map/ppermute | solution.py:24
  12.7 4.2 %collective-permute-done.refs_1_ = bf16[128,768]{1,0:T(8,128)(2,1)S(1)} collective-permute-done((bf16[128,768]{1,0:T(8,128)(2,1)S(1)}, bf16[128,768]{1,0:T(8,128)(2,1)S(1)}, u32[]{:S(2)}, u32[]{:S(2)}) %collective-permute-start) | collective-permute-done | bytes 196640 | tf_op jit(solution)/shard_map/ppermute | solution.py:24
  16.8 4.0 %collective-permute-done.1.refs_2_ = bf16[128,768]{1,0:T(8,128)(2,1)S(1)} collective-permute-done((bf16[128,768]{1,0:T(8,128)(2,1)S(1)}, bf16[128,768]{1,0:T(8,128)(2,1)S(1)}, u32[]{:S(2)}, u32[]{:S(2)}) %collective-permute-start.1) | collective-permute-done | bytes 196640 | tf_op jit(solution)/shard_map/ppermute | solution.py:24
  23.5 3.6 %collective-permute-start.14 = (bf16[128,512]{1,0:T(8,128)(2,1)S(1)}, bf16[128,512]{1,0:T(8,128)(2,1)S(1)}, u32[]{:S(2)}, u32[]{:S(2)}) collective-permute-start(bf16[128,512]{1,0:T(8,128)(2,1)S(1)} %constant_dynamic-update-slice_fusion.refs_0_), channel_id=1, source_target_pairs={{0,6},{1,7},{2,4},{3,5},{4,2},{5,3},{6,0},{7,1},{8,14},{9,15},{10,... | collective-permute-start | bytes 393224 | tf_op jit(solution)/shard_map/ppermute | solution.py:24
  27.9 3.4 %collective-permute-done.14.refs_6_ = bf16[128,512]{1,0:T(8,128)(2,1)S(1)} collective-permute-done((bf16[128,512]{1,0:T(8,128)(2,1)S(1)}, bf16[128,512]{1,0:T(8,128)(2,1)S(1)}, u32[]{:S(2)}, u32[]{:S(2)}) %collective-permute-start.14) | collective-permute-done | bytes 131104 | tf_op jit(solution)/shard_map/ppermute | solution.py:24
  31.3 1.5 %collective-permute-start.5 = (bf16[512,256]{1,0:T(8,128)(2,1)S(1)}, bf16[512,256]{1,0:T(8,128)(2,1)S(1)}, u32[]{:S(2)}, u32[]{:S(2)}) collective-permute-start(bf16[512,256]{1,0:T(8,128)(2,1)S(1)} %get-tuple-element.55.refs_0_), channel_id=1, source_target_pairs={{0,24},{8,16},{16,8},{24,0},{1,25},{9,17},{17,9},{25,1},{2,26},{10... | collective-permute-start | bytes 786440 | tf_op jit(solution)/shard_map/ppermute | solution.py:24
  32.9 3.3 %collective-permute-done.12.refs_4_ = bf16[128,512]{1,0:T(8,128)(2,1)S(1)} collective-permute-done((bf16[128,512]{1,0:T(8,128)(2,1)S(1)}, bf16[128,512]{1,0:T(8,128)(2,1)S(1)}, u32[]{:S(2)}, u32[]{:S(2)}) %collective-permute-start.12) | collective-permute-done | bytes 131104 | tf_op jit(solution)/shard_map/ppermute | solution.py:24
  41.6 6.6 %collective-permute-done.4.refs_2_ = bf16[512,256]{1,0:T(8,128)(2,1)S(1)} collective-permute-done((bf16[512,256]{1,0:T(8,128)(2,1)S(1)}, bf16[512,256]{1,0:T(8,128)(2,1)S(1)}, u32[]{:S(2)}, u32[]{:S(2)}) %collective-permute-start.4) | collective-permute-done | bytes 262176 | tf_op jit(solution)/shard_map/ppermute | solution.py:24
  48.2 4.2 %shard_map.113 = (bf16[512,512]{1,0:T(8,128)(2,1)S(1)}, f32[512,512]{1,0:T(8,128)S(1)}, bf16[128,512]{1,0:T(8,128)(2,1)S(1)}, bf16[128,512]{1,0:T(8,128)(2,1)S(1...) custom-call(bf16[512,256]{1,0:T(8,128)(2,1)S(1)} %get-tuple-element.55.refs_0_, ...), custom_call_target="tpu_custom_call" | custom-call | flops 536870912 | bytes 4321280 | tf_op jit(solution)/shard_map/pallas_call | solution.py:32
  52.4 5.7 %shard_map.116 = (bf16[512,512]{1,0:T(8,128)(2,1)S(1)}, f32[32,512]{1,0:T(8,128)S(1)}, bf16[512,256]{1,0:T(8,128)(2,1)S(1)}, bf16[512,256]{1,0:T(8,128)(2,1)S(1)...) custom-call(bf16[128,512]{1,0:T(8,128)(2,1)S(1)} %get-tuple-element.65.refs_0_, ...), custom_call_target="tpu_custom_call" | custom-call | flops 536870912 | bytes 4911104 | tf_op jit(solution)/shard_map/pallas_call | solution.py:32
  60.2 2.2 %collective-permute-start.24 = (bf16[512,256]{1,0:T(8,128)(2,1)S(1)}, bf16[512,256]{1,0:T(8,128)(2,1)S(1)}, u32[]{:S(2)}, u32[]{:S(2)}) collective-permute-start(bf16[512,256]{1,0:T(8,128)(2,1)S(1)} %get-tuple-element.74), channel_id=1, source_target_pairs={{0,24},{8,16},{16,8},{24,0},{1,25},{9,17},{17,9},{25,1},{2,26},{10... | collective-permute-start | bytes 786440 | tf_op jit(solution)/shard_map/ppermute | solution.py:24
  62.6 1.6 %collective-permute-start.29 = (bf16[160,512]{1,0:T(8,128)(2,1)S(1)}, bf16[160,512]{1,0:T(8,128)(2,1)S(1)}, u32[]{:S(2)}, u32[]{:S(2)}) collective-permute-start(bf16[160,512]{1,0:T(8,128)(2,1)S(1)} %get-tuple-element.87), channel_id=1, source_target_pairs={{0,2},{1,3},{2,0},{3,1},{4,6},{5,7},{6,4},{7,5},{8,10},{9,11},{10,... | collective-permute-start | bytes 491528 | tf_op jit(solution)/shard_map/ppermute | solution.py:24
  64.2 1.7 %collective-permute-start.30 = (bf16[160,512]{1,0:T(8,128)(2,1)S(1)}, bf16[160,512]{1,0:T(8,128)(2,1)S(1)}, u32[]{:S(2)}, u32[]{:S(2)}) collective-permute-start(bf16[160,512]{1,0:T(8,128)(2,1)S(1)} %get-tuple-element.88), channel_id=1, source_target_pairs={{0,4},{1,5},{2,6},{3,7},{4,0},{5,1},{6,2},{7,3},{8,12},{9,13},{10,... | collective-permute-start | bytes 491528 | tf_op jit(solution)/shard_map/ppermute | solution.py:24
  65.9 2.2 %collective-permute-done.22.refs_2_ = bf16[512,256]{1,0:T(8,128)(2,1)S(1)} collective-permute-done((bf16[512,256]{1,0:T(8,128)(2,1)S(1)}, bf16[512,256]{1,0:T(8,128)(2,1)S(1)}, u32[]{:S(2)}, u32[]{:S(2)}) %collective-permute-start.22) | collective-permute-done | bytes 262176 | tf_op jit(solution)/shard_map/ppermute | solution.py:24
  68.1 2.7 %collective-permute-start.31 = (bf16[160,512]{1,0:T(8,128)(2,1)S(1)}, bf16[160,512]{1,0:T(8,128)(2,1)S(1)}, u32[]{:S(2)}, u32[]{:S(2)}) collective-permute-start(bf16[160,512]{1,0:T(8,128)(2,1)S(1)} %get-tuple-element.89), channel_id=1, source_target_pairs={{0,6},{1,7},{2,4},{3,5},{4,2},{5,3},{6,0},{7,1},{8,14},{9,15},{10,... | collective-permute-start | bytes 491528 | tf_op jit(solution)/shard_map/ppermute | solution.py:24
  70.8 3.0 %collective-permute-done.23.refs_3_ = bf16[512,256]{1,0:T(8,128)(2,1)S(1)} collective-permute-done((bf16[512,256]{1,0:T(8,128)(2,1)S(1)}, bf16[512,256]{1,0:T(8,128)(2,1)S(1)}, u32[]{:S(2)}, u32[]{:S(2)}) %collective-permute-start.23) | collective-permute-done | bytes 262176 | tf_op jit(solution)/shard_map/ppermute | solution.py:24
  75.0 2.6 %shard_map.117 = (bf16[128,768]{1,0:T(8,128)(2,1)S(1)}, bf16[128,768]{1,0:T(8,128)(2,1)S(1)}, bf16[128,768]{1,0:T(8,128)(2,1)S(1)}, bf16[128,768]{1,0:T(8,128)(2,1)S(1)}) custom-call(bf16[512,768]{1,0:T(8,128)(2,1)S(1)} %get-tuple-element.64.refs_0_, bf16[512,256]{1,0:T(8,128)(2,1)S(1)} %get-tuple-element.71.refs_1_, ...), custom_call_target="tpu_custom_call" | custom-call | flops 671088640 | bytes 2621440 | tf_op jit(solution)/shard_map/pallas_call | solution.py:32
  78.7 2.0 %collective-permute-start.26 = (bf16[128,768]{1,0:T(8,128)(2,1)S(1)}, bf16[128,768]{1,0:T(8,128)(2,1)S(1)}, u32[]{:S(2)}, u32[]{:S(2)}) collective-permute-start(bf16[128,768]{1,0:T(8,128)(2,1)S(1)} %get-tuple-element.77), channel_id=1, source_target_pairs={{0,16},{8,24},{16,0},{24,8},{1,17},{9,25},{17,1},{25,9},{2,18},{10... | collective-permute-start | bytes 589832 | tf_op jit(solution)/shard_map/ppermute | solution.py:24
  82.1 1.6 %collective-permute-start.18 = (bf16[128,512]{1,0:T(8,128)(2,1)S(1)}, bf16[128,512]{1,0:T(8,128)(2,1)S(1)}, u32[]{:S(2)}, u32[]{:S(2)}) collective-permute-start(bf16[128,512]{1,0:T(8,128)(2,1)S(1)} %get-tuple-element.63), channel_id=1, source_target_pairs={{0,24},{8,16},{16,8},{24,0},{1,25},{9,17},{17,9},{25,1},{2,26},{10... | collective-permute-start | bytes 393224 | tf_op jit(solution)/shard_map/ppermute | solution.py:24
  83.8 7.4 %collective-permute-done.17.refs_2_ = bf16[128,512]{1,0:T(8,128)(2,1)S(1)} collective-permute-done((bf16[128,512]{1,0:T(8,128)(2,1)S(1)}, bf16[128,512]{1,0:T(8,128)(2,1)S(1)}, u32[]{:S(2)}, u32[]{:S(2)}) %collective-permute-start.17) | collective-permute-done | bytes 131104 | tf_op jit(solution)/shard_map/ppermute | solution.py:24
  91.2 2.4 %collective-permute-start.32 = (bf16[64,512]{1,0:T(8,128)(2,1)S(1)}, bf16[64,512]{1,0:T(8,128)(2,1)S(1)}, u32[]{:S(2)}, u32[]{:S(2)}) collective-permute-start(bf16[64,512]{1,0:T(8,128)(2,1)S(1)} %get-tuple-element.91), channel_id=1, source_target_pairs={{0,8},{8,0},{16,24},{24,16},{1,9},{9,1},{17,25},{25,17},{2,10},{10... | collective-permute-start | bytes 196616 | tf_op jit(solution)/shard_map/ppermute | solution.py:24
  (76 shorter events, 24.9 us)
Async XLA Ops:
  1.5 11.0 %collective-permute-start.6 = (bf16[32,512]{1,0:T(8,128)(2,1)S(1)}, bf16[32,512]{1,0:T(8,128)(2,1)S(1)}, u32[]{:S(2)}, u32[]{:S(2)}) collective-permute-start(bf16[32,512]{1,0:T(8,128)(2,1)S(1)} %get-tuple-element.57), channel_id=1, source_target_pairs={{0,8},{8,0},{16,24},{24,16},{1,9},{9,1},{17,25},{25,17},{2,10},{10... | collective-permute-start | bytes 98312 | tf_op jit(solution)/shard_map/ppermute | solution.py:24
  6.1 17.4 %collective-permute-start.8 = (bf16[32,512]{1,0:T(8,128)(2,1)S(1)}, bf16[32,512]{1,0:T(8,128)(2,1)S(1)}, u32[]{:S(2)}, u32[]{:S(2)}) collective-permute-start(bf16[32,512]{1,0:T(8,128)(2,1)S(1)} %get-tuple-element.59), channel_id=1, source_target_pairs={{0,24},{8,16},{16,8},{24,0},{1,25},{9,17},{17,9},{25,1},{2,26},{10... | collective-permute-start | bytes 98312 | tf_op jit(solution)/shard_map/ppermute | solution.py:24
  11.1 9.8 %collective-permute-start.1 = (bf16[128,768]{1,0:T(8,128)(2,1)S(1)}, bf16[128,768]{1,0:T(8,128)(2,1)S(1)}, u32[]{:S(2)}, u32[]{:S(2)}) collective-permute-start(bf16[128,768]{1,0:T(8,128)(2,1)S(1)} %get-tuple-element.53), channel_id=1, source_target_pairs={{0,16},{8,24},{16,0},{24,8},{1,17},{9,25},{17,1},{25,9},{2,18},{10... | collective-permute-start | bytes 589832 | tf_op jit(solution)/shard_map/ppermute | solution.py:24
  12.6 8.3 %collective-permute-start.2 = (bf16[128,768]{1,0:T(8,128)(2,1)S(1)}, bf16[128,768]{1,0:T(8,128)(2,1)S(1)}, u32[]{:S(2)}, u32[]{:S(2)}) collective-permute-start(bf16[128,768]{1,0:T(8,128)(2,1)S(1)} %get-tuple-element.54), channel_id=1, source_target_pairs={{0,24},{8,16},{16,8},{24,0},{1,25},{9,17},{17,9},{25,1},{2,26},{10... | collective-permute-start | bytes 589832 | tf_op jit(solution)/shard_map/ppermute | solution.py:24
  22.3 14.9 %collective-permute-start.3 = (bf16[512,256]{1,0:T(8,128)(2,1)S(1)}, bf16[512,256]{1,0:T(8,128)(2,1)S(1)}, u32[]{:S(2)}, u32[]{:S(2)}) collective-permute-start(bf16[512,256]{1,0:T(8,128)(2,1)S(1)} %get-tuple-element.55.refs_0_), channel_id=1, source_target_pairs={{0,8},{8,0},{16,24},{24,16},{1,9},{9,1},{17,25},{25,17},{2,10},{10... | collective-permute-start | bytes 786440 | tf_op jit(solution)/shard_map/ppermute | solution.py:24
  27.1 9.0 %collective-permute-start.12 = (bf16[128,512]{1,0:T(8,128)(2,1)S(1)}, bf16[128,512]{1,0:T(8,128)(2,1)S(1)}, u32[]{:S(2)}, u32[]{:S(2)}) collective-permute-start(bf16[128,512]{1,0:T(8,128)(2,1)S(1)} %constant_dynamic-update-slice_fusion.refs_0_), channel_id=1, source_target_pairs={{0,4},{1,5},{2,6},{3,7},{4,0},{5,1},{6,2},{7,3},{8,12},{9,13},{10,... | collective-permute-start | bytes 393224 | tf_op jit(solution)/shard_map/ppermute | solution.py:24
  27.1 9.5 %collective-permute-start.10 = (bf16[128,512]{1,0:T(8,128)(2,1)S(1)}, bf16[128,512]{1,0:T(8,128)(2,1)S(1)}, u32[]{:S(2)}, u32[]{:S(2)}) collective-permute-start(bf16[128,512]{1,0:T(8,128)(2,1)S(1)} %constant_dynamic-update-slice_fusion.refs_0_), channel_id=1, source_target_pairs={{0,2},{1,3},{2,0},{3,1},{4,6},{5,7},{6,4},{7,5},{8,10},{9,11},{10,... | collective-permute-start | bytes 393224 | tf_op jit(solution)/shard_map/ppermute | solution.py:24
  27.9 8.8 %collective-permute-start.9 = (bf16[128,512]{1,0:T(8,128)(2,1)S(1)}, bf16[128,512]{1,0:T(8,128)(2,1)S(1)}, u32[]{:S(2)}, u32[]{:S(2)}) collective-permute-start(bf16[128,512]{1,0:T(8,128)(2,1)S(1)} %constant_dynamic-update-slice_fusion.refs_0_), channel_id=1, source_target_pairs={{0,1},{1,0},{2,3},{3,2},{4,5},{5,4},{6,7},{7,6},{8,9},{9,8},{10,11... | collective-permute-start | bytes 393224 | tf_op jit(solution)/shard_map/ppermute | solution.py:24
  31.3 10.3 %collective-permute-start.5 = (bf16[512,256]{1,0:T(8,128)(2,1)S(1)}, bf16[512,256]{1,0:T(8,128)(2,1)S(1)}, u32[]{:S(2)}, u32[]{:S(2)}) collective-permute-start(bf16[512,256]{1,0:T(8,128)(2,1)S(1)} %get-tuple-element.55.refs_0_), channel_id=1, source_target_pairs={{0,24},{8,16},{16,8},{24,0},{1,25},{9,17},{17,9},{25,1},{2,26},{10... | collective-permute-start | bytes 786440 | tf_op jit(solution)/shard_map/ppermute | solution.py:24
  36.1 12.1 %collective-permute-start.4 = (bf16[512,256]{1,0:T(8,128)(2,1)S(1)}, bf16[512,256]{1,0:T(8,128)(2,1)S(1)}, u32[]{:S(2)}, u32[]{:S(2)}) collective-permute-start(bf16[512,256]{1,0:T(8,128)(2,1)S(1)} %get-tuple-element.55.refs_0_), channel_id=1, source_target_pairs={{0,16},{8,24},{16,0},{24,8},{1,17},{9,25},{17,1},{25,9},{2,18},{10... | collective-permute-start | bytes 786440 | tf_op jit(solution)/shard_map/ppermute | solution.py:24
  38.0 14.4 %collective-permute-start.19 = (bf16[128,512]{1,0:T(8,128)(2,1)S(1)}, bf16[128,512]{1,0:T(8,128)(2,1)S(1)}, u32[]{:S(2)}, u32[]{:S(2)}) collective-permute-start(bf16[128,512]{1,0:T(8,128)(2,1)S(1)} %get-tuple-element.66), channel_id=1, source_target_pairs={{0,8},{8,0},{16,24},{24,16},{1,9},{9,1},{17,25},{25,17},{2,10},{10... | collective-permute-start | bytes 393224 | tf_op jit(solution)/shard_map/ppermute | solution.py:24
  38.8 13.6 %collective-permute-start.20 = (bf16[128,512]{1,0:T(8,128)(2,1)S(1)}, bf16[128,512]{1,0:T(8,128)(2,1)S(1)}, u32[]{:S(2)}, u32[]{:S(2)}) collective-permute-start(bf16[128,512]{1,0:T(8,128)(2,1)S(1)} %get-tuple-element.67), channel_id=1, source_target_pairs={{0,16},{8,24},{16,0},{24,8},{1,17},{9,25},{17,1},{25,9},{2,18},{10... | collective-permute-start | bytes 393224 | tf_op jit(solution)/shard_map/ppermute | solution.py:24
  40.3 12.1 %collective-permute-start.21 = (bf16[128,512]{1,0:T(8,128)(2,1)S(1)}, bf16[128,512]{1,0:T(8,128)(2,1)S(1)}, u32[]{:S(2)}, u32[]{:S(2)}) collective-permute-start(bf16[128,512]{1,0:T(8,128)(2,1)S(1)} %get-tuple-element.68), channel_id=1, source_target_pairs={{0,24},{8,16},{16,8},{24,0},{1,25},{9,17},{17,9},{25,1},{2,26},{10... | collective-permute-start | bytes 393224 | tf_op jit(solution)/shard_map/ppermute | solution.py:24
  58.9 9.2 %collective-permute-start.22 = (bf16[512,256]{1,0:T(8,128)(2,1)S(1)}, bf16[512,256]{1,0:T(8,128)(2,1)S(1)}, u32[]{:S(2)}, u32[]{:S(2)}) collective-permute-start(bf16[512,256]{1,0:T(8,128)(2,1)S(1)} %get-tuple-element.72), channel_id=1, source_target_pairs={{0,8},{8,0},{16,24},{24,16},{1,9},{9,1},{17,25},{25,17},{2,10},{10... | collective-permute-start | bytes 786440 | tf_op jit(solution)/shard_map/ppermute | solution.py:24
  59.7 14.0 %collective-permute-start.23 = (bf16[512,256]{1,0:T(8,128)(2,1)S(1)}, bf16[512,256]{1,0:T(8,128)(2,1)S(1)}, u32[]{:S(2)}, u32[]{:S(2)}) collective-permute-start(bf16[512,256]{1,0:T(8,128)(2,1)S(1)} %get-tuple-element.73), channel_id=1, source_target_pairs={{0,16},{8,24},{16,0},{24,8},{1,17},{9,25},{17,1},{25,9},{2,18},{10... | collective-permute-start | bytes 786440 | tf_op jit(solution)/shard_map/ppermute | solution.py:24
  60.2 14.8 %collective-permute-start.24 = (bf16[512,256]{1,0:T(8,128)(2,1)S(1)}, bf16[512,256]{1,0:T(8,128)(2,1)S(1)}, u32[]{:S(2)}, u32[]{:S(2)}) collective-permute-start(bf16[512,256]{1,0:T(8,128)(2,1)S(1)} %get-tuple-element.74), channel_id=1, source_target_pairs={{0,24},{8,16},{16,8},{24,0},{1,25},{9,17},{17,9},{25,1},{2,26},{10... | collective-permute-start | bytes 786440 | tf_op jit(solution)/shard_map/ppermute | solution.py:24
  62.6 16.1 %collective-permute-start.29 = (bf16[160,512]{1,0:T(8,128)(2,1)S(1)}, bf16[160,512]{1,0:T(8,128)(2,1)S(1)}, u32[]{:S(2)}, u32[]{:S(2)}) collective-permute-start(bf16[160,512]{1,0:T(8,128)(2,1)S(1)} %get-tuple-element.87), channel_id=1, source_target_pairs={{0,2},{1,3},{2,0},{3,1},{4,6},{5,7},{6,4},{7,5},{8,10},{9,11},{10,... | collective-permute-start | bytes 491528 | tf_op jit(solution)/shard_map/ppermute | solution.py:24
  64.2 16.5 %collective-permute-start.30 = (bf16[160,512]{1,0:T(8,128)(2,1)S(1)}, bf16[160,512]{1,0:T(8,128)(2,1)S(1)}, u32[]{:S(2)}, u32[]{:S(2)}) collective-permute-start(bf16[160,512]{1,0:T(8,128)(2,1)S(1)} %get-tuple-element.88), channel_id=1, source_target_pairs={{0,4},{1,5},{2,6},{3,7},{4,0},{5,1},{6,2},{7,3},{8,12},{9,13},{10,... | collective-permute-start | bytes 491528 | tf_op jit(solution)/shard_map/ppermute | solution.py:24
  68.1 14.0 %collective-permute-start.31 = (bf16[160,512]{1,0:T(8,128)(2,1)S(1)}, bf16[160,512]{1,0:T(8,128)(2,1)S(1)}, u32[]{:S(2)}, u32[]{:S(2)}) collective-permute-start(bf16[160,512]{1,0:T(8,128)(2,1)S(1)} %get-tuple-element.89), channel_id=1, source_target_pairs={{0,6},{1,7},{2,4},{3,5},{4,2},{5,3},{6,0},{7,1},{8,14},{9,15},{10,... | collective-permute-start | bytes 491528 | tf_op jit(solution)/shard_map/ppermute | solution.py:24
  77.7 15.9 %collective-permute-start.25 = (bf16[128,768]{1,0:T(8,128)(2,1)S(1)}, bf16[128,768]{1,0:T(8,128)(2,1)S(1)}, u32[]{:S(2)}, u32[]{:S(2)}) collective-permute-start(bf16[128,768]{1,0:T(8,128)(2,1)S(1)} %get-tuple-element.76), channel_id=1, source_target_pairs={{0,8},{8,0},{16,24},{24,16},{1,9},{9,1},{17,25},{25,17},{2,10},{10... | collective-permute-start | bytes 589832 | tf_op jit(solution)/shard_map/ppermute | solution.py:24
  78.7 12.4 %collective-permute-start.17 = (bf16[128,512]{1,0:T(8,128)(2,1)S(1)}, bf16[128,512]{1,0:T(8,128)(2,1)S(1)}, u32[]{:S(2)}, u32[]{:S(2)}) collective-permute-start(bf16[128,512]{1,0:T(8,128)(2,1)S(1)} %get-tuple-element.62), channel_id=1, source_target_pairs={{0,16},{8,24},{16,0},{24,8},{1,17},{9,25},{17,1},{25,9},{2,18},{10... | collective-permute-start | bytes 393224 | tf_op jit(solution)/shard_map/ppermute | solution.py:24
  78.7 17.1 %collective-permute-start.26 = (bf16[128,768]{1,0:T(8,128)(2,1)S(1)}, bf16[128,768]{1,0:T(8,128)(2,1)S(1)}, u32[]{:S(2)}, u32[]{:S(2)}) collective-permute-start(bf16[128,768]{1,0:T(8,128)(2,1)S(1)} %get-tuple-element.77), channel_id=1, source_target_pairs={{0,16},{8,24},{16,0},{24,8},{1,17},{9,25},{17,1},{25,9},{2,18},{10... | collective-permute-start | bytes 589832 | tf_op jit(solution)/shard_map/ppermute | solution.py:24
  80.7 15.1 %collective-permute-start.27 = (bf16[128,768]{1,0:T(8,128)(2,1)S(1)}, bf16[128,768]{1,0:T(8,128)(2,1)S(1)}, u32[]{:S(2)}, u32[]{:S(2)}) collective-permute-start(bf16[128,768]{1,0:T(8,128)(2,1)S(1)} %get-tuple-element.78), channel_id=1, source_target_pairs={{0,24},{8,16},{16,8},{24,0},{1,25},{9,17},{17,9},{25,1},{2,26},{10... | collective-permute-start | bytes 589832 | tf_op jit(solution)/shard_map/ppermute | solution.py:24
  82.1 11.4 %collective-permute-start.18 = (bf16[128,512]{1,0:T(8,128)(2,1)S(1)}, bf16[128,512]{1,0:T(8,128)(2,1)S(1)}, u32[]{:S(2)}, u32[]{:S(2)}) collective-permute-start(bf16[128,512]{1,0:T(8,128)(2,1)S(1)} %get-tuple-element.63), channel_id=1, source_target_pairs={{0,24},{8,16},{16,8},{24,0},{1,25},{9,17},{17,9},{25,1},{2,26},{10... | collective-permute-start | bytes 393224 | tf_op jit(solution)/shard_map/ppermute | solution.py:24
  (17 other events, 82.1 us)

commit v2 on v1

v2 whole, which is shorter than its diff:
```python
import functools
import math

import jax
import jax.numpy as jnp
from jax import lax
from jax.experimental import pallas as pl
from jax.experimental.pallas import tpu as pltpu
from jax.sharding import PartitionSpec as P

HDIM = 128
KERNEL = 31
LANES = 128
TILE = 64
TAPS = 32
CONV_COST = 600
ATTEND_COST = 24
BACK_COST = 48
PACK_LIMIT = 60
F32 = jnp.float32
BF16 = jnp.bfloat16
ROOT = 1.0 / math.sqrt(HDIM)


def swap(cells, axis, mask):
    count = lax.axis_size(axis)
    return lax.ppermute(cells, axis, [(i, i ^ mask) for i in range(count)])


def exchange(sent):
    return [sent[0]] + [swap(sent[k], "fsdp", k) for k in range(1, len(sent))]


def masks_of(count):
    return [1 << i for i in range(count.bit_length() - 1)]


def order_of(count):
    order = [0]
    for mask in reversed(masks_of(count)):
        order += [n ^ mask for n in order]
    return order


def call(body, outs, *operands, scratch=(), flops=0, near=True, stored=False, after=(), limit=40):
    vmem = pl.BlockSpec(memory_space=pltpu.VMEM)
    hbm = pl.BlockSpec(memory_space=pltpu.HBM)
    count = len(operands)
    moved = sum(x.size * x.dtype.itemsize for x in operands)
    moved += sum(math.prod(s) * jnp.dtype(t).itemsize for s, t in outs)
    return pl.pallas_call(
        lambda *refs: body(*refs[:count], *refs[count + len(after) :]),
        out_shape=[jax.ShapeDtypeStruct(s, t) for s, t in outs],
        in_specs=[vmem if near else hbm] * count + [pl.BlockSpec(memory_space=pl.ANY)] * len(after),
        out_specs=[hbm if stored else vmem] * len(outs),
        scratch_shapes=list(scratch),
        cost_estimate=pl.CostEstimate(flops=flops, bytes_accessed=moved, transcendentals=0),
        compiler_params=pltpu.CompilerParams(vmem_limit_bytes=limit * 1024 * 1024),
    )(*operands, *after)


def block(index, size, unit):
    return pl.ds(pl.multiple_of(index * size, unit), size)


def product(left, right, left_dim, right_dim):
    return lax.dot_general(
        left, right, (((left_dim,), (right_dim,)), ((), ())), preferred_element_type=F32
    )


def tree_sum(terms):
    while len(terms) > 1:
        terms = [terms[i] + terms[i + 1] for i in range(0, len(terms), 2)]
    return terms[0]


def places(top, end, rows):
    return (
        (0, 0, top[0], 0),
        (1, 0, top[1], 0),
        (2, 0, top[2], 0),
        (3, 0, top[2], rows),
        (0, 1, end[0], 0),
        (2, 1, end[1], 0),
        (1, 1, end[2], 0),
        (3, 1, end[2], rows),
    )


def split_up(outs, k, rows, columns, cells):
    own, beside, across, later_across, later_beside = outs
    half = rows // 2
    top, end = cells[:half, :], cells[half:, :]
    if k == 0:
        own[:, columns] = cells
    elif k == 1:
        beside[:half, columns] = top
        later_beside[:, columns] = end
    elif k == 2:
        later_across[:, columns] = top
        across[:half, columns] = end
    else:
        beside[half:, columns] = top
        across[half:, columns] = end


def pack_rows(groups, *refs):
    sources = refs[:5]
    outs = refs[5 : -groups - 6]
    weight_outs = refs[-groups - 6 : -6]
    held = refs[-6:-1]
    arrived = refs[-1]
    copies = [pltpu.make_async_copy(sources[i], held[i], arrived.at[i]) for i in range(5)]
    for copy in copies:
        copy.start()
    for copy in copies:
        copy.wait()
    me = lax.axis_index("fsdp")
    for k in range(groups):
        at = 0
        for source in held[:4]:
            width = source.shape[1] // groups
            there = slice(at, at + width)
            cells = source[:, block(me ^ k, width, LANES)]
            if groups == 4:
                split_up(outs, k, cells.shape[0], there, cells)
            else:
                outs[k][:, there] = cells
            at += width
        weight_outs[k][...] = held[4][:, block(me ^ k, held[4].shape[1] // groups, LANES)]


def stack_parts(mine, other, out):
    rows = mine.shape[0]
    out[:rows, :] = mine[...]
    out[rows:, :] = other[rows:, :]


def stack_all(*refs):
    at = 0
    for source in refs[:-1]:
        refs[-1][at : at + source.shape[0], :] = source[...]
        at += source.shape[0]


def attend(groups, *refs):
    folded = groups == 4
    pieces = refs[: 5 if folded else groups]
    rows_ref = refs[len(pieces)]
    upstream_ref = refs[len(pieces) + 1]
    outs = refs[len(pieces) + 2 :]
    edge = rows_ref.shape[1]
    me = lax.axis_index("fsdp")
    local = pieces[0].shape[0]
    half, width = outs[0].shape
    if folded:
        share = local // 2
        own, beside, later_across, across, later_beside = pieces
        ends = ((own, beside, later_across), (own, across, later_beside))
        for k, i, source, at in places(*ends, share):
            if k == 0:
                at = i * share
            start = pl.multiple_of((me ^ k) * local + i * share, share)
            rows_ref[pl.ds(start, share), :] = source[at : at + share, :edge]
            upstream_ref[pl.ds(start, share), :] = source[at : at + share, edge:]
    else:
        for k in range(groups):
            rows_ref[block(me ^ k, local, local), :] = pieces[k][:, :edge]
            upstream_ref[block(me ^ k, local, local), :] = pieces[k][:, edge:]
    for head in range(width // HDIM):
        at = head * HDIM
        queries = rows_ref[:, at : at + HDIM]
        keys = rows_ref[:, width + at : width + at + HDIM]
        values = rows_ref[:, 2 * width + at : 2 * width + at + HDIM]
        scores = product(queries, keys, 1, 1) * ROOT
        exponent = jnp.exp(scores - jnp.max(scores, axis=1, keepdims=True))
        probs = exponent * (1.0 / jnp.sum(exponent, axis=1, keepdims=True))
        mixed = product(probs.astype(BF16), values, 1, 0).astype(BF16)
        for i, out in enumerate(outs):
            out[:, at : at + HDIM] = mixed[i * half : (i + 1) * half, :]


def join_weight(groups, count, mine, other, out):
    me = lax.axis_index("frame")
    rows = mine.shape[0] // (count // 2 * groups)
    width = rows * count
    for i, n in enumerate(order_of(count)[: count // 2]):
        for k in range(groups):
            at = (i * groups + k) * rows
            for core, source in enumerate((mine, other)):
                start = pl.multiple_of(k * width + (me ^ n ^ core) * rows, rows)
                out[pl.ds(start, rows), :] = source[at : at + rows, :]


def shifted(padded, start, tile):
    for residue in range(8):
        taps = range(residue, KERNEL, 8)
        reach = 8 * (len(taps) - 1)
        rows = padded[start + 1 + residue : start + 1 + residue + tile + reach, :]
        yield taps, rows


def convolve(groups, *refs):
    pieces = refs[: -groups - 8]
    weight, taps_ref, attention, projected_ref, slope_ref = refs[-groups - 8 : -groups - 3]
    ahead = refs[-groups - 3 : -3]
    padded, taps, result = refs[-3:]
    me = lax.axis_index("fsdp")
    frames = attention.shape[0]
    channels = weight.shape[1]
    local = frames // groups
    padded[0:16, :] = jnp.zeros((16, LANES), F32)
    padded[frames + 16 : frames + 32, :] = jnp.zeros((16, LANES), F32)
    if groups == 4:
        half, depth = pieces[0].shape
        for k, i, source, at in places(pieces[:3], pieces[3:], half):
            start = i * half
            attention[start : start + half, k * depth : (k + 1) * depth] = source[at : at + half, :]
    else:
        depth = pieces[0].shape[1]
        for k in range(groups):
            attention[:, k * depth : (k + 1) * depth] = pieces[k][...]
    projected_ref[...] = product(attention[...], weight[...], 1, 0).astype(BF16)

    def lane_block(c, carry):
        columns = block(c, LANES, LANES)
        padded[16 : frames + 16, :] = projected_ref[:, columns].astype(F32)
        taps[0:KERNEL, :] = taps_ref[:, block(me * (channels // LANES) + c, LANES, LANES)].astype(F32)
        for start in range(0, frames, TILE):
            conv = jnp.zeros((TILE, LANES), F32)
            for indices, rows in shifted(padded, start, TILE):
                for at, j in enumerate(indices):
                    conv += taps[j : j + 1, :] * rows[8 * at : 8 * at + TILE, :]
            gate = 1.0 / (1.0 + jnp.exp(-conv))
            own = padded[start + 16 : start + 16 + TILE, :]
            result[start : start + TILE, :] = own + conv * gate
            slope_ref[start : start + TILE, columns] = gate * (1.0 + conv * (1.0 - gate))
        for k in range(groups):
            ahead[k][:, columns] = result[block(me ^ k, local, local), :].astype(BF16)
        return carry

    lax.fori_loop(0, channels // LANES, lane_block, 0)


def convolve_back(groups, *refs):
    upstream, projected_ref, slope_ref, weight, taps_ref, grad_ref, tap_ref = refs[:7]
    outs = refs[-groups - 4 : -4]
    padded, taps, above, sums = refs[-4:]
    me = lax.axis_index("fsdp")
    frames, channels = projected_ref.shape
    local = frames // groups
    depth = weight.shape[0] // groups
    padded[0:16, :] = jnp.zeros((16, LANES), F32)
    padded[frames + 16 : frames + 32, :] = jnp.zeros((16, LANES), F32)

    def lane_block(c, carry):
        columns = block(c, LANES, LANES)
        above[...] = upstream[:, columns].astype(F32)
        taps[0:KERNEL, :] = taps_ref[:, block(me * (channels // LANES) + c, LANES, LANES)].astype(F32)
        padded[16 : frames + 16, :] = (above[...] * slope_ref[:, columns]).astype(BF16).astype(F32)
        sums[...] = jnp.zeros(sums.shape, F32)
        for start in range(0, frames, TILE):
            total = above[start : start + TILE, :]
            own = projected_ref[start : start + TILE, columns].astype(F32)
            for indices, rows in shifted(padded, start, TILE):
                for at, j in enumerate(indices):
                    part = rows[8 * at : 8 * at + TILE, :]
                    tap = KERNEL - 1 - j
                    total += taps[tap : tap + 1, :] * part
                    terms = own * part
                    sums[8 * tap : 8 * tap + 8, :] += tree_sum(
                        [terms[8 * i : 8 * i + 8, :] for i in range(TILE // 8)]
                    )
            grad_ref[start : start + TILE, columns] = total.astype(BF16)
        tap_ref[:, columns] = jnp.sum(sums[...].reshape(TAPS, 8, LANES), axis=1)
        return carry

    lax.fori_loop(0, channels // LANES, lane_block, 0)
    grads = grad_ref[...]
    for k in range(groups):
        terms = product(grads, weight[k * depth : (k + 1) * depth, :], 1, 1).astype(BF16)
        if groups == 4:
            half = frames // 2
            top, end = outs[k % 2], outs[2 + k // 2]
            top[k // 2 * half : (k // 2 + 1) * half, :] = terms[:half, :]
            end[k % 2 * half : (k % 2 + 1) * half, :] = terms[half:, :]
        else:
            outs[k][...] = terms


def weight_terms(groups, order, rows, *refs):
    attention, grads, tap_ref = refs[:3]
    outs = refs[3:5]
    terms = refs[5]
    me = lax.axis_index("frame")
    depth = attention.shape[1] // groups
    half = len(order) // 2
    for k in range(groups):
        terms[...] = product(attention[:, k * depth : (k + 1) * depth], grads[...], 0, 0)
        for i, n in enumerate(order):
            there = pl.ds(pl.multiple_of((me ^ n) * rows, rows), rows)
            at = TAPS + ((i % half) * groups + k) * rows
            outs[i // half][at : at + rows, :] = terms[there, :].astype(BF16)
    for out in outs:
        out[0:TAPS, :] = tap_ref[...].astype(BF16)


def plain_terms(attention, grads, out):
    out[...] = product(attention[...], grads[...], 0, 0).astype(BF16)


def add_halves(mine, other, *outs):
    total = mine[...].astype(F32) + other[...].astype(F32)
    share = (total.shape[0] - TAPS) // len(outs)
    for k, out in enumerate(outs):
        at = TAPS + k * share
        out[0:TAPS, :] = total[0:TAPS, :].astype(BF16)
        out[TAPS:, :] = total[at : at + share, :].astype(BF16)


def fold(mine, other, stays, goes):
    total = (mine[...].astype(F32) + other[...].astype(F32)).astype(BF16)
    half = stays.shape[0]
    stays[...] = total[:half, :]
    goes[...] = total[half:, :]


def attend_back(groups, *refs):
    rows_ref = refs[0]
    upstream = refs[1 : groups + 1]
    outs = refs[groups + 1 : -2]
    grads, result = refs[-2:]
    me = lax.axis_index("fsdp")
    width = upstream[0].shape[1]
    local = outs[0].shape[0]
    if groups == 4:
        half = upstream[0].shape[0]
        for i in range(2):
            total = upstream[2 * i][...].astype(F32) + upstream[2 * i + 1][...].astype(F32)
            grads[i * half : (i + 1) * half, :] = total.astype(BF16)
    else:
        grads[...] = tree_sum([ref[...].astype(F32) for ref in upstream]).astype(BF16)
    for head in range(width // HDIM):
        at = head * HDIM
        queries = rows_ref[:, at : at + HDIM]
        keys = rows_ref[:, width + at : width + at + HDIM]
        values = rows_ref[:, 2 * width + at : 2 * width + at + HDIM]
        above = grads[:, at : at + HDIM]
        scores = product(queries, keys, 1, 1) * ROOT
        exponent = jnp.exp(scores - jnp.max(scores, axis=1, keepdims=True))
        weights = exponent * (1.0 / jnp.sum(exponent, axis=1, keepdims=True))
        slopes = product(above, values, 1, 1)
        row_dot = jnp.sum(weights * slopes, axis=1, keepdims=True)
        grad_scores = (weights * (slopes - row_dot)).astype(BF16)
        result[:, at : at + HDIM] = (product(grad_scores, keys, 1, 0) * ROOT).astype(BF16)
        result[:, width + at : width + at + HDIM] = (
            product(grad_scores, queries, 0, 0) * ROOT
        ).astype(BF16)
        result[:, 2 * width + at : 2 * width + at + HDIM] = product(
            weights.astype(BF16), above, 0, 0
        ).astype(BF16)
    for k in range(groups):
        piece = result[block(me ^ k, local, local), :]
        if groups == 4:
            split_up(outs, k, local, slice(None), piece)
        else:
            outs[k][...] = piece


def join_all(groups, scale, *refs):
    folded = groups == 4
    count = 5 if folded else groups
    ahead = refs[: (len(refs) - count - 9) // 2]
    sums = refs[len(ahead) : -count - 9]
    pieces = refs[-count - 9 : -9]
    outs = refs[-9:-3]
    weight_ref, tap_ref, sent = refs[-3:]
    me = lax.axis_index("fsdp")
    copies = []

    def store(source, target):
        copy = pltpu.make_async_copy(source, target, sent.at[len(copies)])
        copy.start()
        copies.append(copy)

    local, width = pieces[0].shape
    width //= 3
    if folded:
        share = local // 2
        own, beside, later_across, across, later_beside = pieces
        ends = ((own, beside, later_across), (own, across, later_beside))
        found = [(k, i * share, share, x, at) for k, i, x, at in places(*ends, share) if k]
        found.append((0, 0, local, own, 0))
    else:
        found = [(k, 0, local, pieces[k], 0) for k in range(groups)]
    for k, start, size, source, first in found:
        columns = block(me ^ k, width, LANES)
        for at in range(3):
            part = source.at[first : first + size, at * width : (at + 1) * width]
            store(part, outs[1 + at].at[0, start : start + size, columns])
    rows, channels = sums[0].shape
    for k in range(groups):
        columns = block(me ^ k, channels, LANES)
        i = min(k, len(ahead) - 1)
        at = local if k > i else 0
        store(ahead[i].at[at : at + local], outs[0].at[0, :, columns])
        at = rows if k > i else 0
        tap_ref[:, columns] = sums[i][at : at + KERNEL, :].astype(F32) * scale
        weight_ref[:, columns] = sums[i][at + TAPS : at + rows, :].astype(F32) * scale
    store(weight_ref, outs[4])
    store(tap_ref, outs[5])
    for copy in copies:
        copy.wait()


def stack(*arrays, after=()):
    shape = (sum(x.shape[0] for x in arrays),) + arrays[0].shape[1:]
    return call(stack_all, [(shape, arrays[0].dtype)], *arrays, after=after)[0]


def exchange_split(sent, after=()):
    if len(sent) != 5:
        return exchange(sent)
    own, beside, across, later_across, later_beside = sent
    shape = [(beside.shape, beside.dtype)]
    beside, across = swap(beside, "fsdp", 1), swap(across, "fsdp", 2)
    (later_across,) = call(stack_parts, shape, later_across, beside, after=after)
    (later_beside,) = call(stack_parts, shape, later_beside, across, after=after)
    return [own, beside, swap(later_across, "fsdp", 2), across, swap(later_beside, "fsdp", 1)]


def turn(sent):
    if len(sent) != 4:
        return exchange(sent)
    rows = sent[0].shape[0]
    first = swap(stack(sent[1], sent[3]), "fsdp", 1)
    second = swap(call(stack_parts, [((2 * rows, sent[0].shape[1]), BF16)], sent[2], first)[0], "fsdp", 2)
    return [sent[0], first, second]


def gather_weight(gathered, masks, groups, count, after):
    rows, channels = gathered.shape[0] * 2 ** (len(masks) + 1) // (groups * count), gathered.shape[1]
    for mask in masks:
        gathered = stack(gathered, swap(gathered, "frame", mask), after=after)
    other = swap(gathered, "frame", 1)
    if rows % 16 == 0:
        return call(
            functools.partial(join_weight, groups, count),
            [((groups * count * rows, channels), BF16)],
            gathered,
            other,
        )[0]
    me = lax.axis_index("frame")
    order = order_of(count)
    place = jnp.array([order.index(n) for n in range(count)])
    both = jnp.concatenate([gathered, other], axis=0).reshape(count, groups, rows, channels)
    ordered = jnp.take(both, place[me ^ jnp.arange(count)], axis=0)
    return ordered.transpose(1, 0, 2, 3).reshape(groups * count * rows, channels)


def weight_halves(attention, grads, tap_terms, groups, count, rows):
    channels = grads.shape[1]
    depth = attention.shape[1] // groups
    share = count // 2 * groups * rows
    bits = count.bit_length() - 1
    order = [sum((i >> b & 1) << (bits - 1 - b) for b in range(bits)) for i in range(count)]
    if rows % 16 == 0:
        halves = call(
            functools.partial(weight_terms, groups, order, rows),
            [((TAPS + share, channels), BF16)] * 2,
            attention,
            grads,
            tap_terms,
            scratch=[pltpu.VMEM((depth, channels), F32)],
        )
    else:
        (terms,) = call(plain_terms, [((groups * depth, channels), BF16)], attention, grads)
        me = lax.axis_index("frame")
        terms = terms.reshape(groups, count, rows, channels)
        terms = jnp.take(terms, me ^ jnp.array(order), axis=1)
        terms = terms.transpose(1, 0, 2, 3).reshape(2, share, channels)
        halves = [jnp.concatenate([tap_terms.astype(BF16), x], axis=0) for x in terms]
    return halves


def add_up(halves, mask, pieces):
    mine, other = halves
    share = (mine.shape[0] - TAPS) // pieces
    return call(
        add_halves,
        [((TAPS + share, mine.shape[1]), BF16)] * pieces,
        mine,
        swap(other, "frame", mask),
    )


def shards(queries, key_rows, value_rows, out_weight, conv_weight, grad_out):
    local, inner = queries.shape[1:]
    rows, model = out_weight.shape
    groups = lax.axis_size("fsdp")
    count = lax.axis_size("frame")
    frames = local * groups
    width = inner // groups
    channels = model // groups
    scale = 1.0 / math.sqrt(frames * count)
    conv_flops = CONV_COST * KERNEL * frames * channels

    folded = groups == 4
    def split(size):
        shape, small = ((local, size), BF16), ((local // 2, size), BF16)
        return [shape, shape, shape, small, small] if folded else [shape] * groups

    sent = call(
        functools.partial(pack_rows, groups),
        split(3 * width + channels) + [((rows, channels), BF16)] * groups,
        queries[0],
        key_rows[0],
        value_rows[0],
        grad_out[0],
        out_weight,
        near=False,
        limit=PACK_LIMIT,
        scratch=[pltpu.VMEM((local, inner), BF16)] * 3
        + [pltpu.VMEM((local, model), BF16), pltpu.VMEM((rows, model), BF16)]
        + [pltpu.SemaphoreType.DMA((5,))],
    )
    gathered = stack(*exchange(sent[-groups:]))
    pieces = exchange_split(sent[:-groups], after=[gathered])
    first, *masks = reversed(masks_of(count)[1:])
    gathered = stack(gathered, swap(gathered, "frame", first))
    held, upstream, *own = call(
        functools.partial(attend, groups),
        [((frames, 3 * width), BF16), ((frames, channels), BF16)]
        + ([((frames // 2, width), BF16)] * 2 if folded else [((frames, width), BF16)]),
        *pieces,
        flops=ATTEND_COST * frames * frames * width,
        after=[gathered],
    )
    gathered = stack(gathered, after=own[:1])
    if folded:
        top, end = own
        beside, across = swap(top, "fsdp", 1), swap(end, "fsdp", 2)
        attention = [top, beside, swap(stack(top, beside), "fsdp", 2)]
        attention += [end, across, swap(stack(end, across), "fsdp", 1)]
        weight = gather_weight(gathered, masks, groups, count, [beside, across])
    else:
        attention = exchange(own * groups)
        weight = gather_weight(gathered, masks, groups, count, attention[1:2])

    outs = call(
        functools.partial(convolve, groups),
        [((frames, inner), BF16), ((frames, channels), BF16), ((frames, channels), F32)]
        + [((local, channels), BF16)] * groups,
        *attention,
        weight,
        conv_weight,
        scratch=[
            pltpu.VMEM((frames + 32, LANES), F32),
            pltpu.VMEM((TAPS, LANES), F32),
            pltpu.VMEM((frames, LANES), F32),
        ],
        flops=conv_flops,
    )
    whole, projected, slope = outs[:3]
    ahead = turn(outs[3:])

    outs = call(
        functools.partial(convolve_back, groups),
        [((frames, channels), BF16), ((TAPS, channels), F32)] + [((frames, width), BF16)] * groups,
        upstream,
        projected,
        slope,
        weight,
        conv_weight,
        scratch=[
            pltpu.VMEM((frames + 32, LANES), F32),
            pltpu.VMEM((TAPS, LANES), F32),
            pltpu.VMEM((frames, LANES), F32),
            pltpu.VMEM((8 * TAPS, LANES), F32),
        ],
        flops=conv_flops * 3 // 2,
    )
    grads, tap_terms = outs[:2]
    if folded:
        stay_top, go_top, stay_end, go_end = outs[2:]
        shapes = [((frames // 2, width), BF16)] * 2
        stay_top, go_top = call(fold, shapes, stay_top, swap(go_top, "fsdp", 1))
        stay_end, go_end = call(fold, shapes, stay_end, swap(go_end, "fsdp", 2))
        above = [stay_top, swap(go_top, "fsdp", 2), stay_end, swap(go_end, "fsdp", 1)]
    else:
        above = exchange(outs[2:])
    halves = weight_halves(whole, grads, tap_terms, groups, count, rows)
    masks = masks_of(count)
    for mask in masks[:-1]:
        halves = add_up(halves, mask, 2)
    sent = call(
        functools.partial(attend_back, groups),
        split(3 * width),
        held,
        *above,
        scratch=[pltpu.VMEM((frames, width), BF16), pltpu.VMEM((frames, 3 * width), BF16)],
        flops=BACK_COST * frames * frames * width,
        after=[halves[1]],
    )
    pieces = exchange_split(sent)
    sums = turn(add_up(halves, masks[-1], groups))
    return tuple(
        call(
            functools.partial(join_all, groups, scale),
            [((1, local, model), BF16)]
            + [((1, local, inner), BF16)] * 3
            + [((rows, model), F32), ((KERNEL, model), F32)],
            *ahead,
            *sums,
            *pieces,
            stored=True,
            scratch=[
                pltpu.VMEM((rows, model), F32),
                pltpu.VMEM((KERNEL, model), F32),
                pltpu.SemaphoreType.DMA((8 * groups,)),
            ],
        )
    )


def solution(mesh):
    return jax.shard_map(
        shards,
        mesh=mesh,
        in_specs=(
            P("frame", "fsdp", None),
            P("frame", "fsdp", None),
            P("frame", "fsdp", None),
            P(("fsdp", "frame"), None),
            P(),
            P("frame", "fsdp", None),
        ),
        out_specs=(
            P("frame", "fsdp", None),
            P("frame", "fsdp", None),
            P("frame", "fsdp", None),
            P("frame", "fsdp", None),
            P(("fsdp", "frame"), None),
            P(),
        ),
        check_vma=False,
    )
```

time: 99.8 us -> 94.2 us (0.944)
  starting transfers between devices: 40.3 us -> 35.5 us
  local copies, waits for them, and re-layouts: 3.77 us -> 0.78 us
  waiting for transfers between devices: 37 us -> 38.2 us
    ppermute x35 -> x29, starting transfers between devices: 40.3 us -> 35.5 us  [swap(): return lax.ppermute(cells, axis, [(i, i ^ mask) for i in range(count)])]
    unnamed x15 -> x10, local copies, waits for them, and re-layouts: 3.76 us -> 0.78 us
    ppermute x35 -> x29, waiting for transfers between devices: 37 us -> 38.2 us  [swap(): return lax.ppermute(cells, axis, [(i, i ^ mask) for i in range(count)])]
    pallas_call x14 -> x27, Pallas kernels: 17.7 us -> 18.6 us  [call(): pl.pallas_call(lambda *refs: body(*refs[:count], *refs[count + len(after)...]
  transfers between devices with their start and end apart: 35 -> 29, of which waited for: 12 -> 16; matrix products, arithmetic and copies ran while one was open for 0% -> 0% of each run, Pallas kernels for 11% -> 3%
where the time goes in v2:
time: 94.2 us; the launch traced here: 94 us
  waiting for transfers between devices  38.2 us (41%)
  starting transfers between devices  35.5 us (38%)
  Pallas kernels  18.6 us (20%)
    ppermute x29, waiting for transfers between devices, swap(): return lax.ppermute(cells, axis, [(i, i ^ mask) for i in range(count)])  38.2 us
    ppermute x29, starting transfers between devices, swap(): return lax.ppermute(cells, axis, [(i, i ^ mask) for i in range(count)])  35.5 us
    pallas_call x27, Pallas kernels, call(): pl.pallas_call(lambda *refs: body(*refs[:count], *refs[count + len(after)...  18.6 us
  transfers between devices with their start and end apart: 29, of which 16 were waited for; matrix products, arithmetic and copies ran while one was open for 0% of the time, Pallas kernels for 3%

profile of v2, /device:TPU:0, one launch (start us, length us, event | category | flops | bytes accessed | tf_op | source)
XLA Modules:
  0.0 94.0 jit_solution(4557407671304946484)
XLA Ops:
  0.6 2.6 %shard_map.109 = (bf16[128,1280]{1,0:T(8,128)(2,1)}, bf16[128,1280]{1,0:T(8,128)(2,1)}, bf16[128,1280]{1,0:T(8,128)(2,1)}, bf16[64,1280]{1,0:T(8,128)(2,1)}, bf1...) custom-call(bf16[128,1024]{1,0:T(8,128)(2,1)} %bitcast.5, ...), custom_call_target="tpu_custom_call" | custom-call | bytes 2883584 | tf_op jit(solution)/shard_map/pallas_call | solution.py:51
  3.2 3.0 %collective-permute-start = (bf16[128,1280]{1,0:T(8,128)(2,1)}, bf16[128,1280]{1,0:T(8,128)(2,1)S(1)}, u32[]{:S(2)}, u32[]{:S(2)}) collective-permute-start(bf16[128,1280]{1,0:T(8,128)(2,1)} %get-tuple-element.52), channel_id=1, source_target_pairs={{0,8},{8,0},{16,24},{24,16},{1,9},{9,1},{17,25},{25,17},{2,10},{10... | collective-permute-start | bytes 983048 | tf_op jit(solution)/shard_map/ppermute | solution.py:27
  6.2 1.5 %collective-permute-start.5 = (bf16[128,1280]{1,0:T(8,128)(2,1)}, bf16[128,1280]{1,0:T(8,128)(2,1)S(1)}, u32[]{:S(2)}, u32[]{:S(2)}) collective-permute-start(bf16[128,1280]{1,0:T(8,128)(2,1)} %get-tuple-element.58), channel_id=1, source_target_pairs={{0,16},{8,24},{16,0},{24,8},{1,17},{9,25},{17,1},{25,9},{2,18},{10... | collective-permute-start | bytes 983048 | tf_op jit(solution)/shard_map/ppermute | solution.py:27
  8.3 2.9 %collective-permute-start.3 = (bf16[32,512]{1,0:T(8,128)(2,1)}, bf16[32,512]{1,0:T(8,128)(2,1)S(1)}, u32[]{:S(2)}, u32[]{:S(2)}) collective-permute-start(bf16[32,512]{1,0:T(8,128)(2,1)} %get-tuple-element.57), channel_id=1, source_target_pairs={{0,24},{8,16},{16,8},{24,0},{1,25},{9,17},{17,9},{25,1},{2,26},{10... | collective-permute-start | bytes 98312 | tf_op jit(solution)/shard_map/ppermute | solution.py:27
  11.2 4.0 %collective-permute-done.1.refs_1_ = bf16[32,512]{1,0:T(8,128)(2,1)S(1)} collective-permute-done((bf16[32,512]{1,0:T(8,128)(2,1)}, bf16[32,512]{1,0:T(8,128)(2,1)S(1)}, u32[]{:S(2)}, u32[]{:S(2)}) %collective-permute-start.1) | collective-permute-done | bytes 32800 | tf_op jit(solution)/shard_map/ppermute | solution.py:27
  15.2 1.8 %collective-permute-done.2.refs_2_ = bf16[32,512]{1,0:T(8,128)(2,1)S(1)} collective-permute-done((bf16[32,512]{1,0:T(8,128)(2,1)}, bf16[32,512]{1,0:T(8,128)(2,1)S(1)}, u32[]{:S(2)}, u32[]{:S(2)}) %collective-permute-start.2) | collective-permute-done | bytes 32800 | tf_op jit(solution)/shard_map/ppermute | solution.py:27
  17.9 1.6 %collective-permute-start.4 = (bf16[128,1280]{1,0:T(8,128)(2,1)S(1)}, bf16[128,1280]{1,0:T(8,128)(2,1)S(1)}, u32[]{:S(2)}, u32[]{:S(2)}) collective-permute-start(bf16[128,1280]{1,0:T(8,128)(2,1)S(1)} %shard_map.111), channel_id=1, source_target_pairs={{0,16},{8,24},{16,0},{24,8},{1,17},{9,25},{17,1},{25,9},{2,18},{10... | collective-permute-start | bytes 983048 | tf_op jit(solution)/shard_map/ppermute | solution.py:27
  20.1 2.6 %collective-permute-start.7 = (bf16[128,512]{1,0:T(8,128)(2,1)S(1)}, bf16[128,512]{1,0:T(8,128)(2,1)S(1)}, u32[]{:S(2)}, u32[]{:S(2)}) collective-permute-start(bf16[128,512]{1,0:T(8,128)(2,1)S(1)} %shard_map.110.refs_2_.refs_0_), channel_id=1, source_target_pairs={{0,4},{1,5},{2,6},{3,7},{4,0},{5,1},{6,2},{7,3},{8,12},{9,13},{10,... | collective-permute-start | bytes 393224 | tf_op jit(solution)/shard_map/ppermute | solution.py:27
  22.7 4.9 %collective-permute-done.7.refs_1_ = bf16[128,512]{1,0:T(8,128)(2,1)S(1)} collective-permute-done((bf16[128,512]{1,0:T(8,128)(2,1)S(1)}, bf16[128,512]{1,0:T(8,128)(2,1)S(1)}, u32[]{:S(2)}, u32[]{:S(2)}) %collective-permute-start.7) | collective-permute-done | bytes 131104 | tf_op jit(solution)/shard_map/ppermute | solution.py:27
  27.6 1.4 %shard_map.114 = (bf16[512,768]{1,0:T(8,128)(2,1)S(1)}, bf16[512,512]{1,0:T(8,128)(2,1)S(1)}, bf16[256,256]{1,0:T(8,128)(2,1)S(1)}, bf16[256,256]{1,0:T(8,128)(2,1)S(1)}) custom-call(bf16[128,1280]{1,0:T(8,128)(2,1)S(1)} %copy-done.3, bf16[128,1280]{1,0:T(8,128)(2,1)S(1)} %collective-permute-done.refs_1_, ...), custom_call_target="tpu_custom_call" | custom-call | flops 1610612736 | bytes 3211264 | tf_op jit(solution)/shard_map/pallas_call | solution.py:51
  32.4 2.8 %collective-permute-done.10.refs_1_.refs_3_.refs_4_ = bf16[256,256]{1,0:T(8,128)(2,1)S(1)} collective-permute-done((bf16[256,256]{1,0:T(8,128)(2,1)S(1)}, bf16[256,256]{1,0:T(8,128)(2,1)S(1)}, u32[]{:S(2)}, u32[]{:S(2)}) %collective-permute-start.10) | collective-permute-done | bytes 131104 | tf_op jit(solution)/shard_map/ppermute | solution.py:27
  38.9 6.4 %collective-permute-done.11.refs_5_ = bf16[512,256]{1,0:T(8,128)(2,1)S(1)} collective-permute-done((bf16[512,256]{1,0:T(8,128)(2,1)S(1)}, bf16[512,256]{1,0:T(8,128)(2,1)S(1)}, u32[]{:S(2)}, u32[]{:S(2)}) %collective-permute-start.11) | collective-permute-done | bytes 262176 | tf_op jit(solution)/shard_map/ppermute | solution.py:27
  46.1 3.4 %shard_map.120 = (bf16[512,1024]{1,0:T(8,128)(2,1)S(1)}, bf16[512,512]{1,0:T(8,128)(2,1)S(1)}, f32[512,512]{1,0:T(8,128)S(1)}, bf16[128,512]{1,0:T(8,128)(2,1)S(...) custom-call(bf16[256,256]{1,0:T(8,128)(2,1)S(1)} %get-tuple-element.60.refs_0_.refs_1_,, ...), custom_call_target="tpu_custom_call" | custom-call | flops 4875878400 | bytes 5369856 | tf_op jit(solution)/shard_map/pallas_call | solution.py:51
  49.5 5.6 %shard_map.123 = (bf16[512,512]{1,0:T(8,128)(2,1)S(1)}, f32[32,512]{1,0:T(8,128)S(1)}, bf16[512,256]{1,0:T(8,128)(2,1)S(1)}, bf16[512,256]{1,0:T(8,128)(2,1)S(1)...) custom-call(bf16[512,512]{1,0:T(8,128)(2,1)S(1)} %get-tuple-element.67.refs_0_, ...), custom_call_target="tpu_custom_call" | custom-call | flops 7313817600 | bytes 4911104 | tf_op jit(solution)/shard_map/pallas_call | solution.py:51
  59.1 5.6 %collective-permute-done.21.refs_1_ = bf16[512,256]{1,0:T(8,128)(2,1)S(1)} collective-permute-done((bf16[512,256]{1,0:T(8,128)(2,1)S(1)}, bf16[512,256]{1,0:T(8,128)(2,1)S(1)}, u32[]{:S(2)}, u32[]{:S(2)}) %collective-permute-start.21) | collective-permute-done | bytes 262176 | tf_op jit(solution)/shard_map/ppermute | solution.py:27
  67.0 1.2 %collective-permute-start.14 = (bf16[256,512]{1,0:T(8,128)(2,1)S(1)}, bf16[256,512]{1,0:T(8,128)(2,1)S(1)}, u32[]{:S(2)}, u32[]{:S(2)}) collective-permute-start(bf16[256,512]{1,0:T(8,128)(2,1)S(1)} %shard_map.121), channel_id=1, source_target_pairs={{0,8},{8,0},{16,24},{24,16},{1,9},{9,1},{17,25},{25,17},{2,10},{10... | collective-permute-start | bytes 786440 | tf_op jit(solution)/shard_map/ppermute | solution.py:27
  68.3 3.1 %collective-permute-start.18 = (bf16[160,512]{1,0:T(8,128)(2,1)S(1)}, bf16[160,512]{1,0:T(8,128)(2,1)S(1)}, u32[]{:S(2)}, u32[]{:S(2)}) collective-permute-start(bf16[160,512]{1,0:T(8,128)(2,1)S(1)} %get-tuple-element.77.refs_5_), channel_id=1, source_target_pairs={{0,4},{1,5},{2,6},{3,7},{4,0},{5,1},{6,2},{7,3},{8,12},{9,13},{10,... | collective-permute-start | bytes 491528 | tf_op jit(solution)/shard_map/ppermute | solution.py:27
  72.5 2.6 %shard_map.132 = (bf16[128,768]{1,0:T(8,128)(2,1)S(1)}, bf16[128,768]{1,0:T(8,128)(2,1)S(1)}, bf16[128,768]{1,0:T(8,128)(2,1)S(1)}, bf16[64,768]{1,0:T(8,128)(2,1)S(1)}, bf16[64,768]{1,0:T(8,128)(2,1)S(1)}) custom-call(bf16[512,768]{1,0:T(8,128)(2,1)S(1)} %get-tuple-element.82.refs_0_, bf16[256,256]{1,0:T(8,128)(2,1)S(1)} %get-tuple-element.85.refs_1_, ...), custom_call_target="tpu_custom_call" | custom-call | flops 3221225472 | bytes 2097152 | tf_op jit(solution)/shard_map/pallas_call | solution.py:51
  82.1 1.8 %collective-permute-done.27.refs_1_.refs_9_ = bf16[128,768]{1,0:T(8,128)(2,1)S(1)} collective-permute-done((bf16[128,768]{1,0:T(8,128)(2,1)S(1)}, bf16[128,768]{1,0:T(8,128)(2,1)S(1)}, u32[]{:S(2)}, u32[]{:S(2)}) %collective-permute-start.27) | collective-permute-done | bytes 196640 | tf_op jit(solution)/shard_map/ppermute | solution.py:27
  83.9 1.2 %collective-permute-start.28 = (bf16[128,768]{1,0:T(8,128)(2,1)S(1)}, bf16[128,768]{1,0:T(8,128)(2,1)S(1)}, u32[]{:S(2)}, u32[]{:S(2)}) collective-permute-start(bf16[128,768]{1,0:T(8,128)(2,1)S(1)} %shard_map.134), channel_id=1, source_target_pairs={{0,8},{8,0},{16,24},{24,16},{1,9},{9,1},{17,25},{25,17},{2,10},{10... | collective-permute-start | bytes 589832 | tf_op jit(solution)/shard_map/ppermute | solution.py:27
  86.5 2.5 %collective-permute-done.15.refs_2_ = bf16[256,512]{1,0:T(8,128)(2,1)S(1)} collective-permute-done((bf16[256,512]{1,0:T(8,128)(2,1)S(1)}, bf16[256,512]{1,0:T(8,128)(2,1)S(1)}, u32[]{:S(2)}, u32[]{:S(2)}) %collective-permute-start.15) | collective-permute-done | bytes 262176 | tf_op jit(solution)/shard_map/ppermute | solution.py:27
  89.0 2.1 %collective-permute-done.26.refs_8_ = bf16[128,768]{1,0:T(8,128)(2,1)S(1)} collective-permute-done((bf16[128,768]{1,0:T(8,128)(2,1)S(1)}, bf16[128,768]{1,0:T(8,128)(2,1)S(1)}, u32[]{:S(2)}, u32[]{:S(2)}) %collective-permute-start.26) | collective-permute-done | bytes 196640 | tf_op jit(solution)/shard_map/ppermute | solution.py:27
  91.1 1.4 %collective-permute-done.20.refs_5_ = bf16[128,512]{1,0:T(8,128)(2,1)S(1)} collective-permute-done((bf16[128,512]{1,0:T(8,128)(2,1)S(1)}, bf16[128,512]{1,0:T(8,128)(2,1)S(1)}, u32[]{:S(2)}, u32[]{:S(2)}) %collective-permute-start.20) | collective-permute-done | bytes 131104 | tf_op jit(solution)/shard_map/ppermute | solution.py:27
  92.5 1.5 %shard_map.135 = (bf16[1,128,2048]{2,1,0:T(8,128)(2,1)}, bf16[1,128,1024]{2,1,0:T(8,128)(2,1)}, bf16[1,128,1024]{2,1,0:T(8,128)(2,1)}, bf16[1,128,1024]{2,1,0:T(...) custom-call(bf16[128,512]{1,0:T(8,128)(2,1)S(1)} %get-tuple-element.62.refs_0_, ...), custom_call_target="tpu_custom_call" | custom-call | bytes 3792896 | tf_op jit(solution)/shard_map/pallas_call | solution.py:51
  (71 shorter events, 25.5 us)
Async XLA Ops:
  3.2 14.6 %collective-permute-start = (bf16[128,1280]{1,0:T(8,128)(2,1)}, bf16[128,1280]{1,0:T(8,128)(2,1)S(1)}, u32[]{:S(2)}, u32[]{:S(2)}) collective-permute-start(bf16[128,1280]{1,0:T(8,128)(2,1)} %get-tuple-element.52), channel_id=1, source_target_pairs={{0,8},{8,0},{16,24},{24,16},{1,9},{9,1},{17,25},{25,17},{2,10},{10... | collective-permute-start | bytes 983048 | tf_op jit(solution)/shard_map/ppermute | solution.py:27
  6.2 13.2 %collective-permute-start.5 = (bf16[128,1280]{1,0:T(8,128)(2,1)}, bf16[128,1280]{1,0:T(8,128)(2,1)S(1)}, u32[]{:S(2)}, u32[]{:S(2)}) collective-permute-start(bf16[128,1280]{1,0:T(8,128)(2,1)} %get-tuple-element.58), channel_id=1, source_target_pairs={{0,16},{8,24},{16,0},{24,8},{1,17},{9,25},{17,1},{25,9},{2,18},{10... | collective-permute-start | bytes 983048 | tf_op jit(solution)/shard_map/ppermute | solution.py:27
  7.8 7.4 %collective-permute-start.1 = (bf16[32,512]{1,0:T(8,128)(2,1)}, bf16[32,512]{1,0:T(8,128)(2,1)S(1)}, u32[]{:S(2)}, u32[]{:S(2)}) collective-permute-start(bf16[32,512]{1,0:T(8,128)(2,1)} %get-tuple-element.55), channel_id=1, source_target_pairs={{0,8},{8,0},{16,24},{24,16},{1,9},{9,1},{17,25},{25,17},{2,10},{10... | collective-permute-start | bytes 98312 | tf_op jit(solution)/shard_map/ppermute | solution.py:27
  8.3 8.7 %collective-permute-start.2 = (bf16[32,512]{1,0:T(8,128)(2,1)}, bf16[32,512]{1,0:T(8,128)(2,1)S(1)}, u32[]{:S(2)}, u32[]{:S(2)}) collective-permute-start(bf16[32,512]{1,0:T(8,128)(2,1)} %get-tuple-element.56), channel_id=1, source_target_pairs={{0,16},{8,24},{16,0},{24,8},{1,17},{9,25},{17,1},{25,9},{2,18},{10... | collective-permute-start | bytes 98312 | tf_op jit(solution)/shard_map/ppermute | solution.py:27
  8.3 8.7 %collective-permute-start.3 = (bf16[32,512]{1,0:T(8,128)(2,1)}, bf16[32,512]{1,0:T(8,128)(2,1)S(1)}, u32[]{:S(2)}, u32[]{:S(2)}) collective-permute-start(bf16[32,512]{1,0:T(8,128)(2,1)} %get-tuple-element.57), channel_id=1, source_target_pairs={{0,24},{8,16},{16,8},{24,0},{1,25},{9,17},{17,9},{25,1},{2,26},{10... | collective-permute-start | bytes 98312 | tf_op jit(solution)/shard_map/ppermute | solution.py:27
  17.9 9.7 %collective-permute-start.4 = (bf16[128,1280]{1,0:T(8,128)(2,1)S(1)}, bf16[128,1280]{1,0:T(8,128)(2,1)S(1)}, u32[]{:S(2)}, u32[]{:S(2)}) collective-permute-start(bf16[128,1280]{1,0:T(8,128)(2,1)S(1)} %shard_map.111), channel_id=1, source_target_pairs={{0,16},{8,24},{16,0},{24,8},{1,17},{9,25},{17,1},{25,9},{2,18},{10... | collective-permute-start | bytes 983048 | tf_op jit(solution)/shard_map/ppermute | solution.py:27
  19.5 8.1 %collective-permute-start.6 = (bf16[128,1280]{1,0:T(8,128)(2,1)S(1)}, bf16[128,1280]{1,0:T(8,128)(2,1)S(1)}, u32[]{:S(2)}, u32[]{:S(2)}) collective-permute-start(bf16[128,1280]{1,0:T(8,128)(2,1)S(1)} %shard_map.112), channel_id=1, source_target_pairs={{0,8},{8,0},{16,24},{24,16},{1,9},{9,1},{17,25},{25,17},{2,10},{10... | collective-permute-start | bytes 983048 | tf_op jit(solution)/shard_map/ppermute | solution.py:27
  20.1 7.5 %collective-permute-start.7 = (bf16[128,512]{1,0:T(8,128)(2,1)S(1)}, bf16[128,512]{1,0:T(8,128)(2,1)S(1)}, u32[]{:S(2)}, u32[]{:S(2)}) collective-permute-start(bf16[128,512]{1,0:T(8,128)(2,1)S(1)} %shard_map.110.refs_2_.refs_0_), channel_id=1, source_target_pairs={{0,4},{1,5},{2,6},{3,7},{4,0},{5,1},{6,2},{7,3},{8,12},{9,13},{10,... | collective-permute-start | bytes 393224 | tf_op jit(solution)/shard_map/ppermute | solution.py:27
  29.1 7.3 %collective-permute-start.12 = (bf16[256,512]{1,0:T(8,128)(2,1)S(1)}, bf16[256,512]{1,0:T(8,128)(2,1)S(1)}, u32[]{:S(2)}, u32[]{:S(2)}) collective-permute-start(bf16[256,512]{1,0:T(8,128)(2,1)S(1)} %shard_map.117.refs_0_), channel_id=1, source_target_pairs={{0,2},{1,3},{2,0},{3,1},{4,6},{5,7},{6,4},{7,5},{8,10},{9,11},{10,... | collective-permute-start | bytes 786440 | tf_op jit(solution)/shard_map/ppermute | solution.py:27
  36.5 8.8 %collective-permute-start.11 = (bf16[512,256]{1,0:T(8,128)(2,1)S(1)}, bf16[512,256]{1,0:T(8,128)(2,1)S(1)}, u32[]{:S(2)}, u32[]{:S(2)}) collective-permute-start(bf16[512,256]{1,0:T(8,128)(2,1)S(1)} %shard_map.116), channel_id=1, source_target_pairs={{0,8},{8,0},{16,24},{24,16},{1,9},{9,1},{17,25},{25,17},{2,10},{10... | collective-permute-start | bytes 786440 | tf_op jit(solution)/shard_map/ppermute | solution.py:27
  37.6 8.5 %collective-permute-start.9 = (bf16[512,256]{1,0:T(8,128)(2,1)S(1)}, bf16[512,256]{1,0:T(8,128)(2,1)S(1)}, u32[]{:S(2)}, u32[]{:S(2)}) collective-permute-start(bf16[512,256]{1,0:T(8,128)(2,1)S(1)} %shard_map.115), channel_id=1, source_target_pairs={{0,16},{8,24},{16,0},{24,8},{1,17},{9,25},{17,1},{25,9},{2,18},{10... | collective-permute-start | bytes 786440 | tf_op jit(solution)/shard_map/ppermute | solution.py:27
  56.0 8.7 %collective-permute-start.21 = (bf16[512,256]{1,0:T(8,128)(2,1)S(1)}, bf16[512,256]{1,0:T(8,128)(2,1)S(1)}, u32[]{:S(2)}, u32[]{:S(2)}) collective-permute-start(bf16[512,256]{1,0:T(8,128)(2,1)S(1)} %get-tuple-element.84), channel_id=1, source_target_pairs={{0,8},{8,0},{16,24},{24,16},{1,9},{9,1},{17,25},{25,17},{2,10},{10... | collective-permute-start | bytes 786440 | tf_op jit(solution)/shard_map/ppermute | solution.py:27
  57.1 8.9 %collective-permute-start.23 = (bf16[512,256]{1,0:T(8,128)(2,1)S(1)}, bf16[512,256]{1,0:T(8,128)(2,1)S(1)}, u32[]{:S(2)}, u32[]{:S(2)}) collective-permute-start(bf16[512,256]{1,0:T(8,128)(2,1)S(1)} %get-tuple-element.88), channel_id=1, source_target_pairs={{0,16},{8,24},{16,0},{24,8},{1,17},{9,25},{17,1},{25,9},{2,18},{10... | collective-permute-start | bytes 786440 | tf_op jit(solution)/shard_map/ppermute | solution.py:27
  58.1 10.1 %collective-permute-start.17 = (bf16[288,512]{1,0:T(8,128)(2,1)S(1)}, bf16[288,512]{1,0:T(8,128)(2,1)S(1)}, u32[]{:S(2)}, u32[]{:S(2)}) collective-permute-start(bf16[288,512]{1,0:T(8,128)(2,1)S(1)} %get-tuple-element.75), channel_id=1, source_target_pairs={{0,2},{1,3},{2,0},{3,1},{4,6},{5,7},{6,4},{7,5},{8,10},{9,11},{10,... | collective-permute-start | bytes 884744 | tf_op jit(solution)/shard_map/ppermute | solution.py:27
  64.8 6.6 %collective-permute-start.22 = (bf16[256,256]{1,0:T(8,128)(2,1)S(1)}, bf16[256,256]{1,0:T(8,128)(2,1)S(1)}, u32[]{:S(2)}, u32[]{:S(2)}) collective-permute-start(bf16[256,256]{1,0:T(8,128)(2,1)S(1)} %get-tuple-element.86), channel_id=1, source_target_pairs={{0,16},{8,24},{16,0},{24,8},{1,17},{9,25},{17,1},{25,9},{2,18},{10... | collective-permute-start | bytes 393224 | tf_op jit(solution)/shard_map/ppermute | solution.py:27
  66.0 6.5 %collective-permute-start.24 = (bf16[256,256]{1,0:T(8,128)(2,1)S(1)}, bf16[256,256]{1,0:T(8,128)(2,1)S(1)}, u32[]{:S(2)}, u32[]{:S(2)}) collective-permute-start(bf16[256,256]{1,0:T(8,128)(2,1)S(1)} %get-tuple-element.90), channel_id=1, source_target_pairs={{0,8},{8,0},{16,24},{24,16},{1,9},{9,1},{17,25},{25,17},{2,10},{10... | collective-permute-start | bytes 393224 | tf_op jit(solution)/shard_map/ppermute | solution.py:27
  67.0 10.7 %collective-permute-start.14 = (bf16[256,512]{1,0:T(8,128)(2,1)S(1)}, bf16[256,512]{1,0:T(8,128)(2,1)S(1)}, u32[]{:S(2)}, u32[]{:S(2)}) collective-permute-start(bf16[256,512]{1,0:T(8,128)(2,1)S(1)} %shard_map.121), channel_id=1, source_target_pairs={{0,8},{8,0},{16,24},{24,16},{1,9},{9,1},{17,25},{25,17},{2,10},{10... | collective-permute-start | bytes 786440 | tf_op jit(solution)/shard_map/ppermute | solution.py:27
  68.3 10.6 %collective-permute-start.18 = (bf16[160,512]{1,0:T(8,128)(2,1)S(1)}, bf16[160,512]{1,0:T(8,128)(2,1)S(1)}, u32[]{:S(2)}, u32[]{:S(2)}) collective-permute-start(bf16[160,512]{1,0:T(8,128)(2,1)S(1)} %get-tuple-element.77.refs_5_), channel_id=1, source_target_pairs={{0,4},{1,5},{2,6},{3,7},{4,0},{5,1},{6,2},{7,3},{8,12},{9,13},{10,... | collective-permute-start | bytes 491528 | tf_op jit(solution)/shard_map/ppermute | solution.py:27
  76.1 7.8 %collective-permute-start.27 = (bf16[128,768]{1,0:T(8,128)(2,1)S(1)}, bf16[128,768]{1,0:T(8,128)(2,1)S(1)}, u32[]{:S(2)}, u32[]{:S(2)}) collective-permute-start(bf16[128,768]{1,0:T(8,128)(2,1)S(1)} %get-tuple-element.94), channel_id=1, source_target_pairs={{0,16},{8,24},{16,0},{24,8},{1,17},{9,25},{17,1},{25,9},{2,18},{10... | collective-permute-start | bytes 589832 | tf_op jit(solution)/shard_map/ppermute | solution.py:27
  77.7 11.3 %collective-permute-start.15 = (bf16[256,512]{1,0:T(8,128)(2,1)S(1)}, bf16[256,512]{1,0:T(8,128)(2,1)S(1)}, u32[]{:S(2)}, u32[]{:S(2)}) collective-permute-start(bf16[256,512]{1,0:T(8,128)(2,1)S(1)} %shard_map.122), channel_id=1, source_target_pairs={{0,16},{8,24},{16,0},{24,8},{1,17},{9,25},{17,1},{25,9},{2,18},{10... | collective-permute-start | bytes 786440 | tf_op jit(solution)/shard_map/ppermute | solution.py:27
  78.9 6.5 %collective-permute-start.19 = (bf16[128,512]{1,0:T(8,128)(2,1)S(1)}, bf16[128,512]{1,0:T(8,128)(2,1)S(1)}, u32[]{:S(2)}, u32[]{:S(2)}) collective-permute-start(bf16[128,512]{1,0:T(8,128)(2,1)S(1)} %shard_map.128), channel_id=1, source_target_pairs={{0,8},{8,0},{16,24},{24,16},{1,9},{9,1},{17,25},{25,17},{2,10},{10... | collective-permute-start | bytes 393224 | tf_op jit(solution)/shard_map/ppermute | solution.py:27
  80.9 10.2 %collective-permute-start.26 = (bf16[128,768]{1,0:T(8,128)(2,1)S(1)}, bf16[128,768]{1,0:T(8,128)(2,1)S(1)}, u32[]{:S(2)}, u32[]{:S(2)}) collective-permute-start(bf16[128,768]{1,0:T(8,128)(2,1)S(1)} %shard_map.133), channel_id=1, source_target_pairs={{0,16},{8,24},{16,0},{24,8},{1,17},{9,25},{17,1},{25,9},{2,18},{10... | collective-permute-start | bytes 589832 | tf_op jit(solution)/shard_map/ppermute | solution.py:27
  83.9 7.2 %collective-permute-start.28 = (bf16[128,768]{1,0:T(8,128)(2,1)S(1)}, bf16[128,768]{1,0:T(8,128)(2,1)S(1)}, u32[]{:S(2)}, u32[]{:S(2)}) collective-permute-start(bf16[128,768]{1,0:T(8,128)(2,1)S(1)} %shard_map.134), channel_id=1, source_target_pairs={{0,8},{8,0},{16,24},{24,16},{1,9},{9,1},{17,25},{25,17},{2,10},{10... | collective-permute-start | bytes 589832 | tf_op jit(solution)/shard_map/ppermute | solution.py:27
  85.5 7.0 %collective-permute-start.20 = (bf16[128,512]{1,0:T(8,128)(2,1)S(1)}, bf16[128,512]{1,0:T(8,128)(2,1)S(1)}, u32[]{:S(2)}, u32[]{:S(2)}) collective-permute-start(bf16[128,512]{1,0:T(8,128)(2,1)S(1)} %shard_map.129), channel_id=1, source_target_pairs={{0,16},{8,24},{16,0},{24,8},{1,17},{9,25},{17,1},{25,9},{2,18},{10... | collective-permute-start | bytes 393224 | tf_op jit(solution)/shard_map/ppermute | solution.py:27
  (10 other events, 53.8 us)

commit v3 on v2

--- a/solution.py
+++ b/solution.py
@@ -42,7 +42,7 @@
     return order
 
 
-def call(body, outs, *operands, scratch=(), flops=0, near=True, stored=False, after=(), limit=40):
+def call(body, outs, *operands, scratch=(), flops=0, near=True, stored=False, after=(), limit=40, pinned=False):
     vmem = pl.BlockSpec(memory_space=pltpu.VMEM)
     hbm = pl.BlockSpec(memory_space=pltpu.HBM)
     count = len(operands)
@@ -50,7 +50,7 @@
     moved += sum(math.prod(s) * jnp.dtype(t).itemsize for s, t in outs)
     return pl.pallas_call(
         lambda *refs: body(*refs[:count], *refs[count + len(after) :]),
-        out_shape=[jax.ShapeDtypeStruct(s, t) for s, t in outs],
+        out_shape=[(pltpu.VMEM if pinned else jax.ShapeDtypeStruct)(s, t) for s, t in outs],
         in_specs=[vmem if near else hbm] * count + [pl.BlockSpec(memory_space=pl.ANY)] * len(after),
         out_specs=[hbm if stored else vmem] * len(outs),
         scratch_shapes=list(scratch),
@@ -106,29 +106,40 @@
 
 
 def pack_rows(groups, *refs):
-    sources = refs[:5]
-    outs = refs[5 : -groups - 6]
-    weight_outs = refs[-groups - 6 : -6]
-    held = refs[-6:-1]
+    sources = refs[:4]
+    outs = refs[4 : 4 + groups]
+    weight_outs = refs[4 + groups : -5]
+    held = refs[-5:-1]
     arrived = refs[-1]
-    copies = [pltpu.make_async_copy(sources[i], held[i], arrived.at[i]) for i in range(5)]
+    copies = [pltpu.make_async_copy(sources[i], held[i], arrived.at[i]) for i in range(4)]
     for copy in copies:
         copy.start()
     for copy in copies:
         copy.wait()
     me = lax.axis_index("fsdp")
+    local, inner = held[0].shape
+    rows, model = held[3].shape
+    width, channels = inner // groups, model // groups
     for k in range(groups):
-        at = 0
-        for source in held[:4]:
-            width = source.shape[1] // groups
-            there = slice(at, at + width)
-            cells = source[:, block(me ^ k, width, LANES)]
-            if groups == 4:
-                split_up(outs, k, cells.shape[0], there, cells)
-            else:
-                outs[k][:, there] = cells
-            at += width
-        weight_outs[k][...] = held[4][:, block(me ^ k, held[4].shape[1] // groups, LANES)]
+        columns = block(me ^ k, width, LANES)
+        for at in range(3):
+            outs[k][:local, at * width : (at + 1) * width] = held[at][:, columns]
+        cells = held[3][:, block(me ^ k, channels, LANES)]
+        if weight_outs:
+            weight_outs[k][...] = cells
+        else:
+            half = rows // 2
+            outs[k][local : local + half, :channels] = cells[:half, :]
+            outs[k][local : local + half, channels:] = cells[half:, :width]
+            outs[k][local + half : local + rows, :width] = cells[half:, width:]
+
+
+def pack_columns(groups, *refs):
+    source = refs[0]
+    me = lax.axis_index("fsdp")
+    width = source.shape[1] // groups
+    for k in range(groups):
+        refs[1 + k][...] = source[:, block(me ^ k, width, LANES)]
 
 
 def stack_parts(mine, other, out):
@@ -145,29 +156,25 @@
 
 
 def attend(groups, *refs):
-    folded = groups == 4
-    pieces = refs[: 5 if folded else groups]
-    rows_ref = refs[len(pieces)]
-    upstream_ref = refs[len(pieces) + 1]
-    outs = refs[len(pieces) + 2 :]
-    edge = rows_ref.shape[1]
+    pieces = refs[:groups]
+    rows_ref = refs[groups]
+    outs = refs[groups + 1 : 3 + groups if groups == 4 else 2 + groups]
+    weight_refs = refs[groups + 1 + len(outs) :]
     me = lax.axis_index("fsdp")
-    local = pieces[0].shape[0]
+    local = rows_ref.shape[0] // groups
     half, width = outs[0].shape
-    if folded:
-        share = local // 2
-        own, beside, later_across, across, later_beside = pieces
-        ends = ((own, beside, later_across), (own, across, later_beside))
-        for k, i, source, at in places(*ends, share):
-            if k == 0:
-                at = i * share
-            start = pl.multiple_of((me ^ k) * local + i * share, share)
-            rows_ref[pl.ds(start, share), :] = source[at : at + share, :edge]
-            upstream_ref[pl.ds(start, share), :] = source[at : at + share, edge:]
-    else:
+    for k in range(groups):
+        rows_ref[block(me ^ k, local, local), :] = pieces[k][:local, :]
+    if weight_refs:
+        rows = pieces[0].shape[0] - local
+        share = rows // 2
+        channels = weight_refs[0].shape[1]
         for k in range(groups):
-            rows_ref[block(me ^ k, local, local), :] = pieces[k][:, :edge]
-            upstream_ref[block(me ^ k, local, local), :] = pieces[k][:, edge:]
+            at = k * rows
+            top, end = pieces[k][local : local + share, :], pieces[k][local + share :, :]
+            weight_refs[0][at : at + share, :] = top[:, :channels]
+            weight_refs[0][at + share : at + rows, :width] = top[:, channels:]
+            weight_refs[0][at + share : at + rows, width:] = end[:, :width]
     for head in range(width // HDIM):
         at = head * HDIM
         queries = rows_ref[:, at : at + HDIM]
@@ -202,9 +209,10 @@
 
 
 def convolve(groups, *refs):
-    pieces = refs[: -groups - 8]
-    weight, taps_ref, attention, projected_ref, slope_ref = refs[-groups - 8 : -groups - 3]
-    ahead = refs[-groups - 3 : -3]
+    count = 6 if groups == 4 else groups
+    pieces = refs[:count]
+    weight, taps_ref, attention, projected_ref, slope_ref = refs[count : count + 5]
+    ahead = refs[count + 5 : -3]
     padded, taps, result = refs[-3:]
     me = lax.axis_index("fsdp")
     frames = attention.shape[0]
@@ -237,14 +245,19 @@
             result[start : start + TILE, :] = own + conv * gate
             slope_ref[start : start + TILE, columns] = gate * (1.0 + conv * (1.0 - gate))
         for k in range(groups):
-            ahead[k][:, columns] = result[block(me ^ k, local, local), :].astype(BF16)
+            cells = result[block(me ^ k, local, local), :].astype(BF16)
+            if groups == 4:
+                split_up(ahead, k, local, columns, cells)
+            else:
+                ahead[k][:, columns] = cells
         return carry
 
     lax.fori_loop(0, channels // LANES, lane_block, 0)
 
 
 def convolve_back(groups, *refs):
-    upstream, projected_ref, slope_ref, weight, taps_ref, grad_ref, tap_ref = refs[:7]
+    upstream = refs[:groups]
+    projected_ref, slope_ref, weight, taps_ref, grad_ref, tap_ref = refs[groups : groups + 6]
     outs = refs[-groups - 4 : -4]
     padded, taps, above, sums = refs[-4:]
     me = lax.axis_index("fsdp")
@@ -256,7 +269,8 @@
 
     def lane_block(c, carry):
         columns = block(c, LANES, LANES)
-        above[...] = upstream[:, columns].astype(F32)
+        for k in range(groups):
+            above[block(me ^ k, local, local), :] = upstream[k][:, columns].astype(F32)
         taps[0:KERNEL, :] = taps_ref[:, block(me * (channels // LANES) + c, LANES, LANES)].astype(F32)
         padded[16 : frames + 16, :] = (above[...] * slope_ref[:, columns]).astype(BF16).astype(F32)
         sums[...] = jnp.zeros(sums.shape, F32)
@@ -369,10 +383,9 @@
 
 
 def join_all(groups, scale, *refs):
-    folded = groups == 4
-    count = 5 if folded else groups
-    ahead = refs[: (len(refs) - count - 9) // 2]
-    sums = refs[len(ahead) : -count - 9]
+    count = 5 if groups == 4 else groups
+    ahead = refs[:count]
+    sums = refs[count : -count - 9]
     pieces = refs[-count - 9 : -9]
     outs = refs[-9:-3]
     weight_ref, tap_ref, sent = refs[-3:]
@@ -386,28 +399,31 @@
 
     local, width = pieces[0].shape
     width //= 3
-    if folded:
+    channels = sums[0].shape[1]
+
+    def found(arrays):
+        if groups != 4:
+            return [(k, 0, local, arrays[k], 0) for k in range(groups)]
         share = local // 2
-        own, beside, later_across, across, later_beside = pieces
-        ends = ((own, beside, later_across), (own, across, later_beside))
-        found = [(k, i * share, share, x, at) for k, i, x, at in places(*ends, share) if k]
-        found.append((0, 0, local, own, 0))
-    else:
-        found = [(k, 0, local, pieces[k], 0) for k in range(groups)]
-    for k, start, size, source, first in found:
+        ends = ((arrays[0], arrays[1], arrays[2]), (arrays[0], arrays[3], arrays[4]))
+        parts = [(k, i * share, share, x, at) for k, i, x, at in places(*ends, share) if k]
+        return parts + [(0, 0, local, arrays[0], 0)]
+
+    for k, start, size, source, first in found(ahead):
+        there = outs[0].at[0, start : start + size, block(me ^ k, channels, LANES)]
+        store(source.at[first : first + size], there)
+    for k, start, size, source, first in found(pieces):
         columns = block(me ^ k, width, LANES)
         for at in range(3):
             part = source.at[first : first + size, at * width : (at + 1) * width]
             store(part, outs[1 + at].at[0, start : start + size, columns])
-    rows, channels = sums[0].shape
     for k in range(groups):
         columns = block(me ^ k, channels, LANES)
-        i = min(k, len(ahead) - 1)
-        at = local if k > i else 0
-        store(ahead[i].at[at : at + local], outs[0].at[0, :, columns])
-        at = rows if k > i else 0
-        tap_ref[:, columns] = sums[i][at : at + KERNEL, :].astype(F32) * scale
-        weight_ref[:, columns] = sums[i][at + TAPS : at + rows, :].astype(F32) * scale
+        i = min(k, len(sums) - 1)
+        first = sums[0].shape[0] if k > i else 0
+        last = first + sums[0].shape[0]
+        tap_ref[:, columns] = sums[i][first : first + KERNEL, :].astype(F32) * scale
+        weight_ref[:, columns] = sums[i][first + TAPS : last, :].astype(F32) * scale
     store(weight_ref, outs[4])
     store(tap_ref, outs[5])
     for copy in copies:
@@ -433,9 +449,9 @@
 def turn(sent):
     if len(sent) != 4:
         return exchange(sent)
-    rows = sent[0].shape[0]
+    shape = [((2 * sent[0].shape[0], sent[0].shape[1]), BF16)]
     first = swap(stack(sent[1], sent[3]), "fsdp", 1)
-    second = swap(call(stack_parts, [((2 * rows, sent[0].shape[1]), BF16)], sent[2], first)[0], "fsdp", 2)
+    second = swap(call(stack_parts, shape, sent[2], first)[0], "fsdp", 2)
     return [sent[0], first, second]
 
 
@@ -459,7 +475,7 @@
     return ordered.transpose(1, 0, 2, 3).reshape(groups * count * rows, channels)
 
 
-def weight_halves(attention, grads, tap_terms, groups, count, rows):
+def weight_halves(attention, grads, tap_terms, groups, count, rows, after):
     channels = grads.shape[1]
     depth = attention.shape[1] // groups
     share = count // 2 * groups * rows
@@ -473,6 +489,7 @@
             grads,
             tap_terms,
             scratch=[pltpu.VMEM((depth, channels), F32)],
+            after=after,
         )
     else:
         (terms,) = call(plain_terms, [((groups * depth, channels), BF16)], attention, grads)
@@ -511,47 +528,57 @@
         shape, small = ((local, size), BF16), ((local // 2, size), BF16)
         return [shape, shape, shape, small, small] if folded else [shape] * groups
 
+    merged = folded and rows % 32 == 0 and channels == 2 * width
+    whole = (groups * rows, channels)
     sent = call(
         functools.partial(pack_rows, groups),
-        split(3 * width + channels) + [((rows, channels), BF16)] * groups,
+        [((local + (rows if merged else 0), 3 * width), BF16)] * groups
+        + ([] if merged else [((rows, channels), BF16)] * groups),
         queries[0],
         key_rows[0],
         value_rows[0],
-        grad_out[0],
         out_weight,
         near=False,
         limit=PACK_LIMIT,
+        pinned=True,
         scratch=[pltpu.VMEM((local, inner), BF16)] * 3
-        + [pltpu.VMEM((local, model), BF16), pltpu.VMEM((rows, model), BF16)]
-        + [pltpu.SemaphoreType.DMA((5,))],
-    )
-    gathered = stack(*exchange(sent[-groups:]))
-    pieces = exchange_split(sent[:-groups], after=[gathered])
+        + [pltpu.VMEM((rows, model), BF16), pltpu.SemaphoreType.DMA((4,))],
+    )
+    half = ((frames // 2, width), BF16)
+    held, *own = call(
+        functools.partial(attend, groups),
+        [((frames, 3 * width), BF16)]
+        + ([half, half] if folded else [((frames, width), BF16)])
+        + ([(whole, BF16)] if merged else []),
+        *exchange(sent[:groups]),
+        flops=ATTEND_COST * frames * frames * width,
+    )
+    gathered = own.pop() if merged else stack(*exchange(sent[groups:]))
     first, *masks = reversed(masks_of(count)[1:])
-    gathered = stack(gathered, swap(gathered, "frame", first))
-    held, upstream, *own = call(
-        functools.partial(attend, groups),
-        [((frames, 3 * width), BF16), ((frames, channels), BF16)]
-        + ([((frames // 2, width), BF16)] * 2 if folded else [((frames, width), BF16)]),
-        *pieces,
-        flops=ATTEND_COST * frames * frames * width,
-        after=[gathered],
-    )
-    gathered = stack(gathered, after=own[:1])
     if folded:
         top, end = own
         beside, across = swap(top, "fsdp", 1), swap(end, "fsdp", 2)
+        step = [beside, across]
         attention = [top, beside, swap(stack(top, beside), "fsdp", 2)]
         attention += [end, across, swap(stack(end, across), "fsdp", 1)]
-        weight = gather_weight(gathered, masks, groups, count, [beside, across])
+        last = [attention[2], attention[5]]
     else:
         attention = exchange(own * groups)
-        weight = gather_weight(gathered, masks, groups, count, attention[1:2])
+        step = last = attention[1:2]
+    gathered = stack(gathered, swap(gathered, "frame", first), after=step)
+    sent = call(
+        functools.partial(pack_columns, groups),
+        [((local, channels), BF16)] * groups,
+        grad_out[0],
+        after=step,
+    )
+    upstream = exchange(sent)
+    weight = gather_weight(gathered, masks, groups, count, last + upstream[1:3])
 
     outs = call(
         functools.partial(convolve, groups),
         [((frames, inner), BF16), ((frames, channels), BF16), ((frames, channels), F32)]
-        + [((local, channels), BF16)] * groups,
+        + split(channels),
         *attention,
         weight,
         conv_weight,
@@ -563,12 +590,12 @@
         flops=conv_flops,
     )
     whole, projected, slope = outs[:3]
-    ahead = turn(outs[3:])
+    ahead = exchange_split(outs[3:])
 
     outs = call(
         functools.partial(convolve_back, groups),
         [((frames, channels), BF16), ((TAPS, channels), F32)] + [((frames, width), BF16)] * groups,
-        upstream,
+        *upstream,
         projected,
         slope,
         weight,
@@ -590,7 +617,7 @@
         above = [stay_top, swap(go_top, "fsdp", 2), stay_end, swap(go_end, "fsdp", 1)]
     else:
         above = exchange(outs[2:])
-    halves = weight_halves(whole, grads, tap_terms, groups, count, rows)
+    halves = weight_halves(whole, grads, tap_terms, groups, count, rows, ahead[1:4:2])
     masks = masks_of(count)
     for mask in masks[:-1]:
         halves = add_up(halves, mask, 2)
@@ -601,7 +628,7 @@
         *above,
         scratch=[pltpu.VMEM((frames, width), BF16), pltpu.VMEM((frames, 3 * width), BF16)],
         flops=BACK_COST * frames * frames * width,
-        after=[halves[1]],
+        after=[halves[1], *(ahead[2:5:2] if folded else ())],
     )
     pieces = exchange_split(sent)
     sums = turn(add_up(halves, masks[-1], groups))
@@ -618,7 +645,7 @@
             scratch=[
                 pltpu.VMEM((rows, model), F32),
                 pltpu.VMEM((KERNEL, model), F32),
-                pltpu.SemaphoreType.DMA((8 * groups,)),
+                pltpu.SemaphoreType.DMA((8 * groups + 2,)),
             ],
         )
     )

time: 94.2 us -> 84.3 us (0.89)
  waiting for transfers between devices: 38.2 us -> 31.2 us
  Pallas kernels: 18.6 us -> 17.3 us
    ppermute x29 -> x30, waiting for transfers between devices: 38.2 us -> 31.2 us  [swap(): return lax.ppermute(cells, axis, [(i, i ^ mask) for i in range(count)])]
    pallas_call x27 -> x24, Pallas kernels: 18.6 us -> 17.3 us  [call(): pl.pallas_call(lambda *refs: body(*refs[:count], *refs[count + len(after)...]
    ppermute x29 -> x30, starting transfers between devices: 35.5 us -> 34.8 us  [swap(): return lax.ppermute(cells, axis, [(i, i ^ mask) for i in range(count)])]
  transfers between devices with their start and end apart: 29 -> 30, of which waited for: 16 -> 15; matrix products, arithmetic and copies ran while one was open for 0% -> 0% of each run, Pallas kernels for 3% -> 15%
where the time goes in v3:
time: 84.3 us; the launch traced here: 84.1 us
  starting transfers between devices  34.8 us (41%)
  waiting for transfers between devices  31.2 us (37%)
  Pallas kernels  17.3 us (21%)
    ppermute x30, starting transfers between devices, swap(): return lax.ppermute(cells, axis, [(i, i ^ mask) for i in range(count)])  34.8 us
    ppermute x30, waiting for transfers between devices, swap(): return lax.ppermute(cells, axis, [(i, i ^ mask) for i in range(count)])  31.2 us
    pallas_call x24, Pallas kernels, call(): pl.pallas_call(lambda *refs: body(*refs[:count], *refs[count + len(after)...  17.3 us
  transfers between devices with their start and end apart: 30, of which 15 were waited for; matrix products, arithmetic and copies ran while one was open for 0% of the time, Pallas kernels for 15%

profile of v3, /device:TPU:0, one launch (start us, length us, event | category | flops | bytes accessed | tf_op | source)
XLA Modules:
  0.0 84.1 jit_solution(13306592307706903275)
XLA Ops:
  1.9 3.0 %collective-permute-start = (bf16[160,768]{1,0:T(8,128)(2,1)S(1)}, bf16[160,768]{1,0:T(8,128)(2,1)S(1)}, u32[]{:S(2)}, u32[]{:S(2)}) collective-permute-start(bf16[160,768]{1,0:T(8,128)(2,1)S(1)} %get-tuple-element.52), channel_id=1, source_target_pairs={{0,8},{8,0},{16,24},{24,16},{1,9},{9,1},{17,25},{25,17},{2,10},{10... | collective-permute-start | bytes 737288 | tf_op jit(solution)/shard_map/ppermute | solution.py:27
  4.9 1.5 %collective-permute-start.1 = (bf16[160,768]{1,0:T(8,128)(2,1)S(1)}, bf16[160,768]{1,0:T(8,128)(2,1)S(1)}, u32[]{:S(2)}, u32[]{:S(2)}) collective-permute-start(bf16[160,768]{1,0:T(8,128)(2,1)S(1)} %get-tuple-element.53), channel_id=1, source_target_pairs={{0,16},{8,24},{16,0},{24,8},{1,17},{9,25},{17,1},{25,9},{2,18},{10... | collective-permute-start | bytes 737288 | tf_op jit(solution)/shard_map/ppermute | solution.py:27
  6.5 5.2 %collective-permute-done.refs_1_ = bf16[160,768]{1,0:T(8,128)(2,1)S(1)} collective-permute-done((bf16[160,768]{1,0:T(8,128)(2,1)S(1)}, bf16[160,768]{1,0:T(8,128)(2,1)S(1)}, u32[]{:S(2)}, u32[]{:S(2)}) %collective-permute-start) | collective-permute-done | bytes 245792 | tf_op jit(solution)/shard_map/ppermute | solution.py:27
  11.7 5.9 %collective-permute-done.1.refs_2_ = bf16[160,768]{1,0:T(8,128)(2,1)S(1)} collective-permute-done((bf16[160,768]{1,0:T(8,128)(2,1)S(1)}, bf16[160,768]{1,0:T(8,128)(2,1)S(1)}, u32[]{:S(2)}, u32[]{:S(2)}) %collective-permute-start.1) | collective-permute-done | bytes 245792 | tf_op jit(solution)/shard_map/ppermute | solution.py:27
  21.1 2.6 %collective-permute-start.7 = (bf16[128,512]{1,0:T(8,128)(2,1)S(1)}, bf16[128,512]{1,0:T(8,128)(2,1)S(1)}, u32[]{:S(2)}, u32[]{:S(2)}) collective-permute-start(bf16[128,512]{1,0:T(8,128)(2,1)S(1)} %get-tuple-element.57.refs_0_), channel_id=1, source_target_pairs={{0,4},{1,5},{2,6},{3,7},{4,0},{5,1},{6,2},{7,3},{8,12},{9,13},{10,... | collective-permute-start | bytes 393224 | tf_op jit(solution)/shard_map/ppermute | solution.py:27
  24.1 1.6 %collective-permute-start.4 = (bf16[512,256]{1,0:T(8,128)(2,1)S(1)}, bf16[512,256]{1,0:T(8,128)(2,1)S(1)}, u32[]{:S(2)}, u32[]{:S(2)}) collective-permute-start(bf16[512,256]{1,0:T(8,128)(2,1)S(1)} %shard_map.111), channel_id=1, source_target_pairs={{0,16},{8,24},{16,0},{24,8},{1,17},{9,25},{17,1},{25,9},{2,18},{10... | collective-permute-start | bytes 786440 | tf_op jit(solution)/shard_map/ppermute | solution.py:27
  26.5 2.0 %collective-permute-done.7.refs_1_ = bf16[128,512]{1,0:T(8,128)(2,1)S(1)} collective-permute-done((bf16[128,512]{1,0:T(8,128)(2,1)S(1)}, bf16[128,512]{1,0:T(8,128)(2,1)S(1)}, u32[]{:S(2)}, u32[]{:S(2)}) %collective-permute-start.7) | collective-permute-done | bytes 131104 | tf_op jit(solution)/shard_map/ppermute | solution.py:27
  29.2 1.6 %collective-permute-start.9 = (bf16[128,512]{1,0:T(8,128)(2,1)S(1)}, bf16[128,512]{1,0:T(8,128)(2,1)S(1)}, u32[]{:S(2)}, u32[]{:S(2)}) collective-permute-start(bf16[128,512]{1,0:T(8,128)(2,1)S(1)} %get-tuple-element.58), channel_id=1, source_target_pairs={{0,8},{8,0},{16,24},{24,16},{1,9},{9,1},{17,25},{25,17},{2,10},{10... | collective-permute-start | bytes 393224 | tf_op jit(solution)/shard_map/ppermute | solution.py:27
  31.3 3.2 %collective-permute-done.9.refs_4_.refs_1_ = bf16[128,512]{1,0:T(8,128)(2,1)S(1)} collective-permute-done((bf16[128,512]{1,0:T(8,128)(2,1)S(1)}, bf16[128,512]{1,0:T(8,128)(2,1)S(1)}, u32[]{:S(2)}, u32[]{:S(2)}) %collective-permute-start.9) | collective-permute-done | bytes 131104 | tf_op jit(solution)/shard_map/ppermute | solution.py:27
  35.9 1.5 %collective-permute-start.16 = (bf16[128,512]{1,0:T(8,128)(2,1)S(1)}, bf16[128,512]{1,0:T(8,128)(2,1)S(1)}, u32[]{:S(2)}, u32[]{:S(2)}) collective-permute-start(bf16[128,512]{1,0:T(8,128)(2,1)S(1)} %get-tuple-element.67), channel_id=1, source_target_pairs={{0,24},{8,16},{16,8},{24,0},{1,25},{9,17},{17,9},{25,1},{2,26},{10... | collective-permute-start | bytes 393224 | tf_op jit(solution)/shard_map/ppermute | solution.py:27
  37.9 3.4 %shard_map.117 = (bf16[512,1024]{1,0:T(8,128)(2,1)S(1)}, bf16[512,512]{1,0:T(8,128)(2,1)S(1)}, f32[512,512]{1,0:T(8,128)S(1)}, bf16[128,512]{1,0:T(8,128)(2,1)S(...) custom-call(bf16[256,256]{1,0:T(8,128)(2,1)S(1)} %get-tuple-element., ...), custom_call_target="tpu_custom_call" | custom-call | flops 4875878400 | bytes 5369856 | tf_op jit(solution)/shard_map/pallas_call | solution.py:51
  43.4 5.7 %shard_map.120 = (bf16[512,512]{1,0:T(8,128)(2,1)S(1)}, f32[32,512]{1,0:T(8,128)S(1)}, bf16[512,256]{1,0:T(8,128)(2,1)S(1)}, bf16[512,256]{1,0:T(8,128)(2,1)S(1)...) custom-call(bf16[128,512]{1,0:T(8,128)(2,1)S(1)} %get-tuple-element.66.refs_0_, ...), custom_call_target="tpu_custom_call" | custom-call | flops 7313817600 | bytes 4911104 | tf_op jit(solution)/shard_map/pallas_call | solution.py:51
  50.6 1.5 %collective-permute-start.24 = (bf16[512,256]{1,0:T(8,128)(2,1)S(1)}, bf16[512,256]{1,0:T(8,128)(2,1)S(1)}, u32[]{:S(2)}, u32[]{:S(2)}) collective-permute-start(bf16[512,256]{1,0:T(8,128)(2,1)S(1)} %get-tuple-element.88), channel_id=1, source_target_pairs={{0,16},{8,24},{16,0},{24,8},{1,17},{9,25},{17,1},{25,9},{2,18},{10... | collective-permute-start | bytes 786440 | tf_op jit(solution)/shard_map/ppermute | solution.py:27
  52.2 1.5 %collective-permute-start.18 = (bf16[288,512]{1,0:T(8,128)(2,1)S(1)}, bf16[288,512]{1,0:T(8,128)(2,1)S(1)}, u32[]{:S(2)}, u32[]{:S(2)}) collective-permute-start(bf16[288,512]{1,0:T(8,128)(2,1)S(1)} %get-tuple-element.75), channel_id=1, source_target_pairs={{0,2},{1,3},{2,0},{3,1},{4,6},{5,7},{6,4},{7,5},{8,10},{9,11},{10,... | collective-permute-start | bytes 884744 | tf_op jit(solution)/shard_map/ppermute | solution.py:27
  54.2 1.5 %collective-permute-start.15 = (bf16[128,512]{1,0:T(8,128)(2,1)S(1)}, bf16[128,512]{1,0:T(8,128)(2,1)S(1)}, u32[]{:S(2)}, u32[]{:S(2)}) collective-permute-start(bf16[128,512]{1,0:T(8,128)(2,1)S(1)} %shard_map.119), channel_id=1, source_target_pairs={{0,8},{8,0},{16,24},{24,16},{1,9},{9,1},{17,25},{25,17},{2,10},{10... | collective-permute-start | bytes 393224 | tf_op jit(solution)/shard_map/ppermute | solution.py:27
  55.7 3.4 %collective-permute-done.22.refs_1_ = bf16[512,256]{1,0:T(8,128)(2,1)S(1)} collective-permute-done((bf16[512,256]{1,0:T(8,128)(2,1)S(1)}, bf16[512,256]{1,0:T(8,128)(2,1)S(1)}, u32[]{:S(2)}, u32[]{:S(2)}) %collective-permute-start.22) | collective-permute-done | bytes 262176 | tf_op jit(solution)/shard_map/ppermute | solution.py:27
  61.5 3.5 %collective-permute-start.19 = (bf16[160,512]{1,0:T(8,128)(2,1)S(1)}, bf16[160,512]{1,0:T(8,128)(2,1)S(1)}, u32[]{:S(2)}, u32[]{:S(2)}) collective-permute-start(bf16[160,512]{1,0:T(8,128)(2,1)S(1)} %get-tuple-element.77.refs_5_), channel_id=1, source_target_pairs={{0,4},{1,5},{2,6},{3,7},{4,0},{5,1},{6,2},{7,3},{8,12},{9,13},{10,... | collective-permute-start | bytes 491528 | tf_op jit(solution)/shard_map/ppermute | solution.py:27
  65.0 2.6 %shard_map.129 = (bf16[128,768]{1,0:T(8,128)(2,1)S(1)}, bf16[128,768]{1,0:T(8,128)(2,1)S(1)}, bf16[128,768]{1,0:T(8,128)(2,1)S(1)}, bf16[64,768]{1,0:T(8,128)(2,1)S(1)}, bf16[64,768]{1,0:T(8,128)(2,1)S(1)}) custom-call(bf16[512,768]{1,0:T(8,128)(2,1)S(1)} %get-tuple-element.82.refs_0_, bf16[256,256]{1,0:T(8,128)(2,1)S(1)} %get-tuple-element.85.refs_1_, ...), custom_call_target="tpu_custom_call" | custom-call | flops 3221225472 | bytes 2097152 | tf_op jit(solution)/shard_map/pallas_call | solution.py:51
  69.7 1.9 %collective-permute-done.19.refs_1_ = bf16[160,512]{1,0:T(8,128)(2,1)S(1)} collective-permute-done((bf16[160,512]{1,0:T(8,128)(2,1)S(1)}, bf16[160,512]{1,0:T(8,128)(2,1)S(1)}, u32[]{:S(2)}, u32[]{:S(2)}) %collective-permute-start.19) | collective-permute-done | bytes 163872 | tf_op jit(solution)/shard_map/ppermute | solution.py:27
  73.4 1.5 %collective-permute-start.27 = (bf16[128,768]{1,0:T(8,128)(2,1)S(1)}, bf16[128,768]{1,0:T(8,128)(2,1)S(1)}, u32[]{:S(2)}, u32[]{:S(2)}) collective-permute-start(bf16[128,768]{1,0:T(8,128)(2,1)S(1)} %shard_map.130), channel_id=1, source_target_pairs={{0,16},{8,24},{16,0},{24,8},{1,17},{9,25},{17,1},{25,9},{2,18},{10... | collective-permute-start | bytes 589832 | tf_op jit(solution)/shard_map/ppermute | solution.py:27
  75.5 2.0 %collective-permute-done.20.refs_1_.refs_6_ = bf16[128,512]{1,0:T(8,128)(2,1)S(1)} collective-permute-done((bf16[128,512]{1,0:T(8,128)(2,1)S(1)}, bf16[128,512]{1,0:T(8,128)(2,1)S(1)}, u32[]{:S(2)}, u32[]{:S(2)}) %collective-permute-start.20) | collective-permute-done | bytes 131104 | tf_op jit(solution)/shard_map/ppermute | solution.py:27
  79.7 1.4 %collective-permute-done.29.refs_12_ = bf16[128,768]{1,0:T(8,128)(2,1)S(1)} collective-permute-done((bf16[128,768]{1,0:T(8,128)(2,1)S(1)}, bf16[128,768]{1,0:T(8,128)(2,1)S(1)}, u32[]{:S(2)}, u32[]{:S(2)}) %collective-permute-start.29) | collective-permute-done | bytes 196640 | tf_op jit(solution)/shard_map/ppermute | solution.py:27
  81.1 1.5 %collective-permute-done.21.refs_7_ = bf16[128,512]{1,0:T(8,128)(2,1)S(1)} collective-permute-done((bf16[128,512]{1,0:T(8,128)(2,1)S(1)}, bf16[128,512]{1,0:T(8,128)(2,1)S(1)}, u32[]{:S(2)}, u32[]{:S(2)}) %collective-permute-start.21) | collective-permute-done | bytes 131104 | tf_op jit(solution)/shard_map/ppermute | solution.py:27
  82.6 1.5 %shard_map.132 = (bf16[1,128,2048]{2,1,0:T(8,128)(2,1)}, bf16[1,128,1024]{2,1,0:T(8,128)(2,1)}, bf16[1,128,1024]{2,1,0:T(8,128)(2,1)}, bf16[1,128,1024]{2,1,0:T(...) custom-call(bf16[128,512]{1,0:T(8,128)(2,1)S(1)} %get-tuple-element.60.refs_0_, ...), custom_call_target="tpu_custom_call" | custom-call | bytes 3792896 | tf_op jit(solution)/shard_map/pallas_call | solution.py:51
  (64 shorter events, 22.3 us)
Async XLA Ops:
  1.9 9.8 %collective-permute-start = (bf16[160,768]{1,0:T(8,128)(2,1)S(1)}, bf16[160,768]{1,0:T(8,128)(2,1)S(1)}, u32[]{:S(2)}, u32[]{:S(2)}) collective-permute-start(bf16[160,768]{1,0:T(8,128)(2,1)S(1)} %get-tuple-element.52), channel_id=1, source_target_pairs={{0,8},{8,0},{16,24},{24,16},{1,9},{9,1},{17,25},{25,17},{2,10},{10... | collective-permute-start | bytes 737288 | tf_op jit(solution)/shard_map/ppermute | solution.py:27
  4.9 12.7 %collective-permute-start.1 = (bf16[160,768]{1,0:T(8,128)(2,1)S(1)}, bf16[160,768]{1,0:T(8,128)(2,1)S(1)}, u32[]{:S(2)}, u32[]{:S(2)}) collective-permute-start(bf16[160,768]{1,0:T(8,128)(2,1)S(1)} %get-tuple-element.53), channel_id=1, source_target_pairs={{0,16},{8,24},{16,0},{24,8},{1,17},{9,25},{17,1},{25,9},{2,18},{10... | collective-permute-start | bytes 737288 | tf_op jit(solution)/shard_map/ppermute | solution.py:27
  6.5 11.2 %collective-permute-start.2 = (bf16[160,768]{1,0:T(8,128)(2,1)S(1)}, bf16[160,768]{1,0:T(8,128)(2,1)S(1)}, u32[]{:S(2)}, u32[]{:S(2)}) collective-permute-start(bf16[160,768]{1,0:T(8,128)(2,1)S(1)} %get-tuple-element.54), channel_id=1, source_target_pairs={{0,24},{8,16},{16,8},{24,0},{1,25},{9,17},{17,9},{25,1},{2,26},{10... | collective-permute-start | bytes 737288 | tf_op jit(solution)/shard_map/ppermute | solution.py:27
  20.3 6.0 %collective-permute-start.5 = (bf16[256,256]{1,0:T(8,128)(2,1)S(1)}, bf16[256,256]{1,0:T(8,128)(2,1)S(1)}, u32[]{:S(2)}, u32[]{:S(2)}) collective-permute-start(bf16[256,256]{1,0:T(8,128)(2,1)S(1)} %get-tuple-element.56.refs_0_.refs_3_), channel_id=1, source_target_pairs={{0,16},{8,24},{16,0},{24,8},{1,17},{9,25},{17,1},{25,9},{2,18},{10... | collective-permute-start | bytes 393224 | tf_op jit(solution)/shard_map/ppermute | solution.py:27
  21.1 7.4 %collective-permute-start.7 = (bf16[128,512]{1,0:T(8,128)(2,1)S(1)}, bf16[128,512]{1,0:T(8,128)(2,1)S(1)}, u32[]{:S(2)}, u32[]{:S(2)}) collective-permute-start(bf16[128,512]{1,0:T(8,128)(2,1)S(1)} %get-tuple-element.57.refs_0_), channel_id=1, source_target_pairs={{0,4},{1,5},{2,6},{3,7},{4,0},{5,1},{6,2},{7,3},{8,12},{9,13},{10,... | collective-permute-start | bytes 393224 | tf_op jit(solution)/shard_map/ppermute | solution.py:27
  24.1 11.7 %collective-permute-start.4 = (bf16[512,256]{1,0:T(8,128)(2,1)S(1)}, bf16[512,256]{1,0:T(8,128)(2,1)S(1)}, u32[]{:S(2)}, u32[]{:S(2)}) collective-permute-start(bf16[512,256]{1,0:T(8,128)(2,1)S(1)} %shard_map.111), channel_id=1, source_target_pairs={{0,16},{8,24},{16,0},{24,8},{1,17},{9,25},{17,1},{25,9},{2,18},{10... | collective-permute-start | bytes 786440 | tf_op jit(solution)/shard_map/ppermute | solution.py:27
  26.4 9.4 %collective-permute-start.6 = (bf16[512,256]{1,0:T(8,128)(2,1)S(1)}, bf16[512,256]{1,0:T(8,128)(2,1)S(1)}, u32[]{:S(2)}, u32[]{:S(2)}) collective-permute-start(bf16[512,256]{1,0:T(8,128)(2,1)S(1)} %shard_map.112), channel_id=1, source_target_pairs={{0,8},{8,0},{16,24},{24,16},{1,9},{9,1},{17,25},{25,17},{2,10},{10... | collective-permute-start | bytes 786440 | tf_op jit(solution)/shard_map/ppermute | solution.py:27
  28.5 7.2 %collective-permute-start.8 = (bf16[256,512]{1,0:T(8,128)(2,1)S(1)}, bf16[256,512]{1,0:T(8,128)(2,1)S(1)}, u32[]{:S(2)}, u32[]{:S(2)}) collective-permute-start(bf16[256,512]{1,0:T(8,128)(2,1)S(1)} %shard_map.113.refs_0_), channel_id=1, source_target_pairs={{0,2},{1,3},{2,0},{3,1},{4,6},{5,7},{6,4},{7,5},{8,10},{9,11},{10,... | collective-permute-start | bytes 786440 | tf_op jit(solution)/shard_map/ppermute | solution.py:27
  29.2 5.3 %collective-permute-start.9 = (bf16[128,512]{1,0:T(8,128)(2,1)S(1)}, bf16[128,512]{1,0:T(8,128)(2,1)S(1)}, u32[]{:S(2)}, u32[]{:S(2)}) collective-permute-start(bf16[128,512]{1,0:T(8,128)(2,1)S(1)} %get-tuple-element.58), channel_id=1, source_target_pairs={{0,8},{8,0},{16,24},{24,16},{1,9},{9,1},{17,25},{25,17},{2,10},{10... | collective-permute-start | bytes 393224 | tf_op jit(solution)/shard_map/ppermute | solution.py:27
  35.9 7.5 %collective-permute-start.16 = (bf16[128,512]{1,0:T(8,128)(2,1)S(1)}, bf16[128,512]{1,0:T(8,128)(2,1)S(1)}, u32[]{:S(2)}, u32[]{:S(2)}) collective-permute-start(bf16[128,512]{1,0:T(8,128)(2,1)S(1)} %get-tuple-element.67), channel_id=1, source_target_pairs={{0,24},{8,16},{16,8},{24,0},{1,25},{9,17},{17,9},{25,1},{2,26},{10... | collective-permute-start | bytes 393224 | tf_op jit(solution)/shard_map/ppermute | solution.py:27
  41.3 7.7 %collective-permute-start.12 = (bf16[128,512]{1,0:T(8,128)(2,1)S(1)}, bf16[128,512]{1,0:T(8,128)(2,1)S(1)}, u32[]{:S(2)}, u32[]{:S(2)}) collective-permute-start(bf16[128,512]{1,0:T(8,128)(2,1)S(1)} %get-tuple-element.61), channel_id=1, source_target_pairs={{0,8},{8,0},{16,24},{24,16},{1,9},{9,1},{17,25},{25,17},{2,10},{10... | collective-permute-start | bytes 393224 | tf_op jit(solution)/shard_map/ppermute | solution.py:27
  42.1 7.0 %collective-permute-start.14 = (bf16[128,512]{1,0:T(8,128)(2,1)S(1)}, bf16[128,512]{1,0:T(8,128)(2,1)S(1)}, u32[]{:S(2)}, u32[]{:S(2)}) collective-permute-start(bf16[128,512]{1,0:T(8,128)(2,1)S(1)} %get-tuple-element.63), channel_id=1, source_target_pairs={{0,16},{8,24},{16,0},{24,8},{1,17},{9,25},{17,1},{25,9},{2,18},{10... | collective-permute-start | bytes 393224 | tf_op jit(solution)/shard_map/ppermute | solution.py:27
  49.9 9.2 %collective-permute-start.22 = (bf16[512,256]{1,0:T(8,128)(2,1)S(1)}, bf16[512,256]{1,0:T(8,128)(2,1)S(1)}, u32[]{:S(2)}, u32[]{:S(2)}) collective-permute-start(bf16[512,256]{1,0:T(8,128)(2,1)S(1)} %get-tuple-element.84), channel_id=1, source_target_pairs={{0,8},{8,0},{16,24},{24,16},{1,9},{9,1},{17,25},{25,17},{2,10},{10... | collective-permute-start | bytes 786440 | tf_op jit(solution)/shard_map/ppermute | solution.py:27
  50.6 9.4 %collective-permute-start.24 = (bf16[512,256]{1,0:T(8,128)(2,1)S(1)}, bf16[512,256]{1,0:T(8,128)(2,1)S(1)}, u32[]{:S(2)}, u32[]{:S(2)}) collective-permute-start(bf16[512,256]{1,0:T(8,128)(2,1)S(1)} %get-tuple-element.88), channel_id=1, source_target_pairs={{0,16},{8,24},{16,0},{24,8},{1,17},{9,25},{17,1},{25,9},{2,18},{10... | collective-permute-start | bytes 786440 | tf_op jit(solution)/shard_map/ppermute | solution.py:27
  52.2 9.2 %collective-permute-start.18 = (bf16[288,512]{1,0:T(8,128)(2,1)S(1)}, bf16[288,512]{1,0:T(8,128)(2,1)S(1)}, u32[]{:S(2)}, u32[]{:S(2)}) collective-permute-start(bf16[288,512]{1,0:T(8,128)(2,1)S(1)} %get-tuple-element.75), channel_id=1, source_target_pairs={{0,2},{1,3},{2,0},{3,1},{4,6},{5,7},{6,4},{7,5},{8,10},{9,11},{10,... | collective-permute-start | bytes 884744 | tf_op jit(solution)/shard_map/ppermute | solution.py:27
  53.7 11.3 %collective-permute-start.13 = (bf16[128,512]{1,0:T(8,128)(2,1)S(1)}, bf16[128,512]{1,0:T(8,128)(2,1)S(1)}, u32[]{:S(2)}, u32[]{:S(2)}) collective-permute-start(bf16[128,512]{1,0:T(8,128)(2,1)S(1)} %shard_map.118), channel_id=1, source_target_pairs={{0,16},{8,24},{16,0},{24,8},{1,17},{9,25},{17,1},{25,9},{2,18},{10... | collective-permute-start | bytes 393224 | tf_op jit(solution)/shard_map/ppermute | solution.py:27
  54.2 10.8 %collective-permute-start.15 = (bf16[128,512]{1,0:T(8,128)(2,1)S(1)}, bf16[128,512]{1,0:T(8,128)(2,1)S(1)}, u32[]{:S(2)}, u32[]{:S(2)}) collective-permute-start(bf16[128,512]{1,0:T(8,128)(2,1)S(1)} %shard_map.119), channel_id=1, source_target_pairs={{0,8},{8,0},{16,24},{24,16},{1,9},{9,1},{17,25},{25,17},{2,10},{10... | collective-permute-start | bytes 393224 | tf_op jit(solution)/shard_map/ppermute | solution.py:27
  59.1 5.9 %collective-permute-start.23 = (bf16[256,256]{1,0:T(8,128)(2,1)S(1)}, bf16[256,256]{1,0:T(8,128)(2,1)S(1)}, u32[]{:S(2)}, u32[]{:S(2)}) collective-permute-start(bf16[256,256]{1,0:T(8,128)(2,1)S(1)} %get-tuple-element.86), channel_id=1, source_target_pairs={{0,16},{8,24},{16,0},{24,8},{1,17},{9,25},{17,1},{25,9},{2,18},{10... | collective-permute-start | bytes 393224 | tf_op jit(solution)/shard_map/ppermute | solution.py:27
  61.5 10.1 %collective-permute-start.19 = (bf16[160,512]{1,0:T(8,128)(2,1)S(1)}, bf16[160,512]{1,0:T(8,128)(2,1)S(1)}, u32[]{:S(2)}, u32[]{:S(2)}) collective-permute-start(bf16[160,512]{1,0:T(8,128)(2,1)S(1)} %get-tuple-element.77.refs_5_), channel_id=1, source_target_pairs={{0,4},{1,5},{2,6},{3,7},{4,0},{5,1},{6,2},{7,3},{8,12},{9,13},{10,... | collective-permute-start | bytes 491528 | tf_op jit(solution)/shard_map/ppermute | solution.py:27
  67.7 5.7 %collective-permute-start.26 = (bf16[128,768]{1,0:T(8,128)(2,1)S(1)}, bf16[128,768]{1,0:T(8,128)(2,1)S(1)}, u32[]{:S(2)}, u32[]{:S(2)}) collective-permute-start(bf16[128,768]{1,0:T(8,128)(2,1)S(1)} %get-tuple-element.92), channel_id=1, source_target_pairs={{0,8},{8,0},{16,24},{24,16},{1,9},{9,1},{17,25},{25,17},{2,10},{10... | collective-permute-start | bytes 589832 | tf_op jit(solution)/shard_map/ppermute | solution.py:27
  69.1 5.9 %collective-permute-start.28 = (bf16[128,768]{1,0:T(8,128)(2,1)S(1)}, bf16[128,768]{1,0:T(8,128)(2,1)S(1)}, u32[]{:S(2)}, u32[]{:S(2)}) collective-permute-start(bf16[128,768]{1,0:T(8,128)(2,1)S(1)} %get-tuple-element.94), channel_id=1, source_target_pairs={{0,16},{8,24},{16,0},{24,8},{1,17},{9,25},{17,1},{25,9},{2,18},{10... | collective-permute-start | bytes 589832 | tf_op jit(solution)/shard_map/ppermute | solution.py:27
  71.6 6.0 %collective-permute-start.20 = (bf16[128,512]{1,0:T(8,128)(2,1)S(1)}, bf16[128,512]{1,0:T(8,128)(2,1)S(1)}, u32[]{:S(2)}, u32[]{:S(2)}) collective-permute-start(bf16[128,512]{1,0:T(8,128)(2,1)S(1)} %shard_map.125), channel_id=1, source_target_pairs={{0,8},{8,0},{16,24},{24,16},{1,9},{9,1},{17,25},{25,17},{2,10},{10... | collective-permute-start | bytes 393224 | tf_op jit(solution)/shard_map/ppermute | solution.py:27
  73.4 6.3 %collective-permute-start.27 = (bf16[128,768]{1,0:T(8,128)(2,1)S(1)}, bf16[128,768]{1,0:T(8,128)(2,1)S(1)}, u32[]{:S(2)}, u32[]{:S(2)}) collective-permute-start(bf16[128,768]{1,0:T(8,128)(2,1)S(1)} %shard_map.130), channel_id=1, source_target_pairs={{0,16},{8,24},{16,0},{24,8},{1,17},{9,25},{17,1},{25,9},{2,18},{10... | collective-permute-start | bytes 589832 | tf_op jit(solution)/shard_map/ppermute | solution.py:27
  75.0 6.2 %collective-permute-start.29 = (bf16[128,768]{1,0:T(8,128)(2,1)S(1)}, bf16[128,768]{1,0:T(8,128)(2,1)S(1)}, u32[]{:S(2)}, u32[]{:S(2)}) collective-permute-start(bf16[128,768]{1,0:T(8,128)(2,1)S(1)} %shard_map.131), channel_id=1, source_target_pairs={{0,8},{8,0},{16,24},{24,16},{1,9},{9,1},{17,25},{25,17},{2,10},{10... | collective-permute-start | bytes 589832 | tf_op jit(solution)/shard_map/ppermute | solution.py:27
  (8 other events, 29.1 us)

commit v4 on v3

--- a/solution.py
+++ b/solution.py
@@ -13,6 +13,7 @@
 LANES = 128
 TILE = 64
 TAPS = 32
+FOLD = 32
 CONV_COST = 600
 ATTEND_COST = 24
 BACK_COST = 48
@@ -122,16 +123,23 @@
     width, channels = inner // groups, model // groups
     for k in range(groups):
         columns = block(me ^ k, width, LANES)
-        for at in range(3):
-            outs[k][:local, at * width : (at + 1) * width] = held[at][:, columns]
         cells = held[3][:, block(me ^ k, channels, LANES)]
         if weight_outs:
             weight_outs[k][...] = cells
+            for at in range(3):
+                outs[k][:, at * width : (at + 1) * width] = held[at][:, columns]
         else:
-            half = rows // 2
-            outs[k][local : local + half, :channels] = cells[:half, :]
-            outs[k][local : local + half, channels:] = cells[half:, :width]
-            outs[k][local + half : local + rows, :width] = cells[half:, width:]
+            for at, start, there, column in folds(local, width):
+                outs[k][there : there + FOLD, column : column + width] = held[at][start : start + FOLD, columns]
+            below = outs[k].shape[0] - rows // 2
+            outs[k][below:, :channels] = cells[: rows // 2, :]
+            outs[k][below:, channels:] = cells[rows // 2 :, :]
+
+
+def folds(local, width):
+    tall = 3 * local // 4
+    for start in range(0, 3 * local, FOLD):
+        yield start // local, start % local, start % tall, start // tall * width
 
 
 def pack_columns(groups, *refs):
@@ -164,17 +172,19 @@
     local = rows_ref.shape[0] // groups
     half, width = outs[0].shape
     for k in range(groups):
-        rows_ref[block(me ^ k, local, local), :] = pieces[k][:local, :]
-    if weight_refs:
-        rows = pieces[0].shape[0] - local
-        share = rows // 2
-        channels = weight_refs[0].shape[1]
-        for k in range(groups):
-            at = k * rows
-            top, end = pieces[k][local : local + share, :], pieces[k][local + share :, :]
-            weight_refs[0][at : at + share, :] = top[:, :channels]
-            weight_refs[0][at + share : at + rows, :width] = top[:, channels:]
-            weight_refs[0][at + share : at + rows, width:] = end[:, :width]
+        if weight_refs:
+            for at, start, there, column in folds(local, width):
+                first = pl.multiple_of((me ^ k) * local + start, FOLD)
+                cells = pieces[k][there : there + FOLD, column : column + width]
+                rows_ref[pl.ds(first, FOLD), at * width : (at + 1) * width] = cells
+            channels = weight_refs[0].shape[1]
+            rows = weight_refs[0].shape[0] // groups
+            at, share = k * rows, rows // 2
+            below = pieces[k].shape[0] - share
+            weight_refs[0][at : at + share, :] = pieces[k][below:, :channels]
+            weight_refs[0][at + share : at + rows, :] = pieces[k][below:, channels:]
+        else:
+            rows_ref[block(me ^ k, local, local), :] = pieces[k][...]
     for head in range(width // HDIM):
         at = head * HDIM
         queries = rows_ref[:, at : at + HDIM]
@@ -340,10 +350,21 @@
     goes[...] = total[half:, :]
 
 
+def weigh(rows_ref, out):
+    width = rows_ref.shape[1] // 3
+    for head in range(width // HDIM):
+        at = head * HDIM
+        queries = rows_ref[:, at : at + HDIM]
+        keys = rows_ref[:, width + at : width + at + HDIM]
+        scores = product(queries, keys, 1, 1) * ROOT
+        exponent = jnp.exp(scores - jnp.max(scores, axis=1, keepdims=True))
+        out[head] = exponent * (1.0 / jnp.sum(exponent, axis=1, keepdims=True))
+
+
 def attend_back(groups, *refs):
-    rows_ref = refs[0]
-    upstream = refs[1 : groups + 1]
-    outs = refs[groups + 1 : -2]
+    rows_ref, weights_ref = refs[:2]
+    upstream = refs[2 : groups + 2]
+    outs = refs[groups + 2 : -2]
     grads, result = refs[-2:]
     me = lax.axis_index("fsdp")
     width = upstream[0].shape[1]
@@ -361,9 +382,7 @@
         keys = rows_ref[:, width + at : width + at + HDIM]
         values = rows_ref[:, 2 * width + at : 2 * width + at + HDIM]
         above = grads[:, at : at + HDIM]
-        scores = product(queries, keys, 1, 1) * ROOT
-        exponent = jnp.exp(scores - jnp.max(scores, axis=1, keepdims=True))
-        weights = exponent * (1.0 / jnp.sum(exponent, axis=1, keepdims=True))
+        weights = weights_ref[head]
         slopes = product(above, values, 1, 1)
         row_dot = jnp.sum(weights * slopes, axis=1, keepdims=True)
         grad_scores = (weights * (slopes - row_dot)).astype(BF16)
@@ -455,10 +474,12 @@
     return [sent[0], first, second]
 
 
-def gather_weight(gathered, masks, groups, count, after):
-    rows, channels = gathered.shape[0] * 2 ** (len(masks) + 1) // (groups * count), gathered.shape[1]
-    for mask in masks:
-        gathered = stack(gathered, swap(gathered, "frame", mask), after=after)
+def gather_weight(mine, groups, count, after):
+    rows, channels = mine.shape[0] // groups, mine.shape[1]
+    pieces = [mine]
+    for mask in reversed(masks_of(count)[1:]):
+        pieces += [swap(piece, "frame", mask) for piece in pieces]
+    gathered = stack(*pieces, after=after)
     other = swap(gathered, "frame", 1)
     if rows % 16 == 0:
         return call(
@@ -528,11 +549,12 @@
         shape, small = ((local, size), BF16), ((local // 2, size), BF16)
         return [shape, shape, shape, small, small] if folded else [shape] * groups
 
-    merged = folded and rows % 32 == 0 and channels == 2 * width
+    merged = folded and rows % 32 == 0 and channels == 2 * width and local % (4 * FOLD) == 0
+    shape = (3 * local // 4 + rows // 2, 4 * width) if merged else (local, 3 * width)
     whole = (groups * rows, channels)
     sent = call(
         functools.partial(pack_rows, groups),
-        [((local + (rows if merged else 0), 3 * width), BF16)] * groups
+        [(shape, BF16)] * groups
         + ([] if merged else [((rows, channels), BF16)] * groups),
         queries[0],
         key_rows[0],
@@ -554,7 +576,6 @@
         flops=ATTEND_COST * frames * frames * width,
     )
     gathered = own.pop() if merged else stack(*exchange(sent[groups:]))
-    first, *masks = reversed(masks_of(count)[1:])
     if folded:
         top, end = own
         beside, across = swap(top, "fsdp", 1), swap(end, "fsdp", 2)
@@ -565,7 +586,6 @@
     else:
         attention = exchange(own * groups)
         step = last = attention[1:2]
-    gathered = stack(gathered, swap(gathered, "frame", first), after=step)
     sent = call(
         functools.partial(pack_columns, groups),
         [((local, channels), BF16)] * groups,
@@ -573,7 +593,7 @@
         after=step,
     )
     upstream = exchange(sent)
-    weight = gather_weight(gathered, masks, groups, count, last + upstream[1:3])
+    weight = gather_weight(gathered, groups, count, last + upstream[1:3])
 
     outs = call(
         functools.partial(convolve, groups),
@@ -590,7 +610,8 @@
         flops=conv_flops,
     )
     whole, projected, slope = outs[:3]
-    ahead = exchange_split(outs[3:])
+    (weights,) = call(weigh, [((width // HDIM, frames, frames), F32)], held)
+    ahead = exchange_split(outs[3:], after=[weights])
 
     outs = call(
         functools.partial(convolve_back, groups),
@@ -625,6 +646,7 @@
         functools.partial(attend_back, groups),
         split(3 * width),
         held,
+        weights,
         *above,
         scratch=[pltpu.VMEM((frames, width), BF16), pltpu.VMEM((frames, 3 * width), BF16)],
         flops=BACK_COST * frames * frames * width,

time: 84.3 us -> 83.4 us (0.989)
  waiting for transfers between devices: 31.2 us -> 28.7 us
  starting transfers between devices: 34.8 us -> 36.3 us
    ppermute x30 -> x31, waiting for transfers between devices: 31.2 us -> 28.7 us  [swap(): return lax.ppermute(cells, axis, [(i, i ^ mask) for i in range(count)])]
    ppermute x30 -> x31, starting transfers between devices: 34.8 us -> 36.3 us  [swap(): return lax.ppermute(cells, axis, [(i, i ^ mask) for i in range(count)])]
  transfers between devices with their start and end apart: 30 -> 31, of which waited for: 15 -> 18; matrix products, arithmetic and copies ran while one was open for 0% -> 0% of each run, Pallas kernels for 15% -> 15%
where the time goes in v4:
time: 83.4 us; the launch traced here: 83.2 us
  starting transfers between devices  36.3 us (44%)
  waiting for transfers between devices  28.7 us (34%)
  Pallas kernels  17.4 us (21%)
    ppermute x31, starting transfers between devices, swap(): return lax.ppermute(cells, axis, [(i, i ^ mask) for i in range(count)])  36.3 us
    ppermute x31, waiting for transfers between devices, swap(): return lax.ppermute(cells, axis, [(i, i ^ mask) for i in range(count)])  28.7 us
    pallas_call x24, Pallas kernels, call(): pl.pallas_call(lambda *refs: body(*refs[:count], *refs[count + len(after)...  17.4 us
  transfers between devices with their start and end apart: 31, of which 18 were waited for; matrix products, arithmetic and copies ran while one was open for 0% of the time, Pallas kernels for 15%

profile of v4, /device:TPU:0, one launch (start us, length us, event | category | flops | bytes accessed | tf_op | source)
XLA Modules:
  0.0 83.2 jit_solution(3916657688366909450)
XLA Ops:
  1.9 3.0 %collective-permute-start = (bf16[112,1024]{1,0:T(8,128)(2,1)S(1)}, bf16[112,1024]{1,0:T(8,128)(2,1)S(1)}, u32[]{:S(2)}, u32[]{:S(2)}) collective-permute-start(bf16[112,1024]{1,0:T(8,128)(2,1)S(1)} %get-tuple-element.52), channel_id=1, source_target_pairs={{0,8},{8,0},{16,24},{24,16},{1,9},{9,1},{17,25},{25,17},{2,10},{10... | collective-permute-start | bytes 688136 | tf_op jit(solution)/shard_map/ppermute | solution.py:28
  4.9 1.5 %collective-permute-start.1 = (bf16[112,1024]{1,0:T(8,128)(2,1)S(1)}, bf16[112,1024]{1,0:T(8,128)(2,1)S(1)}, u32[]{:S(2)}, u32[]{:S(2)}) collective-permute-start(bf16[112,1024]{1,0:T(8,128)(2,1)S(1)} %get-tuple-element.53), channel_id=1, source_target_pairs={{0,16},{8,24},{16,0},{24,8},{1,17},{9,25},{17,1},{25,9},{2,18},{10... | collective-permute-start | bytes 688136 | tf_op jit(solution)/shard_map/ppermute | solution.py:28
  6.5 4.9 %collective-permute-done.refs_1_ = bf16[112,1024]{1,0:T(8,128)(2,1)S(1)} collective-permute-done((bf16[112,1024]{1,0:T(8,128)(2,1)S(1)}, bf16[112,1024]{1,0:T(8,128)(2,1)S(1)}, u32[]{:S(2)}, u32[]{:S(2)}) %collective-permute-start) | collective-permute-done | bytes 229408 | tf_op jit(solution)/shard_map/ppermute | solution.py:28
  11.4 5.5 %collective-permute-done.1.refs_2_ = bf16[112,1024]{1,0:T(8,128)(2,1)S(1)} collective-permute-done((bf16[112,1024]{1,0:T(8,128)(2,1)S(1)}, bf16[112,1024]{1,0:T(8,128)(2,1)S(1)}, u32[]{:S(2)}, u32[]{:S(2)}) %collective-permute-start.1) | collective-permute-done | bytes 229408 | tf_op jit(solution)/shard_map/ppermute | solution.py:28
  16.9 1.4 %shard_map.110 = (bf16[512,768]{1,0:T(8,128)(2,1)S(1)}, bf16[256,256]{1,0:T(8,128)(2,1)S(1)}, bf16[256,256]{1,0:T(8,128)(2,1)S(1)}, bf16[128,512]{1,0:T(8,128)(2,1)S(1)}) custom-call(bf16[112,1024]{1,0:T(8,128)(2,1)S(1)} %get-tuple-element.51.refs_0_, bf16[112,1024]{1,0:T(8,128)(2,1)S(1)} %collective-permute-done.refs_1_, ...), custom_call_target="tpu_custom_call" | custom-call | flops 1610612736 | bytes 2097152 | tf_op jit(solution)/shard_map/pallas_call | solution.py:52
  18.3 1.6 %collective-permute-start.5 = (bf16[256,256]{1,0:T(8,128)(2,1)S(1)}, bf16[256,256]{1,0:T(8,128)(2,1)S(1)}, u32[]{:S(2)}, u32[]{:S(2)}) collective-permute-start(bf16[256,256]{1,0:T(8,128)(2,1)S(1)} %get-tuple-element.56.refs_0_.refs_3_), channel_id=1, source_target_pairs={{0,16},{8,24},{16,0},{24,8},{1,17},{9,25},{17,1},{25,9},{2,18},{10... | collective-permute-start | bytes 393224 | tf_op jit(solution)/shard_map/ppermute | solution.py:28
  20.4 2.6 %collective-permute-start.7 = (bf16[128,512]{1,0:T(8,128)(2,1)S(1)}, bf16[128,512]{1,0:T(8,128)(2,1)S(1)}, u32[]{:S(2)}, u32[]{:S(2)}) collective-permute-start(bf16[128,512]{1,0:T(8,128)(2,1)S(1)} %get-tuple-element.57.refs_0_), channel_id=1, source_target_pairs={{0,4},{1,5},{2,6},{3,7},{4,0},{5,1},{6,2},{7,3},{8,12},{9,13},{10,... | collective-permute-start | bytes 393224 | tf_op jit(solution)/shard_map/ppermute | solution.py:28
  23.0 1.6 %collective-permute-start.8 = (bf16[128,512]{1,0:T(8,128)(2,1)S(1)}, bf16[128,512]{1,0:T(8,128)(2,1)S(1)}, u32[]{:S(2)}, u32[]{:S(2)}) collective-permute-start(bf16[128,512]{1,0:T(8,128)(2,1)S(1)} %get-tuple-element.57.refs_0_), channel_id=1, source_target_pairs={{0,2},{1,3},{2,0},{3,1},{4,6},{5,7},{6,4},{7,5},{8,10},{9,11},{10,... | collective-permute-start | bytes 393224 | tf_op jit(solution)/shard_map/ppermute | solution.py:28
  24.6 1.6 %collective-permute-start.6 = (bf16[512,256]{1,0:T(8,128)(2,1)S(1)}, bf16[512,256]{1,0:T(8,128)(2,1)S(1)}, u32[]{:S(2)}, u32[]{:S(2)}) collective-permute-start(bf16[512,256]{1,0:T(8,128)(2,1)S(1)} %shard_map.112), channel_id=1, source_target_pairs={{0,8},{8,0},{16,24},{24,16},{1,9},{9,1},{17,25},{25,17},{2,10},{10... | collective-permute-start | bytes 786440 | tf_op jit(solution)/shard_map/ppermute | solution.py:28
  29.9 3.4 %collective-permute-done.10.refs_6_.refs_1_ = bf16[128,512]{1,0:T(8,128)(2,1)S(1)} collective-permute-done((bf16[128,512]{1,0:T(8,128)(2,1)S(1)}, bf16[128,512]{1,0:T(8,128)(2,1)S(1)}, u32[]{:S(2)}, u32[]{:S(2)}) %collective-permute-start.10) | collective-permute-done | bytes 131104 | tf_op jit(solution)/shard_map/ppermute | solution.py:28
  34.4 1.8 %collective-permute-start.17 = (bf16[128,512]{1,0:T(8,128)(2,1)S(1)}, bf16[128,512]{1,0:T(8,128)(2,1)S(1)}, u32[]{:S(2)}, u32[]{:S(2)}) collective-permute-start(bf16[128,512]{1,0:T(8,128)(2,1)S(1)} %get-tuple-element.68), channel_id=1, source_target_pairs={{0,24},{8,16},{16,8},{24,0},{1,25},{9,17},{17,9},{25,1},{2,26},{10... | collective-permute-start | bytes 393224 | tf_op jit(solution)/shard_map/ppermute | solution.py:28
  36.4 3.4 %shard_map.116 = (bf16[512,1024]{1,0:T(8,128)(2,1)S(1)}, bf16[512,512]{1,0:T(8,128)(2,1)S(1)}, f32[512,512]{1,0:T(8,128)S(1)}, bf16[128,512]{1,0:T(8,128)(2,1)S(...) custom-call(bf16[256,256]{1,0:T(8,128)(2,1)S(1)} %get-tuple-element., ...), custom_call_target="tpu_custom_call" | custom-call | flops 4875878400 | bytes 5369856 | tf_op jit(solution)/shard_map/pallas_call | solution.py:52
  42.2 5.7 %shard_map.120 = (bf16[512,512]{1,0:T(8,128)(2,1)S(1)}, f32[32,512]{1,0:T(8,128)S(1)}, bf16[512,256]{1,0:T(8,128)(2,1)S(1)}, bf16[512,256]{1,0:T(8,128)(2,1)S(1)...) custom-call(bf16[128,512]{1,0:T(8,128)(2,1)S(1)} %get-tuple-element.67.refs_0_, ...), custom_call_target="tpu_custom_call" | custom-call | flops 7313817600 | bytes 4911104 | tf_op jit(solution)/shard_map/pallas_call | solution.py:52
  52.8 1.8 %collective-permute-start.16 = (bf16[128,512]{1,0:T(8,128)(2,1)S(1)}, bf16[128,512]{1,0:T(8,128)(2,1)S(1)}, u32[]{:S(2)}, u32[]{:S(2)}) collective-permute-start(bf16[128,512]{1,0:T(8,128)(2,1)S(1)} %shard_map.119), channel_id=1, source_target_pairs={{0,8},{8,0},{16,24},{24,16},{1,9},{9,1},{17,25},{25,17},{2,10},{10... | collective-permute-start | bytes 393224 | tf_op jit(solution)/shard_map/ppermute | solution.py:28
  54.8 3.1 %collective-permute-done.25.refs_1_ = bf16[512,256]{1,0:T(8,128)(2,1)S(1)} collective-permute-done((bf16[512,256]{1,0:T(8,128)(2,1)S(1)}, bf16[512,256]{1,0:T(8,128)(2,1)S(1)}, u32[]{:S(2)}, u32[]{:S(2)}) %collective-permute-start.25) | collective-permute-done | bytes 262176 | tf_op jit(solution)/shard_map/ppermute | solution.py:28
  60.2 2.1 %collective-permute-start.20 = (bf16[160,512]{1,0:T(8,128)(2,1)S(1)}, bf16[160,512]{1,0:T(8,128)(2,1)S(1)}, u32[]{:S(2)}, u32[]{:S(2)}) collective-permute-start(bf16[160,512]{1,0:T(8,128)(2,1)S(1)} %get-tuple-element.78.refs_6_), channel_id=1, source_target_pairs={{0,4},{1,5},{2,6},{3,7},{4,0},{5,1},{6,2},{7,3},{8,12},{9,13},{10,... | collective-permute-start | bytes 491528 | tf_op jit(solution)/shard_map/ppermute | solution.py:28
  62.3 1.4 %collective-permute-done.26.refs_5_ = bf16[256,256]{1,0:T(8,128)(2,1)S(1)} collective-permute-done((bf16[256,256]{1,0:T(8,128)(2,1)S(1)}, bf16[256,256]{1,0:T(8,128)(2,1)S(1)}, u32[]{:S(2)}, u32[]{:S(2)}) %collective-permute-start.26) | collective-permute-done | bytes 131104 | tf_op jit(solution)/shard_map/ppermute | solution.py:28
  63.9 1.9 %shard_map.129 = (bf16[128,768]{1,0:T(8,128)(2,1)S(1)}, bf16[128,768]{1,0:T(8,128)(2,1)S(1)}, bf16[128,768]{1,0:T(8,128)(2,1)S(1)}, bf16[64,768]{1,0:T(8,128)(2,1)S(1)}, bf16[64,768]{1,0:T(8,128)(2,1)S(1)}) custom-call(bf16[512,768]{1,0:T(8,128)(2,1)S(1)} %get-tuple-element.63.refs_0_, f32[2,512,512]{2,1,0:T(8,128)S(1)} %shard_map.117.refs_2_.refs_1_, ...), custom_call_target="tpu_custom_call" | custom-call | flops 3221225472 | bytes 4194304 | tf_op jit(solution)/shard_map/pallas_call | solution.py:52
  68.0 1.9 %collective-permute-done.20.refs_1_ = bf16[160,512]{1,0:T(8,128)(2,1)S(1)} collective-permute-done((bf16[160,512]{1,0:T(8,128)(2,1)S(1)}, bf16[160,512]{1,0:T(8,128)(2,1)S(1)}, u32[]{:S(2)}, u32[]{:S(2)}) %collective-permute-start.20) | collective-permute-done | bytes 163872 | tf_op jit(solution)/shard_map/ppermute | solution.py:28
  73.2 1.8 %collective-permute-start.28 = (bf16[128,768]{1,0:T(8,128)(2,1)S(1)}, bf16[128,768]{1,0:T(8,128)(2,1)S(1)}, u32[]{:S(2)}, u32[]{:S(2)}) collective-permute-start(bf16[128,768]{1,0:T(8,128)(2,1)S(1)} %shard_map.130), channel_id=1, source_target_pairs={{0,16},{8,24},{16,0},{24,8},{1,17},{9,25},{17,1},{25,9},{2,18},{10... | collective-permute-start | bytes 589832 | tf_op jit(solution)/shard_map/ppermute | solution.py:28
  75.0 1.5 %collective-permute-done.21.refs_1_.refs_6_ = bf16[128,512]{1,0:T(8,128)(2,1)S(1)} collective-permute-done((bf16[128,512]{1,0:T(8,128)(2,1)S(1)}, bf16[128,512]{1,0:T(8,128)(2,1)S(1)}, u32[]{:S(2)}, u32[]{:S(2)}) %collective-permute-start.21) | collective-permute-done | bytes 131104 | tf_op jit(solution)/shard_map/ppermute | solution.py:28
  77.8 2.0 %collective-permute-done.30.refs_12_ = bf16[128,768]{1,0:T(8,128)(2,1)S(1)} collective-permute-done((bf16[128,768]{1,0:T(8,128)(2,1)S(1)}, bf16[128,768]{1,0:T(8,128)(2,1)S(1)}, u32[]{:S(2)}, u32[]{:S(2)}) %collective-permute-start.30) | collective-permute-done | bytes 196640 | tf_op jit(solution)/shard_map/ppermute | solution.py:28
  80.3 1.4 %collective-permute-done.22.refs_7_ = bf16[128,512]{1,0:T(8,128)(2,1)S(1)} collective-permute-done((bf16[128,512]{1,0:T(8,128)(2,1)S(1)}, bf16[128,512]{1,0:T(8,128)(2,1)S(1)}, u32[]{:S(2)}, u32[]{:S(2)}) %collective-permute-start.22) | collective-permute-done | bytes 131104 | tf_op jit(solution)/shard_map/ppermute | solution.py:28
  81.7 1.5 %shard_map.132 = (bf16[1,128,2048]{2,1,0:T(8,128)(2,1)}, bf16[1,128,1024]{2,1,0:T(8,128)(2,1)}, bf16[1,128,1024]{2,1,0:T(8,128)(2,1)}, bf16[1,128,1024]{2,1,0:T(...) custom-call(bf16[128,512]{1,0:T(8,128)(2,1)S(1)} %get-tuple-element.60.refs_0_, ...), custom_call_target="tpu_custom_call" | custom-call | bytes 3792896 | tf_op jit(solution)/shard_map/pallas_call | solution.py:52
  (66 shorter events, 24.1 us)
Async XLA Ops:
  1.9 9.4 %collective-permute-start = (bf16[112,1024]{1,0:T(8,128)(2,1)S(1)}, bf16[112,1024]{1,0:T(8,128)(2,1)S(1)}, u32[]{:S(2)}, u32[]{:S(2)}) collective-permute-start(bf16[112,1024]{1,0:T(8,128)(2,1)S(1)} %get-tuple-element.52), channel_id=1, source_target_pairs={{0,8},{8,0},{16,24},{24,16},{1,9},{9,1},{17,25},{25,17},{2,10},{10... | collective-permute-start | bytes 688136 | tf_op jit(solution)/shard_map/ppermute | solution.py:28
  4.9 12.0 %collective-permute-start.1 = (bf16[112,1024]{1,0:T(8,128)(2,1)S(1)}, bf16[112,1024]{1,0:T(8,128)(2,1)S(1)}, u32[]{:S(2)}, u32[]{:S(2)}) collective-permute-start(bf16[112,1024]{1,0:T(8,128)(2,1)S(1)} %get-tuple-element.53), channel_id=1, source_target_pairs={{0,16},{8,24},{16,0},{24,8},{1,17},{9,25},{17,1},{25,9},{2,18},{10... | collective-permute-start | bytes 688136 | tf_op jit(solution)/shard_map/ppermute | solution.py:28
  6.5 10.5 %collective-permute-start.2 = (bf16[112,1024]{1,0:T(8,128)(2,1)S(1)}, bf16[112,1024]{1,0:T(8,128)(2,1)S(1)}, u32[]{:S(2)}, u32[]{:S(2)}) collective-permute-start(bf16[112,1024]{1,0:T(8,128)(2,1)S(1)} %get-tuple-element.54), channel_id=1, source_target_pairs={{0,24},{8,16},{16,8},{24,0},{1,25},{9,17},{17,9},{25,1},{2,26},{10... | collective-permute-start | bytes 688136 | tf_op jit(solution)/shard_map/ppermute | solution.py:28
  18.3 6.3 %collective-permute-start.5 = (bf16[256,256]{1,0:T(8,128)(2,1)S(1)}, bf16[256,256]{1,0:T(8,128)(2,1)S(1)}, u32[]{:S(2)}, u32[]{:S(2)}) collective-permute-start(bf16[256,256]{1,0:T(8,128)(2,1)S(1)} %get-tuple-element.56.refs_0_.refs_3_), channel_id=1, source_target_pairs={{0,16},{8,24},{16,0},{24,8},{1,17},{9,25},{17,1},{25,9},{2,18},{10... | collective-permute-start | bytes 393224 | tf_op jit(solution)/shard_map/ppermute | solution.py:28
  19.9 6.3 %collective-permute-start.3 = (bf16[256,256]{1,0:T(8,128)(2,1)S(1)}, bf16[256,256]{1,0:T(8,128)(2,1)S(1)}, u32[]{:S(2)}, u32[]{:S(2)}) collective-permute-start(bf16[256,256]{1,0:T(8,128)(2,1)S(1)} %get-tuple-element.55.refs_0_), channel_id=1, source_target_pairs={{0,8},{8,0},{16,24},{24,16},{1,9},{9,1},{17,25},{25,17},{2,10},{10... | collective-permute-start | bytes 393224 | tf_op jit(solution)/shard_map/ppermute | solution.py:28
  20.4 7.7 %collective-permute-start.7 = (bf16[128,512]{1,0:T(8,128)(2,1)S(1)}, bf16[128,512]{1,0:T(8,128)(2,1)S(1)}, u32[]{:S(2)}, u32[]{:S(2)}) collective-permute-start(bf16[128,512]{1,0:T(8,128)(2,1)S(1)} %get-tuple-element.57.refs_0_), channel_id=1, source_target_pairs={{0,4},{1,5},{2,6},{3,7},{4,0},{5,1},{6,2},{7,3},{8,12},{9,13},{10,... | collective-permute-start | bytes 393224 | tf_op jit(solution)/shard_map/ppermute | solution.py:28
  23.0 6.3 %collective-permute-start.8 = (bf16[128,512]{1,0:T(8,128)(2,1)S(1)}, bf16[128,512]{1,0:T(8,128)(2,1)S(1)}, u32[]{:S(2)}, u32[]{:S(2)}) collective-permute-start(bf16[128,512]{1,0:T(8,128)(2,1)S(1)} %get-tuple-element.57.refs_0_), channel_id=1, source_target_pairs={{0,2},{1,3},{2,0},{3,1},{4,6},{5,7},{6,4},{7,5},{8,10},{9,11},{10,... | collective-permute-start | bytes 393224 | tf_op jit(solution)/shard_map/ppermute | solution.py:28
  24.6 9.7 %collective-permute-start.6 = (bf16[512,256]{1,0:T(8,128)(2,1)S(1)}, bf16[512,256]{1,0:T(8,128)(2,1)S(1)}, u32[]{:S(2)}, u32[]{:S(2)}) collective-permute-start(bf16[512,256]{1,0:T(8,128)(2,1)S(1)} %shard_map.112), channel_id=1, source_target_pairs={{0,8},{8,0},{16,24},{24,16},{1,9},{9,1},{17,25},{25,17},{2,10},{10... | collective-permute-start | bytes 786440 | tf_op jit(solution)/shard_map/ppermute | solution.py:28
  26.2 8.1 %collective-permute-start.4 = (bf16[512,256]{1,0:T(8,128)(2,1)S(1)}, bf16[512,256]{1,0:T(8,128)(2,1)S(1)}, u32[]{:S(2)}, u32[]{:S(2)}) collective-permute-start(bf16[512,256]{1,0:T(8,128)(2,1)S(1)} %shard_map.111), channel_id=1, source_target_pairs={{0,16},{8,24},{16,0},{24,8},{1,17},{9,25},{17,1},{25,9},{2,18},{10... | collective-permute-start | bytes 786440 | tf_op jit(solution)/shard_map/ppermute | solution.py:28
  26.8 6.5 %collective-permute-start.10 = (bf16[128,512]{1,0:T(8,128)(2,1)S(1)}, bf16[128,512]{1,0:T(8,128)(2,1)S(1)}, u32[]{:S(2)}, u32[]{:S(2)}) collective-permute-start(bf16[128,512]{1,0:T(8,128)(2,1)S(1)} %get-tuple-element.58), channel_id=1, source_target_pairs={{0,8},{8,0},{16,24},{24,16},{1,9},{9,1},{17,25},{25,17},{2,10},{10... | collective-permute-start | bytes 393224 | tf_op jit(solution)/shard_map/ppermute | solution.py:28
  28.1 5.9 %collective-permute-start.11 = (bf16[128,512]{1,0:T(8,128)(2,1)S(1)}, bf16[128,512]{1,0:T(8,128)(2,1)S(1)}, u32[]{:S(2)}, u32[]{:S(2)}) collective-permute-start(bf16[128,512]{1,0:T(8,128)(2,1)S(1)} %get-tuple-element.59), channel_id=1, source_target_pairs={{0,16},{8,24},{16,0},{24,8},{1,17},{9,25},{17,1},{25,9},{2,18},{10... | collective-permute-start | bytes 393224 | tf_op jit(solution)/shard_map/ppermute | solution.py:28
  34.4 7.8 %collective-permute-start.17 = (bf16[128,512]{1,0:T(8,128)(2,1)S(1)}, bf16[128,512]{1,0:T(8,128)(2,1)S(1)}, u32[]{:S(2)}, u32[]{:S(2)}) collective-permute-start(bf16[128,512]{1,0:T(8,128)(2,1)S(1)} %get-tuple-element.68), channel_id=1, source_target_pairs={{0,24},{8,16},{16,8},{24,0},{1,25},{9,17},{17,9},{25,1},{2,26},{10... | collective-permute-start | bytes 393224 | tf_op jit(solution)/shard_map/ppermute | solution.py:28
  39.8 8.1 %collective-permute-start.13 = (bf16[128,512]{1,0:T(8,128)(2,1)S(1)}, bf16[128,512]{1,0:T(8,128)(2,1)S(1)}, u32[]{:S(2)}, u32[]{:S(2)}) collective-permute-start(bf16[128,512]{1,0:T(8,128)(2,1)S(1)} %get-tuple-element.61), channel_id=1, source_target_pairs={{0,8},{8,0},{16,24},{24,16},{1,9},{9,1},{17,25},{25,17},{2,10},{10... | collective-permute-start | bytes 393224 | tf_op jit(solution)/shard_map/ppermute | solution.py:28
  41.0 6.9 %collective-permute-start.15 = (bf16[128,512]{1,0:T(8,128)(2,1)S(1)}, bf16[128,512]{1,0:T(8,128)(2,1)S(1)}, u32[]{:S(2)}, u32[]{:S(2)}) collective-permute-start(bf16[128,512]{1,0:T(8,128)(2,1)S(1)} %get-tuple-element.64), channel_id=1, source_target_pairs={{0,16},{8,24},{16,0},{24,8},{1,17},{9,25},{17,1},{25,9},{2,18},{10... | collective-permute-start | bytes 393224 | tf_op jit(solution)/shard_map/ppermute | solution.py:28
  48.8 9.2 %collective-permute-start.25 = (bf16[512,256]{1,0:T(8,128)(2,1)S(1)}, bf16[512,256]{1,0:T(8,128)(2,1)S(1)}, u32[]{:S(2)}, u32[]{:S(2)}) collective-permute-start(bf16[512,256]{1,0:T(8,128)(2,1)S(1)} %get-tuple-element.88), channel_id=1, source_target_pairs={{0,16},{8,24},{16,0},{24,8},{1,17},{9,25},{17,1},{25,9},{2,18},{10... | collective-permute-start | bytes 786440 | tf_op jit(solution)/shard_map/ppermute | solution.py:28
  49.7 9.2 %collective-permute-start.23 = (bf16[512,256]{1,0:T(8,128)(2,1)S(1)}, bf16[512,256]{1,0:T(8,128)(2,1)S(1)}, u32[]{:S(2)}, u32[]{:S(2)}) collective-permute-start(bf16[512,256]{1,0:T(8,128)(2,1)S(1)} %get-tuple-element.84), channel_id=1, source_target_pairs={{0,8},{8,0},{16,24},{24,16},{1,9},{9,1},{17,25},{25,17},{2,10},{10... | collective-permute-start | bytes 786440 | tf_op jit(solution)/shard_map/ppermute | solution.py:28
  50.9 9.3 %collective-permute-start.19 = (bf16[288,512]{1,0:T(8,128)(2,1)S(1)}, bf16[288,512]{1,0:T(8,128)(2,1)S(1)}, u32[]{:S(2)}, u32[]{:S(2)}) collective-permute-start(bf16[288,512]{1,0:T(8,128)(2,1)S(1)} %get-tuple-element.76), channel_id=1, source_target_pairs={{0,2},{1,3},{2,0},{3,1},{4,6},{5,7},{6,4},{7,5},{8,10},{9,11},{10,... | collective-permute-start | bytes 884744 | tf_op jit(solution)/shard_map/ppermute | solution.py:28
  52.8 9.5 %collective-permute-start.16 = (bf16[128,512]{1,0:T(8,128)(2,1)S(1)}, bf16[128,512]{1,0:T(8,128)(2,1)S(1)}, u32[]{:S(2)}, u32[]{:S(2)}) collective-permute-start(bf16[128,512]{1,0:T(8,128)(2,1)S(1)} %shard_map.119), channel_id=1, source_target_pairs={{0,8},{8,0},{16,24},{24,16},{1,9},{9,1},{17,25},{25,17},{2,10},{10... | collective-permute-start | bytes 393224 | tf_op jit(solution)/shard_map/ppermute | solution.py:28
  54.6 7.7 %collective-permute-start.14 = (bf16[128,512]{1,0:T(8,128)(2,1)S(1)}, bf16[128,512]{1,0:T(8,128)(2,1)S(1)}, u32[]{:S(2)}, u32[]{:S(2)}) collective-permute-start(bf16[128,512]{1,0:T(8,128)(2,1)S(1)} %shard_map.118), channel_id=1, source_target_pairs={{0,16},{8,24},{16,0},{24,8},{1,17},{9,25},{17,1},{25,9},{2,18},{10... | collective-permute-start | bytes 393224 | tf_op jit(solution)/shard_map/ppermute | solution.py:28
  60.2 9.7 %collective-permute-start.20 = (bf16[160,512]{1,0:T(8,128)(2,1)S(1)}, bf16[160,512]{1,0:T(8,128)(2,1)S(1)}, u32[]{:S(2)}, u32[]{:S(2)}) collective-permute-start(bf16[160,512]{1,0:T(8,128)(2,1)S(1)} %get-tuple-element.78.refs_6_), channel_id=1, source_target_pairs={{0,4},{1,5},{2,6},{3,7},{4,0},{5,1},{6,2},{7,3},{8,12},{9,13},{10,... | collective-permute-start | bytes 491528 | tf_op jit(solution)/shard_map/ppermute | solution.py:28
  67.1 6.1 %collective-permute-start.27 = (bf16[128,768]{1,0:T(8,128)(2,1)S(1)}, bf16[128,768]{1,0:T(8,128)(2,1)S(1)}, u32[]{:S(2)}, u32[]{:S(2)}) collective-permute-start(bf16[128,768]{1,0:T(8,128)(2,1)S(1)} %get-tuple-element.92), channel_id=1, source_target_pairs={{0,8},{8,0},{16,24},{24,16},{1,9},{9,1},{17,25},{25,17},{2,10},{10... | collective-permute-start | bytes 589832 | tf_op jit(solution)/shard_map/ppermute | solution.py:28
  70.0 6.5 %collective-permute-start.21 = (bf16[128,512]{1,0:T(8,128)(2,1)S(1)}, bf16[128,512]{1,0:T(8,128)(2,1)S(1)}, u32[]{:S(2)}, u32[]{:S(2)}) collective-permute-start(bf16[128,512]{1,0:T(8,128)(2,1)S(1)} %shard_map.125), channel_id=1, source_target_pairs={{0,8},{8,0},{16,24},{24,16},{1,9},{9,1},{17,25},{25,17},{2,10},{10... | collective-permute-start | bytes 393224 | tf_op jit(solution)/shard_map/ppermute | solution.py:28
  71.7 8.1 %collective-permute-start.30 = (bf16[128,768]{1,0:T(8,128)(2,1)S(1)}, bf16[128,768]{1,0:T(8,128)(2,1)S(1)}, u32[]{:S(2)}, u32[]{:S(2)}) collective-permute-start(bf16[128,768]{1,0:T(8,128)(2,1)S(1)} %shard_map.131), channel_id=1, source_target_pairs={{0,8},{8,0},{16,24},{24,16},{1,9},{9,1},{17,25},{25,17},{2,10},{10... | collective-permute-start | bytes 589832 | tf_op jit(solution)/shard_map/ppermute | solution.py:28
  73.2 7.1 %collective-permute-start.28 = (bf16[128,768]{1,0:T(8,128)(2,1)S(1)}, bf16[128,768]{1,0:T(8,128)(2,1)S(1)}, u32[]{:S(2)}, u32[]{:S(2)}) collective-permute-start(bf16[128,768]{1,0:T(8,128)(2,1)S(1)} %shard_map.130), channel_id=1, source_target_pairs={{0,16},{8,24},{16,0},{24,8},{1,17},{9,25},{17,1},{25,9},{2,18},{10... | collective-permute-start | bytes 589832 | tf_op jit(solution)/shard_map/ppermute | solution.py:28
  (9 other events, 50.2 us)

commit v5 on v4

--- a/solution.py
+++ b/solution.py
@@ -17,6 +17,8 @@
 CONV_COST = 600
 ATTEND_COST = 24
 BACK_COST = 48
+SPLIT_BACK = False
+PAD = 32
 PACK_LIMIT = 60
 F32 = jnp.float32
 BF16 = jnp.bfloat16
@@ -335,12 +337,15 @@
 
 
 def add_halves(mine, other, *outs):
-    total = mine[...].astype(F32) + other[...].astype(F32)
-    share = (total.shape[0] - TAPS) // len(outs)
+    height = mine.shape[0]
+    total = mine[...].astype(F32) + other[0:height, :].astype(F32)
+    share = (height - TAPS) // len(outs)
     for k, out in enumerate(outs):
         at = TAPS + k * share
         out[0:TAPS, :] = total[0:TAPS, :].astype(BF16)
-        out[TAPS:, :] = total[at : at + share, :].astype(BF16)
+        out[TAPS : TAPS + share, :] = total[at : at + share, :].astype(BF16)
+        if out.shape[0] > TAPS + share:
+            out[TAPS + share :, :] = jnp.zeros((out.shape[0] - TAPS - share, out.shape[1]), BF16)
 
 
 def fold(mine, other, stays, goes):
@@ -395,19 +400,40 @@
         ).astype(BF16)
     for k in range(groups):
         piece = result[block(me ^ k, local, local), :]
-        if groups == 4:
+        if len(outs) != groups:
             split_up(outs, k, local, slice(None), piece)
         else:
             outs[k][...] = piece
 
 
-def join_all(groups, scale, *refs):
+def scale_sums(groups, scale, *refs):
+    sums = refs[:-2]
+    weight_ref, tap_ref = refs[-2:]
+    me = lax.axis_index("fsdp")
+    channels = sums[0].shape[1]
+    for k in range(groups):
+        columns = block(me ^ k, channels, LANES)
+        if len(sums) == groups:
+            tap_ref[:, columns] = sums[k][0:KERNEL, :].astype(F32) * scale
+            weight_ref[:, columns] = sums[k][TAPS:, :].astype(F32) * scale
+    if len(sums) != groups:
+        ends = ((sums[0], sums[1], sums[2]), (sums[0], sums[3], sums[4]))
+        for k, i, source, at in places(*ends, TAPS):
+            at += TAPS if k == 0 and i else 0
+            columns = block(me ^ k, channels, LANES)
+            if i:
+                weight_ref[:, columns] = source[at : at + TAPS, :].astype(F32) * scale
+            else:
+                tap_ref[:, columns] = source[at : at + KERNEL, :].astype(F32) * scale
+
+
+def join_all(groups, several, *refs):
     count = 5 if groups == 4 else groups
     ahead = refs[:count]
-    sums = refs[count : -count - 9]
-    pieces = refs[-count - 9 : -9]
-    outs = refs[-9:-3]
-    weight_ref, tap_ref, sent = refs[-3:]
+    pieces = refs[count : count + several]
+    weight_ref, tap_ref = refs[count + several : -7]
+    outs = refs[-7:-1]
+    sent = refs[-1]
     me = lax.axis_index("fsdp")
     copies = []
 
@@ -418,10 +444,10 @@
 
     local, width = pieces[0].shape
     width //= 3
-    channels = sums[0].shape[1]
+    channels = ahead[0].shape[1]
 
     def found(arrays):
-        if groups != 4:
+        if len(arrays) == groups:
             return [(k, 0, local, arrays[k], 0) for k in range(groups)]
         share = local // 2
         ends = ((arrays[0], arrays[1], arrays[2]), (arrays[0], arrays[3], arrays[4]))
@@ -436,13 +462,6 @@
         for at in range(3):
             part = source.at[first : first + size, at * width : (at + 1) * width]
             store(part, outs[1 + at].at[0, start : start + size, columns])
-    for k in range(groups):
-        columns = block(me ^ k, channels, LANES)
-        i = min(k, len(sums) - 1)
-        first = sums[0].shape[0] if k > i else 0
-        last = first + sums[0].shape[0]
-        tap_ref[:, columns] = sums[i][first : first + KERNEL, :].astype(F32) * scale
-        weight_ref[:, columns] = sums[i][first + TAPS : last, :].astype(F32) * scale
     store(weight_ref, outs[4])
     store(tap_ref, outs[5])
     for copy in copies:
@@ -463,15 +482,6 @@
     (later_across,) = call(stack_parts, shape, later_across, beside, after=after)
     (later_beside,) = call(stack_parts, shape, later_beside, across, after=after)
     return [own, beside, swap(later_across, "fsdp", 2), across, swap(later_beside, "fsdp", 1)]
-
-
-def turn(sent):
-    if len(sent) != 4:
-        return exchange(sent)
-    shape = [((2 * sent[0].shape[0], sent[0].shape[1]), BF16)]
-    first = swap(stack(sent[1], sent[3]), "fsdp", 1)
-    second = swap(call(stack_parts, shape, sent[2], first)[0], "fsdp", 2)
-    return [sent[0], first, second]
 
 
 def gather_weight(mine, groups, count, after):
@@ -522,15 +532,11 @@
     return halves
 
 
-def add_up(halves, mask, pieces):
+def add_up(halves, mask, spare):
     mine, other = halves
-    share = (mine.shape[0] - TAPS) // pieces
-    return call(
-        add_halves,
-        [((TAPS + share, mine.shape[1]), BF16)] * pieces,
-        mine,
-        swap(other, "frame", mask),
-    )
+    height = TAPS + (mine.shape[0] - TAPS) // 2
+    shapes = [((height, mine.shape[1]), BF16), ((height + spare, mine.shape[1]), BF16)]
+    return call(add_halves, shapes, mine, swap(other, "frame", mask))
 
 
 def shards(queries, key_rows, value_rows, out_weight, conv_weight, grad_out):
@@ -641,10 +647,10 @@
     halves = weight_halves(whole, grads, tap_terms, groups, count, rows, ahead[1:4:2])
     masks = masks_of(count)
     for mask in masks[:-1]:
-        halves = add_up(halves, mask, 2)
+        halves = add_up(halves, mask, PAD if mask == masks[-2] and rows % 16 == 0 else 0)
     sent = call(
         functools.partial(attend_back, groups),
-        split(3 * width),
+        split(3 * width) if SPLIT_BACK else [((local, 3 * width), BF16)] * groups,
         held,
         weights,
         *above,
@@ -653,22 +659,23 @@
         after=[halves[1], *(ahead[2:5:2] if folded else ())],
     )
     pieces = exchange_split(sent)
-    sums = turn(add_up(halves, masks[-1], groups))
+    shapes = [((TAPS + rows, channels), BF16)] * groups
+    sums = list(call(add_halves, shapes, halves[0], swap(halves[1], "frame", masks[-1])))
+    sums[-1] = stack(sums[-1], after=pieces[2:3])
+    sums = exchange(sums)
+    shapes = [((rows, model), F32), ((KERNEL, model), F32)]
+    sums = call(functools.partial(scale_sums, groups, scale), shapes, *sums)
     return tuple(
         call(
-            functools.partial(join_all, groups, scale),
+            functools.partial(join_all, groups, len(pieces)),
             [((1, local, model), BF16)]
             + [((1, local, inner), BF16)] * 3
             + [((rows, model), F32), ((KERNEL, model), F32)],
             *ahead,
+            *pieces,
             *sums,
-            *pieces,
             stored=True,
-            scratch=[
-                pltpu.VMEM((rows, model), F32),
-                pltpu.VMEM((KERNEL, model), F32),
-                pltpu.SemaphoreType.DMA((8 * groups + 2,)),
-            ],
+            scratch=[pltpu.SemaphoreType.DMA((8 * groups + 2,))],
         )
     )
 

time: 83.4 us -> 81.6 us (0.978)
  waiting for transfers between devices: 28.7 us -> 27 us
    ppermute x31, waiting for transfers between devices: 28.7 us -> 27 us  [swap(): return lax.ppermute(cells, axis, [(i, i ^ mask) for i in range(count)])]
    pallas_call x24 -> x22, Pallas kernels: 17.4 us -> 17.4 us  [call(): pl.pallas_call(lambda *refs: body(*refs[:count], *refs[count + len(after)...]
  transfers between devices with their start and end apart: 31 -> 31, of which waited for: 18 -> 16; matrix products, arithmetic and copies ran while one was open for 0% -> 0% of each run, Pallas kernels for 15% -> 15%
where the time goes in v5:
time: 81.6 us; the launch traced here: 81.5 us
  starting transfers between devices  36.3 us (44%)
  waiting for transfers between devices  27 us (33%)
  Pallas kernels  17.4 us (21%)
  between operations  0.83 us (1%)
    ppermute x31, starting transfers between devices, swap(): return lax.ppermute(cells, axis, [(i, i ^ mask) for i in range(count)])  36.3 us
    ppermute x31, waiting for transfers between devices, swap(): return lax.ppermute(cells, axis, [(i, i ^ mask) for i in range(count)])  27 us
    pallas_call x22, Pallas kernels, call(): pl.pallas_call(lambda *refs: body(*refs[:count], *refs[count + len(after)...  17.4 us
  transfers between devices with their start and end apart: 31, of which 16 were waited for; matrix products, arithmetic and copies ran while one was open for 0% of the time, Pallas kernels for 15%

profile of v5, /device:TPU:0, one launch (start us, length us, event | category | flops | bytes accessed | tf_op | source)
XLA Modules:
  0.0 81.5 jit_solution(3552407767975317040)
XLA Ops:
  1.9 3.0 %collective-permute-start = (bf16[112,1024]{1,0:T(8,128)(2,1)S(1)}, bf16[112,1024]{1,0:T(8,128)(2,1)S(1)}, u32[]{:S(2)}, u32[]{:S(2)}) collective-permute-start(bf16[112,1024]{1,0:T(8,128)(2,1)S(1)} %get-tuple-element.53), channel_id=1, source_target_pairs={{0,8},{8,0},{16,24},{24,16},{1,9},{9,1},{17,25},{25,17},{2,10},{10... | collective-permute-start | bytes 688136 | tf_op jit(solution)/shard_map/ppermute | solution.py:30
  4.9 1.5 %collective-permute-start.1 = (bf16[112,1024]{1,0:T(8,128)(2,1)S(1)}, bf16[112,1024]{1,0:T(8,128)(2,1)S(1)}, u32[]{:S(2)}, u32[]{:S(2)}) collective-permute-start(bf16[112,1024]{1,0:T(8,128)(2,1)S(1)} %get-tuple-element.54), channel_id=1, source_target_pairs={{0,16},{8,24},{16,0},{24,8},{1,17},{9,25},{17,1},{25,9},{2,18},{10... | collective-permute-start | bytes 688136 | tf_op jit(solution)/shard_map/ppermute | solution.py:30
  6.5 4.9 %collective-permute-done.refs_1_ = bf16[112,1024]{1,0:T(8,128)(2,1)S(1)} collective-permute-done((bf16[112,1024]{1,0:T(8,128)(2,1)S(1)}, bf16[112,1024]{1,0:T(8,128)(2,1)S(1)}, u32[]{:S(2)}, u32[]{:S(2)}) %collective-permute-start) | collective-permute-done | bytes 229408 | tf_op jit(solution)/shard_map/ppermute | solution.py:30
  11.4 5.5 %collective-permute-done.1.refs_2_ = bf16[112,1024]{1,0:T(8,128)(2,1)S(1)} collective-permute-done((bf16[112,1024]{1,0:T(8,128)(2,1)S(1)}, bf16[112,1024]{1,0:T(8,128)(2,1)S(1)}, u32[]{:S(2)}, u32[]{:S(2)}) %collective-permute-start.1) | collective-permute-done | bytes 229408 | tf_op jit(solution)/shard_map/ppermute | solution.py:30
  16.9 1.4 %shard_map.110 = (bf16[512,768]{1,0:T(8,128)(2,1)S(1)}, bf16[256,256]{1,0:T(8,128)(2,1)S(1)}, bf16[256,256]{1,0:T(8,128)(2,1)S(1)}, bf16[128,512]{1,0:T(8,128)(2,1)S(1)}) custom-call(bf16[112,1024]{1,0:T(8,128)(2,1)S(1)} %get-tuple-element.52.refs_0_, bf16[112,1024]{1,0:T(8,128)(2,1)S(1)} %collective-permute-done.refs_1_, ...), custom_call_target="tpu_custom_call" | custom-call | flops 1610612736 | bytes 2097152 | tf_op jit(solution)/shard_map/pallas_call | solution.py:54
  18.3 1.6 %collective-permute-start.5 = (bf16[256,256]{1,0:T(8,128)(2,1)S(1)}, bf16[256,256]{1,0:T(8,128)(2,1)S(1)}, u32[]{:S(2)}, u32[]{:S(2)}) collective-permute-start(bf16[256,256]{1,0:T(8,128)(2,1)S(1)} %get-tuple-element.57.refs_0_.refs_3_), channel_id=1, source_target_pairs={{0,16},{8,24},{16,0},{24,8},{1,17},{9,25},{17,1},{25,9},{2,18},{10... | collective-permute-start | bytes 393224 | tf_op jit(solution)/shard_map/ppermute | solution.py:30
  20.4 2.6 %collective-permute-start.7 = (bf16[128,512]{1,0:T(8,128)(2,1)S(1)}, bf16[128,512]{1,0:T(8,128)(2,1)S(1)}, u32[]{:S(2)}, u32[]{:S(2)}) collective-permute-start(bf16[128,512]{1,0:T(8,128)(2,1)S(1)} %get-tuple-element.58.refs_0_), channel_id=1, source_target_pairs={{0,4},{1,5},{2,6},{3,7},{4,0},{5,1},{6,2},{7,3},{8,12},{9,13},{10,... | collective-permute-start | bytes 393224 | tf_op jit(solution)/shard_map/ppermute | solution.py:30
  23.0 1.6 %collective-permute-start.8 = (bf16[128,512]{1,0:T(8,128)(2,1)S(1)}, bf16[128,512]{1,0:T(8,128)(2,1)S(1)}, u32[]{:S(2)}, u32[]{:S(2)}) collective-permute-start(bf16[128,512]{1,0:T(8,128)(2,1)S(1)} %get-tuple-element.58.refs_0_), channel_id=1, source_target_pairs={{0,2},{1,3},{2,0},{3,1},{4,6},{5,7},{6,4},{7,5},{8,10},{9,11},{10,... | collective-permute-start | bytes 393224 | tf_op jit(solution)/shard_map/ppermute | solution.py:30
  24.6 1.6 %collective-permute-start.6 = (bf16[512,256]{1,0:T(8,128)(2,1)S(1)}, bf16[512,256]{1,0:T(8,128)(2,1)S(1)}, u32[]{:S(2)}, u32[]{:S(2)}) collective-permute-start(bf16[512,256]{1,0:T(8,128)(2,1)S(1)} %shard_map.112), channel_id=1, source_target_pairs={{0,8},{8,0},{16,24},{24,16},{1,9},{9,1},{17,25},{25,17},{2,10},{10... | collective-permute-start | bytes 786440 | tf_op jit(solution)/shard_map/ppermute | solution.py:30
  29.9 3.4 %collective-permute-done.10.refs_6_.refs_1_ = bf16[128,512]{1,0:T(8,128)(2,1)S(1)} collective-permute-done((bf16[128,512]{1,0:T(8,128)(2,1)S(1)}, bf16[128,512]{1,0:T(8,128)(2,1)S(1)}, u32[]{:S(2)}, u32[]{:S(2)}) %collective-permute-start.10) | collective-permute-done | bytes 131104 | tf_op jit(solution)/shard_map/ppermute | solution.py:30
  34.4 1.8 %collective-permute-start.17 = (bf16[128,512]{1,0:T(8,128)(2,1)S(1)}, bf16[128,512]{1,0:T(8,128)(2,1)S(1)}, u32[]{:S(2)}, u32[]{:S(2)}) collective-permute-start(bf16[128,512]{1,0:T(8,128)(2,1)S(1)} %get-tuple-element.68), channel_id=1, source_target_pairs={{0,24},{8,16},{16,8},{24,0},{1,25},{9,17},{17,9},{25,1},{2,26},{10... | collective-permute-start | bytes 393224 | tf_op jit(solution)/shard_map/ppermute | solution.py:30
  36.4 3.4 %shard_map.116 = (bf16[512,1024]{1,0:T(8,128)(2,1)S(1)}, bf16[512,512]{1,0:T(8,128)(2,1)S(1)}, f32[512,512]{1,0:T(8,128)S(1)}, bf16[128,512]{1,0:T(8,128)(2,1)S(...) custom-call(bf16[256,256]{1,0:T(8,128)(2,1)S(1)} %get-tuple-element., ...), custom_call_target="tpu_custom_call" | custom-call | flops 4875878400 | bytes 5369856 | tf_op jit(solution)/shard_map/pallas_call | solution.py:54
  42.2 5.7 %shard_map.120 = (bf16[512,512]{1,0:T(8,128)(2,1)S(1)}, f32[32,512]{1,0:T(8,128)S(1)}, bf16[512,256]{1,0:T(8,128)(2,1)S(1)}, bf16[512,256]{1,0:T(8,128)(2,1)S(1)...) custom-call(bf16[128,512]{1,0:T(8,128)(2,1)S(1)} %get-tuple-element.67.refs_0_, ...), custom_call_target="tpu_custom_call" | custom-call | flops 7313817600 | bytes 4911104 | tf_op jit(solution)/shard_map/pallas_call | solution.py:54
  52.8 1.8 %collective-permute-start.16 = (bf16[128,512]{1,0:T(8,128)(2,1)S(1)}, bf16[128,512]{1,0:T(8,128)(2,1)S(1)}, u32[]{:S(2)}, u32[]{:S(2)}) collective-permute-start(bf16[128,512]{1,0:T(8,128)(2,1)S(1)} %shard_map.119), channel_id=1, source_target_pairs={{0,8},{8,0},{16,24},{24,16},{1,9},{9,1},{17,25},{25,17},{2,10},{10... | collective-permute-start | bytes 393224 | tf_op jit(solution)/shard_map/ppermute | solution.py:30
  54.8 3.1 %collective-permute-done.20.refs_1_ = bf16[512,256]{1,0:T(8,128)(2,1)S(1)} collective-permute-done((bf16[512,256]{1,0:T(8,128)(2,1)S(1)}, bf16[512,256]{1,0:T(8,128)(2,1)S(1)}, u32[]{:S(2)}, u32[]{:S(2)}) %collective-permute-start.20) | collective-permute-done | bytes 262176 | tf_op jit(solution)/shard_map/ppermute | solution.py:30
  60.2 2.1 %collective-permute-start.27 = (bf16[192,512]{1,0:T(8,128)(2,1)S(1)}, bf16[192,512]{1,0:T(8,128)(2,1)S(1)}, u32[]{:S(2)}, u32[]{:S(2)}) collective-permute-start(bf16[192,512]{1,0:T(8,128)(2,1)S(1)} %get-tuple-element.86.refs_6_), channel_id=1, source_target_pairs={{0,4},{1,5},{2,6},{3,7},{4,0},{5,1},{6,2},{7,3},{8,12},{9,13},{10,... | collective-permute-start | bytes 589832 | tf_op jit(solution)/shard_map/ppermute | solution.py:30
  62.3 1.4 %collective-permute-done.21.refs_5_ = bf16[256,256]{1,0:T(8,128)(2,1)S(1)} collective-permute-done((bf16[256,256]{1,0:T(8,128)(2,1)S(1)}, bf16[256,256]{1,0:T(8,128)(2,1)S(1)}, u32[]{:S(2)}, u32[]{:S(2)}) %collective-permute-start.21) | collective-permute-done | bytes 131104 | tf_op jit(solution)/shard_map/ppermute | solution.py:30
  63.9 1.9 %shard_map.126 = (bf16[128,768]{1,0:T(8,128)(2,1)S(1)}, bf16[128,768]{1,0:T(8,128)(2,1)S(1)}, bf16[128,768]{1,0:T(8,128)(2,1)S(1)}, bf16[128,768]{1,0:T(8,128)(2,1)S(1)}) custom-call(bf16[512,768]{1,0:T(8,128)(2,1)S(1)} %get-tuple-element.64.refs_0_, f32[2,512,512]{2,1,0:T(8,128)S(1)} %shard_map.117.refs_2_.refs_1_, ...), custom_call_target="tpu_custom_call" | custom-call | flops 3221225472 | bytes 4194304 | tf_op jit(solution)/shard_map/pallas_call | solution.py:54
  68.0 1.4 %collective-permute-start.26 = (bf16[128,768]{1,0:T(8,128)(2,1)S(1)}, bf16[128,768]{1,0:T(8,128)(2,1)S(1)}, u32[]{:S(2)}, u32[]{:S(2)}) collective-permute-start(bf16[128,768]{1,0:T(8,128)(2,1)S(1)} %get-tuple-element.90), channel_id=1, source_target_pairs={{0,24},{8,16},{16,8},{24,0},{1,25},{9,17},{17,9},{25,1},{2,26},{10... | collective-permute-start | bytes 589832 | tf_op jit(solution)/shard_map/ppermute | solution.py:30
  69.4 2.0 %collective-permute-done.27.refs_1_ = bf16[192,512]{1,0:T(8,128)(2,1)S(1)} collective-permute-done((bf16[192,512]{1,0:T(8,128)(2,1)S(1)}, bf16[192,512]{1,0:T(8,128)(2,1)S(1)}, u32[]{:S(2)}, u32[]{:S(2)}) %collective-permute-start.27) | collective-permute-done | bytes 196640 | tf_op jit(solution)/shard_map/ppermute | solution.py:30
  71.4 1.4 %collective-permute-done.25.refs_1_.refs_7_ = bf16[128,768]{1,0:T(8,128)(2,1)S(1)} collective-permute-done((bf16[128,768]{1,0:T(8,128)(2,1)S(1)}, bf16[128,768]{1,0:T(8,128)(2,1)S(1)}, u32[]{:S(2)}, u32[]{:S(2)}) %collective-permute-start.25) | collective-permute-done | bytes 196640 | tf_op jit(solution)/shard_map/ppermute | solution.py:30
  72.8 1.8 %collective-permute-start.30 = (bf16[64,512]{1,0:T(8,128)(2,1)S(1)}, bf16[64,512]{1,0:T(8,128)(2,1)S(1)}, u32[]{:S(2)}, u32[]{:S(2)}) collective-permute-start(bf16[64,512]{1,0:T(8,128)(2,1)S(1)} %shard_map.128), channel_id=1, source_target_pairs={{0,24},{8,16},{16,8},{24,0},{1,25},{9,17},{17,9},{25,1},{2,26},{10... | collective-permute-start | bytes 196616 | tf_op jit(solution)/shard_map/ppermute | solution.py:30
  76.3 2.9 %collective-permute-done.30.refs_3_ = bf16[64,512]{1,0:T(8,128)(2,1)S(1)} collective-permute-done((bf16[64,512]{1,0:T(8,128)(2,1)S(1)}, bf16[64,512]{1,0:T(8,128)(2,1)S(1)}, u32[]{:S(2)}, u32[]{:S(2)}) %collective-permute-start.30) | collective-permute-done | bytes 65568 | tf_op jit(solution)/shard_map/ppermute | solution.py:30
  80.0 1.5 %shard_map.130 = (bf16[1,128,2048]{2,1,0:T(8,128)(2,1)}, bf16[1,128,1024]{2,1,0:T(8,128)(2,1)}, bf16[1,128,1024]{2,1,0:T(8,128)(2,1)}, bf16[1,128,1024]{2,1,0:T(...) custom-call(bf16[128,512]{1,0:T(8,128)(2,1)S(1)} %get-tuple-element.61.refs_0_, ...), custom_call_target="tpu_custom_call" | custom-call | bytes 3784704 | tf_op jit(solution)/shard_map/pallas_call | solution.py:54
  (64 shorter events, 21.5 us)
Async XLA Ops:
  1.9 9.4 %collective-permute-start = (bf16[112,1024]{1,0:T(8,128)(2,1)S(1)}, bf16[112,1024]{1,0:T(8,128)(2,1)S(1)}, u32[]{:S(2)}, u32[]{:S(2)}) collective-permute-start(bf16[112,1024]{1,0:T(8,128)(2,1)S(1)} %get-tuple-element.53), channel_id=1, source_target_pairs={{0,8},{8,0},{16,24},{24,16},{1,9},{9,1},{17,25},{25,17},{2,10},{10... | collective-permute-start | bytes 688136 | tf_op jit(solution)/shard_map/ppermute | solution.py:30
  4.9 12.0 %collective-permute-start.1 = (bf16[112,1024]{1,0:T(8,128)(2,1)S(1)}, bf16[112,1024]{1,0:T(8,128)(2,1)S(1)}, u32[]{:S(2)}, u32[]{:S(2)}) collective-permute-start(bf16[112,1024]{1,0:T(8,128)(2,1)S(1)} %get-tuple-element.54), channel_id=1, source_target_pairs={{0,16},{8,24},{16,0},{24,8},{1,17},{9,25},{17,1},{25,9},{2,18},{10... | collective-permute-start | bytes 688136 | tf_op jit(solution)/shard_map/ppermute | solution.py:30
  6.5 10.5 %collective-permute-start.2 = (bf16[112,1024]{1,0:T(8,128)(2,1)S(1)}, bf16[112,1024]{1,0:T(8,128)(2,1)S(1)}, u32[]{:S(2)}, u32[]{:S(2)}) collective-permute-start(bf16[112,1024]{1,0:T(8,128)(2,1)S(1)} %get-tuple-element.55), channel_id=1, source_target_pairs={{0,24},{8,16},{16,8},{24,0},{1,25},{9,17},{17,9},{25,1},{2,26},{10... | collective-permute-start | bytes 688136 | tf_op jit(solution)/shard_map/ppermute | solution.py:30
  18.3 6.3 %collective-permute-start.5 = (bf16[256,256]{1,0:T(8,128)(2,1)S(1)}, bf16[256,256]{1,0:T(8,128)(2,1)S(1)}, u32[]{:S(2)}, u32[]{:S(2)}) collective-permute-start(bf16[256,256]{1,0:T(8,128)(2,1)S(1)} %get-tuple-element.57.refs_0_.refs_3_), channel_id=1, source_target_pairs={{0,16},{8,24},{16,0},{24,8},{1,17},{9,25},{17,1},{25,9},{2,18},{10... | collective-permute-start | bytes 393224 | tf_op jit(solution)/shard_map/ppermute | solution.py:30
  19.9 6.3 %collective-permute-start.3 = (bf16[256,256]{1,0:T(8,128)(2,1)S(1)}, bf16[256,256]{1,0:T(8,128)(2,1)S(1)}, u32[]{:S(2)}, u32[]{:S(2)}) collective-permute-start(bf16[256,256]{1,0:T(8,128)(2,1)S(1)} %get-tuple-element.56.refs_0_), channel_id=1, source_target_pairs={{0,8},{8,0},{16,24},{24,16},{1,9},{9,1},{17,25},{25,17},{2,10},{10... | collective-permute-start | bytes 393224 | tf_op jit(solution)/shard_map/ppermute | solution.py:30
  20.4 7.7 %collective-permute-start.7 = (bf16[128,512]{1,0:T(8,128)(2,1)S(1)}, bf16[128,512]{1,0:T(8,128)(2,1)S(1)}, u32[]{:S(2)}, u32[]{:S(2)}) collective-permute-start(bf16[128,512]{1,0:T(8,128)(2,1)S(1)} %get-tuple-element.58.refs_0_), channel_id=1, source_target_pairs={{0,4},{1,5},{2,6},{3,7},{4,0},{5,1},{6,2},{7,3},{8,12},{9,13},{10,... | collective-permute-start | bytes 393224 | tf_op jit(solution)/shard_map/ppermute | solution.py:30
  23.0 6.3 %collective-permute-start.8 = (bf16[128,512]{1,0:T(8,128)(2,1)S(1)}, bf16[128,512]{1,0:T(8,128)(2,1)S(1)}, u32[]{:S(2)}, u32[]{:S(2)}) collective-permute-start(bf16[128,512]{1,0:T(8,128)(2,1)S(1)} %get-tuple-element.58.refs_0_), channel_id=1, source_target_pairs={{0,2},{1,3},{2,0},{3,1},{4,6},{5,7},{6,4},{7,5},{8,10},{9,11},{10,... | collective-permute-start | bytes 393224 | tf_op jit(solution)/shard_map/ppermute | solution.py:30
  24.6 9.7 %collective-permute-start.6 = (bf16[512,256]{1,0:T(8,128)(2,1)S(1)}, bf16[512,256]{1,0:T(8,128)(2,1)S(1)}, u32[]{:S(2)}, u32[]{:S(2)}) collective-permute-start(bf16[512,256]{1,0:T(8,128)(2,1)S(1)} %shard_map.112), channel_id=1, source_target_pairs={{0,8},{8,0},{16,24},{24,16},{1,9},{9,1},{17,25},{25,17},{2,10},{10... | collective-permute-start | bytes 786440 | tf_op jit(solution)/shard_map/ppermute | solution.py:30
  26.2 8.1 %collective-permute-start.4 = (bf16[512,256]{1,0:T(8,128)(2,1)S(1)}, bf16[512,256]{1,0:T(8,128)(2,1)S(1)}, u32[]{:S(2)}, u32[]{:S(2)}) collective-permute-start(bf16[512,256]{1,0:T(8,128)(2,1)S(1)} %shard_map.111), channel_id=1, source_target_pairs={{0,16},{8,24},{16,0},{24,8},{1,17},{9,25},{17,1},{25,9},{2,18},{10... | collective-permute-start | bytes 786440 | tf_op jit(solution)/shard_map/ppermute | solution.py:30
  26.8 6.5 %collective-permute-start.10 = (bf16[128,512]{1,0:T(8,128)(2,1)S(1)}, bf16[128,512]{1,0:T(8,128)(2,1)S(1)}, u32[]{:S(2)}, u32[]{:S(2)}) collective-permute-start(bf16[128,512]{1,0:T(8,128)(2,1)S(1)} %get-tuple-element.59), channel_id=1, source_target_pairs={{0,8},{8,0},{16,24},{24,16},{1,9},{9,1},{17,25},{25,17},{2,10},{10... | collective-permute-start | bytes 393224 | tf_op jit(solution)/shard_map/ppermute | solution.py:30
  28.1 5.9 %collective-permute-start.11 = (bf16[128,512]{1,0:T(8,128)(2,1)S(1)}, bf16[128,512]{1,0:T(8,128)(2,1)S(1)}, u32[]{:S(2)}, u32[]{:S(2)}) collective-permute-start(bf16[128,512]{1,0:T(8,128)(2,1)S(1)} %get-tuple-element.60), channel_id=1, source_target_pairs={{0,16},{8,24},{16,0},{24,8},{1,17},{9,25},{17,1},{25,9},{2,18},{10... | collective-permute-start | bytes 393224 | tf_op jit(solution)/shard_map/ppermute | solution.py:30
  34.4 7.8 %collective-permute-start.17 = (bf16[128,512]{1,0:T(8,128)(2,1)S(1)}, bf16[128,512]{1,0:T(8,128)(2,1)S(1)}, u32[]{:S(2)}, u32[]{:S(2)}) collective-permute-start(bf16[128,512]{1,0:T(8,128)(2,1)S(1)} %get-tuple-element.68), channel_id=1, source_target_pairs={{0,24},{8,16},{16,8},{24,0},{1,25},{9,17},{17,9},{25,1},{2,26},{10... | collective-permute-start | bytes 393224 | tf_op jit(solution)/shard_map/ppermute | solution.py:30
  39.8 8.1 %collective-permute-start.13 = (bf16[128,512]{1,0:T(8,128)(2,1)S(1)}, bf16[128,512]{1,0:T(8,128)(2,1)S(1)}, u32[]{:S(2)}, u32[]{:S(2)}) collective-permute-start(bf16[128,512]{1,0:T(8,128)(2,1)S(1)} %get-tuple-element.62), channel_id=1, source_target_pairs={{0,8},{8,0},{16,24},{24,16},{1,9},{9,1},{17,25},{25,17},{2,10},{10... | collective-permute-start | bytes 393224 | tf_op jit(solution)/shard_map/ppermute | solution.py:30
  41.0 6.9 %collective-permute-start.15 = (bf16[128,512]{1,0:T(8,128)(2,1)S(1)}, bf16[128,512]{1,0:T(8,128)(2,1)S(1)}, u32[]{:S(2)}, u32[]{:S(2)}) collective-permute-start(bf16[128,512]{1,0:T(8,128)(2,1)S(1)} %get-tuple-element.65), channel_id=1, source_target_pairs={{0,16},{8,24},{16,0},{24,8},{1,17},{9,25},{17,1},{25,9},{2,18},{10... | collective-permute-start | bytes 393224 | tf_op jit(solution)/shard_map/ppermute | solution.py:30
  48.8 9.2 %collective-permute-start.20 = (bf16[512,256]{1,0:T(8,128)(2,1)S(1)}, bf16[512,256]{1,0:T(8,128)(2,1)S(1)}, u32[]{:S(2)}, u32[]{:S(2)}) collective-permute-start(bf16[512,256]{1,0:T(8,128)(2,1)S(1)} %get-tuple-element.76), channel_id=1, source_target_pairs={{0,16},{8,24},{16,0},{24,8},{1,17},{9,25},{17,1},{25,9},{2,18},{10... | collective-permute-start | bytes 786440 | tf_op jit(solution)/shard_map/ppermute | solution.py:30
  49.7 9.2 %collective-permute-start.18 = (bf16[512,256]{1,0:T(8,128)(2,1)S(1)}, bf16[512,256]{1,0:T(8,128)(2,1)S(1)}, u32[]{:S(2)}, u32[]{:S(2)}) collective-permute-start(bf16[512,256]{1,0:T(8,128)(2,1)S(1)} %get-tuple-element.72), channel_id=1, source_target_pairs={{0,8},{8,0},{16,24},{24,16},{1,9},{9,1},{17,25},{25,17},{2,10},{10... | collective-permute-start | bytes 786440 | tf_op jit(solution)/shard_map/ppermute | solution.py:30
  50.9 9.3 %collective-permute-start.23 = (bf16[288,512]{1,0:T(8,128)(2,1)S(1)}, bf16[288,512]{1,0:T(8,128)(2,1)S(1)}, u32[]{:S(2)}, u32[]{:S(2)}) collective-permute-start(bf16[288,512]{1,0:T(8,128)(2,1)S(1)} %get-tuple-element.85), channel_id=1, source_target_pairs={{0,2},{1,3},{2,0},{3,1},{4,6},{5,7},{6,4},{7,5},{8,10},{9,11},{10,... | collective-permute-start | bytes 884744 | tf_op jit(solution)/shard_map/ppermute | solution.py:30
  52.8 9.5 %collective-permute-start.16 = (bf16[128,512]{1,0:T(8,128)(2,1)S(1)}, bf16[128,512]{1,0:T(8,128)(2,1)S(1)}, u32[]{:S(2)}, u32[]{:S(2)}) collective-permute-start(bf16[128,512]{1,0:T(8,128)(2,1)S(1)} %shard_map.119), channel_id=1, source_target_pairs={{0,8},{8,0},{16,24},{24,16},{1,9},{9,1},{17,25},{25,17},{2,10},{10... | collective-permute-start | bytes 393224 | tf_op jit(solution)/shard_map/ppermute | solution.py:30
  54.6 7.7 %collective-permute-start.14 = (bf16[128,512]{1,0:T(8,128)(2,1)S(1)}, bf16[128,512]{1,0:T(8,128)(2,1)S(1)}, u32[]{:S(2)}, u32[]{:S(2)}) collective-permute-start(bf16[128,512]{1,0:T(8,128)(2,1)S(1)} %shard_map.118), channel_id=1, source_target_pairs={{0,16},{8,24},{16,0},{24,8},{1,17},{9,25},{17,1},{25,9},{2,18},{10... | collective-permute-start | bytes 393224 | tf_op jit(solution)/shard_map/ppermute | solution.py:30
  60.2 11.1 %collective-permute-start.27 = (bf16[192,512]{1,0:T(8,128)(2,1)S(1)}, bf16[192,512]{1,0:T(8,128)(2,1)S(1)}, u32[]{:S(2)}, u32[]{:S(2)}) collective-permute-start(bf16[192,512]{1,0:T(8,128)(2,1)S(1)} %get-tuple-element.86.refs_6_), channel_id=1, source_target_pairs={{0,4},{1,5},{2,6},{3,7},{4,0},{5,1},{6,2},{7,3},{8,12},{9,13},{10,... | collective-permute-start | bytes 589832 | tf_op jit(solution)/shard_map/ppermute | solution.py:30
  65.8 7.0 %collective-permute-start.25 = (bf16[128,768]{1,0:T(8,128)(2,1)S(1)}, bf16[128,768]{1,0:T(8,128)(2,1)S(1)}, u32[]{:S(2)}, u32[]{:S(2)}) collective-permute-start(bf16[128,768]{1,0:T(8,128)(2,1)S(1)} %get-tuple-element.89), channel_id=1, source_target_pairs={{0,16},{8,24},{16,0},{24,8},{1,17},{9,25},{17,1},{25,9},{2,18},{10... | collective-permute-start | bytes 589832 | tf_op jit(solution)/shard_map/ppermute | solution.py:30
  67.1 12.9 %collective-permute-start.24 = (bf16[128,768]{1,0:T(8,128)(2,1)S(1)}, bf16[128,768]{1,0:T(8,128)(2,1)S(1)}, u32[]{:S(2)}, u32[]{:S(2)}) collective-permute-start(bf16[128,768]{1,0:T(8,128)(2,1)S(1)} %get-tuple-element.88), channel_id=1, source_target_pairs={{0,8},{8,0},{16,24},{24,16},{1,9},{9,1},{17,25},{25,17},{2,10},{10... | collective-permute-start | bytes 589832 | tf_op jit(solution)/shard_map/ppermute | solution.py:30
  68.0 11.9 %collective-permute-start.26 = (bf16[128,768]{1,0:T(8,128)(2,1)S(1)}, bf16[128,768]{1,0:T(8,128)(2,1)S(1)}, u32[]{:S(2)}, u32[]{:S(2)}) collective-permute-start(bf16[128,768]{1,0:T(8,128)(2,1)S(1)} %get-tuple-element.90), channel_id=1, source_target_pairs={{0,24},{8,16},{16,8},{24,0},{1,25},{9,17},{17,9},{25,1},{2,26},{10... | collective-permute-start | bytes 589832 | tf_op jit(solution)/shard_map/ppermute | solution.py:30
  72.8 6.4 %collective-permute-start.30 = (bf16[64,512]{1,0:T(8,128)(2,1)S(1)}, bf16[64,512]{1,0:T(8,128)(2,1)S(1)}, u32[]{:S(2)}, u32[]{:S(2)}) collective-permute-start(bf16[64,512]{1,0:T(8,128)(2,1)S(1)} %shard_map.128), channel_id=1, source_target_pairs={{0,24},{8,16},{16,8},{24,0},{1,25},{9,17},{17,9},{25,1},{2,26},{10... | collective-permute-start | bytes 196616 | tf_op jit(solution)/shard_map/ppermute | solution.py:30
  (9 other events, 48.6 us)

commit v6 on v5

--- a/solution.py
+++ b/solution.py
@@ -12,13 +12,14 @@
 KERNEL = 31
 LANES = 128
 TILE = 64
+BACK_TILE = 32
 TAPS = 32
 FOLD = 32
 CONV_COST = 600
 ATTEND_COST = 24
 BACK_COST = 48
 SPLIT_BACK = False
-PAD = 32
+PAD = 48
 PACK_LIMIT = 60
 F32 = jnp.float32
 BF16 = jnp.bfloat16
@@ -45,7 +46,7 @@
     return order
 
 
-def call(body, outs, *operands, scratch=(), flops=0, near=True, stored=False, after=(), limit=40, pinned=False):
+def call(body, outs, *operands, scratch=(), flops=0, near=True, stored=0, after=(), limit=40, pinned=False):
     vmem = pl.BlockSpec(memory_space=pltpu.VMEM)
     hbm = pl.BlockSpec(memory_space=pltpu.HBM)
     count = len(operands)
@@ -55,7 +56,7 @@
         lambda *refs: body(*refs[:count], *refs[count + len(after) :]),
         out_shape=[(pltpu.VMEM if pinned else jax.ShapeDtypeStruct)(s, t) for s, t in outs],
         in_specs=[vmem if near else hbm] * count + [pl.BlockSpec(memory_space=pl.ANY)] * len(after),
-        out_specs=[hbm if stored else vmem] * len(outs),
+        out_specs=[hbm if i < stored else vmem for i in range(len(outs))],
         scratch_shapes=list(scratch),
         cost_estimate=pl.CostEstimate(flops=flops, bytes_accessed=moved, transcendentals=0),
         compiler_params=pltpu.CompilerParams(vmem_limit_bytes=limit * 1024 * 1024),
@@ -286,19 +287,19 @@
         taps[0:KERNEL, :] = taps_ref[:, block(me * (channels // LANES) + c, LANES, LANES)].astype(F32)
         padded[16 : frames + 16, :] = (above[...] * slope_ref[:, columns]).astype(BF16).astype(F32)
         sums[...] = jnp.zeros(sums.shape, F32)
-        for start in range(0, frames, TILE):
-            total = above[start : start + TILE, :]
-            own = projected_ref[start : start + TILE, columns].astype(F32)
-            for indices, rows in shifted(padded, start, TILE):
+        for start in range(0, frames, BACK_TILE):
+            total = above[start : start + BACK_TILE, :]
+            own = projected_ref[start : start + BACK_TILE, columns].astype(F32)
+            for indices, rows in shifted(padded, start, BACK_TILE):
                 for at, j in enumerate(indices):
-                    part = rows[8 * at : 8 * at + TILE, :]
+                    part = rows[8 * at : 8 * at + BACK_TILE, :]
                     tap = KERNEL - 1 - j
                     total += taps[tap : tap + 1, :] * part
                     terms = own * part
                     sums[8 * tap : 8 * tap + 8, :] += tree_sum(
-                        [terms[8 * i : 8 * i + 8, :] for i in range(TILE // 8)]
+                        [terms[8 * i : 8 * i + 8, :] for i in range(BACK_TILE // 8)]
                     )
-            grad_ref[start : start + TILE, columns] = total.astype(BF16)
+            grad_ref[start : start + BACK_TILE, columns] = total.astype(BF16)
         tap_ref[:, columns] = jnp.sum(sums[...].reshape(TAPS, 8, LANES), axis=1)
         return carry
 
@@ -323,11 +324,12 @@
     depth = attention.shape[1] // groups
     half = len(order) // 2
     for k in range(groups):
-        terms[...] = product(attention[:, k * depth : (k + 1) * depth], grads[...], 0, 0)
+        cells = product(attention[:, k * depth : (k + 1) * depth], grads[...], 0, 0)
+        terms[...] = cells.astype(BF16)
         for i, n in enumerate(order):
             there = pl.ds(pl.multiple_of((me ^ n) * rows, rows), rows)
             at = TAPS + ((i % half) * groups + k) * rows
-            outs[i // half][at : at + rows, :] = terms[there, :].astype(BF16)
+            outs[i // half][at : at + rows, :] = terms[there, :]
     for out in outs:
         out[0:TAPS, :] = tap_ref[...].astype(BF16)
 
@@ -427,12 +429,34 @@
                 tap_ref[:, columns] = source[at : at + KERNEL, :].astype(F32) * scale
 
 
+def join_ahead(groups, *refs):
+    ahead = refs[:-3]
+    out, written, sent = refs[-3:]
+    me = lax.axis_index("fsdp")
+    local, channels = ahead[0].shape
+    copies = []
+    for i, (k, start, size, source, first) in enumerate(found(groups, local, ahead)):
+        there = out.at[0, start : start + size, block(me ^ k, channels, LANES)]
+        copies.append(pltpu.make_async_copy(source.at[first : first + size], there, sent.at[i]))
+        copies[-1].start()
+    for copy in copies:
+        copy.wait()
+    written[...] = jnp.zeros(written.shape, F32)
+
+
+def found(groups, local, arrays):
+    if len(arrays) == groups:
+        return [(k, 0, local, arrays[k], 0) for k in range(groups)]
+    share = local // 2
+    ends = ((arrays[0], arrays[1], arrays[2]), (arrays[0], arrays[3], arrays[4]))
+    parts = [(k, i * share, share, x, at) for k, i, x, at in places(*ends, share) if k]
+    return parts + [(0, 0, local, arrays[0], 0)]
+
+
 def join_all(groups, several, *refs):
-    count = 5 if groups == 4 else groups
-    ahead = refs[:count]
-    pieces = refs[count : count + several]
-    weight_ref, tap_ref = refs[count + several : -7]
-    outs = refs[-7:-1]
+    pieces = refs[:several]
+    weight_ref, tap_ref = refs[several : several + 2]
+    outs = refs[several + 2 : -1]
     sent = refs[-1]
     me = lax.axis_index("fsdp")
     copies = []
@@ -444,26 +468,13 @@
 
     local, width = pieces[0].shape
     width //= 3
-    channels = ahead[0].shape[1]
-
-    def found(arrays):
-        if len(arrays) == groups:
-            return [(k, 0, local, arrays[k], 0) for k in range(groups)]
-        share = local // 2
-        ends = ((arrays[0], arrays[1], arrays[2]), (arrays[0], arrays[3], arrays[4]))
-        parts = [(k, i * share, share, x, at) for k, i, x, at in places(*ends, share) if k]
-        return parts + [(0, 0, local, arrays[0], 0)]
-
-    for k, start, size, source, first in found(ahead):
-        there = outs[0].at[0, start : start + size, block(me ^ k, channels, LANES)]
-        store(source.at[first : first + size], there)
-    for k, start, size, source, first in found(pieces):
+    for k, start, size, source, first in found(groups, local, pieces):
         columns = block(me ^ k, width, LANES)
         for at in range(3):
             part = source.at[first : first + size, at * width : (at + 1) * width]
-            store(part, outs[1 + at].at[0, start : start + size, columns])
-    store(weight_ref, outs[4])
-    store(tap_ref, outs[5])
+            store(part, outs[at].at[0, start : start + size, columns])
+    store(weight_ref, outs[3])
+    store(tap_ref, outs[4])
     for copy in copies:
         copy.wait()
 
@@ -519,7 +530,7 @@
             attention,
             grads,
             tap_terms,
-            scratch=[pltpu.VMEM((depth, channels), F32)],
+            scratch=[pltpu.VMEM((depth, channels), BF16)],
             after=after,
         )
     else:
@@ -659,25 +670,29 @@
         after=[halves[1], *(ahead[2:5:2] if folded else ())],
     )
     pieces = exchange_split(sent)
+    block_out, written = call(
+        functools.partial(join_ahead, groups),
+        [((1, local, model), BF16), ((8, LANES), F32)],
+        *ahead,
+        stored=1,
+        scratch=[pltpu.SemaphoreType.DMA((2 * groups,))],
+    )
     shapes = [((TAPS + rows, channels), BF16)] * groups
-    sums = list(call(add_halves, shapes, halves[0], swap(halves[1], "frame", masks[-1])))
+    other = swap(halves[1], "frame", masks[-1])
+    sums = list(call(add_halves, shapes, halves[0], other, after=[written]))
     sums[-1] = stack(sums[-1], after=pieces[2:3])
     sums = exchange(sums)
     shapes = [((rows, model), F32), ((KERNEL, model), F32)]
     sums = call(functools.partial(scale_sums, groups, scale), shapes, *sums)
-    return tuple(
-        call(
-            functools.partial(join_all, groups, len(pieces)),
-            [((1, local, model), BF16)]
-            + [((1, local, inner), BF16)] * 3
-            + [((rows, model), F32), ((KERNEL, model), F32)],
-            *ahead,
-            *pieces,
-            *sums,
-            stored=True,
-            scratch=[pltpu.SemaphoreType.DMA((8 * groups + 2,))],
-        )
-    )
+    joined = call(
+        functools.partial(join_all, groups, len(pieces)),
+        [((1, local, inner), BF16)] * 3 + [((rows, model), F32), ((KERNEL, model), F32)],
+        *pieces,
+        *sums,
+        stored=5,
+        scratch=[pltpu.SemaphoreType.DMA((8 * groups + 2,))],
+    )
+    return (block_out, *joined)
 
 
 def solution(mesh):

time: 81.6 us -> 81.2 us (level)
  waiting for transfers between devices: 27 us -> 26.1 us
    ppermute x31, waiting for transfers between devices: 27 us -> 26.1 us  [swap(): return lax.ppermute(cells, axis, [(i, i ^ mask) for i in range(count)])]
    pallas_call x22 -> x23, Pallas kernels: 17.4 us -> 17.8 us  [call(): pl.pallas_call(lambda *refs: body(*refs[:count], *refs[count + len(after)...]
  transfers between devices with their start and end apart: 31 -> 31, of which waited for: 16 -> 16; matrix products, arithmetic and copies ran while one was open for 0% -> 0% of each run, Pallas kernels for 15% -> 16%
where the time goes in v6:
time: 81.2 us; the launch traced here: 81.1 us
  starting transfers between devices  36.3 us (45%)
  waiting for transfers between devices  26.1 us (32%)
  Pallas kernels  17.8 us (22%)
  between operations  0.84 us (1%)
    ppermute x31, starting transfers between devices, swap(): return lax.ppermute(cells, axis, [(i, i ^ mask) for i in range(count)])  36.3 us
    ppermute x31, waiting for transfers between devices, swap(): return lax.ppermute(cells, axis, [(i, i ^ mask) for i in range(count)])  26.1 us
    pallas_call x23, Pallas kernels, call(): pl.pallas_call(lambda *refs: body(*refs[:count], *refs[count + len(after)...  17.8 us
  transfers between devices with their start and end apart: 31, of which 16 were waited for; matrix products, arithmetic and copies ran while one was open for 0% of the time, Pallas kernels for 16%

profile of v6, /device:TPU:0, one launch (start us, length us, event | category | flops | bytes accessed | tf_op | source)
XLA Modules:
  0.0 81.1 jit_solution(14319304305046624883)
XLA Ops:
  1.9 3.0 %collective-permute-start = (bf16[112,1024]{1,0:T(8,128)(2,1)S(1)}, bf16[112,1024]{1,0:T(8,128)(2,1)S(1)}, u32[]{:S(2)}, u32[]{:S(2)}) collective-permute-start(bf16[112,1024]{1,0:T(8,128)(2,1)S(1)} %get-tuple-element.60), channel_id=1, source_target_pairs={{0,8},{8,0},{16,24},{24,16},{1,9},{9,1},{17,25},{25,17},{2,10},{10... | collective-permute-start | bytes 688136 | tf_op jit(solution)/shard_map/ppermute | solution.py:31
  4.9 1.5 %collective-permute-start.1 = (bf16[112,1024]{1,0:T(8,128)(2,1)S(1)}, bf16[112,1024]{1,0:T(8,128)(2,1)S(1)}, u32[]{:S(2)}, u32[]{:S(2)}) collective-permute-start(bf16[112,1024]{1,0:T(8,128)(2,1)S(1)} %get-tuple-element.61), channel_id=1, source_target_pairs={{0,16},{8,24},{16,0},{24,8},{1,17},{9,25},{17,1},{25,9},{2,18},{10... | collective-permute-start | bytes 688136 | tf_op jit(solution)/shard_map/ppermute | solution.py:31
  6.5 4.9 %collective-permute-done.refs_1_ = bf16[112,1024]{1,0:T(8,128)(2,1)S(1)} collective-permute-done((bf16[112,1024]{1,0:T(8,128)(2,1)S(1)}, bf16[112,1024]{1,0:T(8,128)(2,1)S(1)}, u32[]{:S(2)}, u32[]{:S(2)}) %collective-permute-start) | collective-permute-done | bytes 229408 | tf_op jit(solution)/shard_map/ppermute | solution.py:31
  11.4 5.5 %collective-permute-done.1.refs_2_ = bf16[112,1024]{1,0:T(8,128)(2,1)S(1)} collective-permute-done((bf16[112,1024]{1,0:T(8,128)(2,1)S(1)}, bf16[112,1024]{1,0:T(8,128)(2,1)S(1)}, u32[]{:S(2)}, u32[]{:S(2)}) %collective-permute-start.1) | collective-permute-done | bytes 229408 | tf_op jit(solution)/shard_map/ppermute | solution.py:31
  16.9 1.4 %shard_map.110 = (bf16[512,768]{1,0:T(8,128)(2,1)S(1)}, bf16[256,256]{1,0:T(8,128)(2,1)S(1)}, bf16[256,256]{1,0:T(8,128)(2,1)S(1)}, bf16[128,512]{1,0:T(8,128)(2,1)S(1)}) custom-call(bf16[112,1024]{1,0:T(8,128)(2,1)S(1)} %get-tuple-element.59.refs_0_, bf16[112,1024]{1,0:T(8,128)(2,1)S(1)} %collective-permute-done.refs_1_, ...), custom_call_target="tpu_custom_call" | custom-call | flops 1610612736 | bytes 2097152 | tf_op jit(solution)/shard_map/pallas_call | solution.py:55
  18.3 1.6 %collective-permute-start.5 = (bf16[256,256]{1,0:T(8,128)(2,1)S(1)}, bf16[256,256]{1,0:T(8,128)(2,1)S(1)}, u32[]{:S(2)}, u32[]{:S(2)}) collective-permute-start(bf16[256,256]{1,0:T(8,128)(2,1)S(1)} %get-tuple-element.64.refs_0_.refs_3_), channel_id=1, source_target_pairs={{0,16},{8,24},{16,0},{24,8},{1,17},{9,25},{17,1},{25,9},{2,18},{10... | collective-permute-start | bytes 393224 | tf_op jit(solution)/shard_map/ppermute | solution.py:31
  20.4 2.6 %collective-permute-start.7 = (bf16[128,512]{1,0:T(8,128)(2,1)S(1)}, bf16[128,512]{1,0:T(8,128)(2,1)S(1)}, u32[]{:S(2)}, u32[]{:S(2)}) collective-permute-start(bf16[128,512]{1,0:T(8,128)(2,1)S(1)} %get-tuple-element.65.refs_0_), channel_id=1, source_target_pairs={{0,4},{1,5},{2,6},{3,7},{4,0},{5,1},{6,2},{7,3},{8,12},{9,13},{10,... | collective-permute-start | bytes 393224 | tf_op jit(solution)/shard_map/ppermute | solution.py:31
  23.0 1.6 %collective-permute-start.8 = (bf16[128,512]{1,0:T(8,128)(2,1)S(1)}, bf16[128,512]{1,0:T(8,128)(2,1)S(1)}, u32[]{:S(2)}, u32[]{:S(2)}) collective-permute-start(bf16[128,512]{1,0:T(8,128)(2,1)S(1)} %get-tuple-element.65.refs_0_), channel_id=1, source_target_pairs={{0,2},{1,3},{2,0},{3,1},{4,6},{5,7},{6,4},{7,5},{8,10},{9,11},{10,... | collective-permute-start | bytes 393224 | tf_op jit(solution)/shard_map/ppermute | solution.py:31
  24.6 1.6 %collective-permute-start.6 = (bf16[512,256]{1,0:T(8,128)(2,1)S(1)}, bf16[512,256]{1,0:T(8,128)(2,1)S(1)}, u32[]{:S(2)}, u32[]{:S(2)}) collective-permute-start(bf16[512,256]{1,0:T(8,128)(2,1)S(1)} %shard_map.112), channel_id=1, source_target_pairs={{0,8},{8,0},{16,24},{24,16},{1,9},{9,1},{17,25},{25,17},{2,10},{10... | collective-permute-start | bytes 786440 | tf_op jit(solution)/shard_map/ppermute | solution.py:31
  26.8 1.3 %collective-permute-start.10 = (bf16[128,512]{1,0:T(8,128)(2,1)S(1)}, bf16[128,512]{1,0:T(8,128)(2,1)S(1)}, u32[]{:S(2)}, u32[]{:S(2)}) collective-permute-start(bf16[128,512]{1,0:T(8,128)(2,1)S(1)} %get-tuple-element.66), channel_id=1, source_target_pairs={{0,8},{8,0},{16,24},{24,16},{1,9},{9,1},{17,25},{25,17},{2,10},{10... | collective-permute-start | bytes 393224 | tf_op jit(solution)/shard_map/ppermute | solution.py:31
  29.9 3.4 %collective-permute-done.10.refs_6_.refs_1_ = bf16[128,512]{1,0:T(8,128)(2,1)S(1)} collective-permute-done((bf16[128,512]{1,0:T(8,128)(2,1)S(1)}, bf16[128,512]{1,0:T(8,128)(2,1)S(1)}, u32[]{:S(2)}, u32[]{:S(2)}) %collective-permute-start.10) | collective-permute-done | bytes 131104 | tf_op jit(solution)/shard_map/ppermute | solution.py:31
  34.4 1.8 %collective-permute-start.17 = (bf16[128,512]{1,0:T(8,128)(2,1)S(1)}, bf16[128,512]{1,0:T(8,128)(2,1)S(1)}, u32[]{:S(2)}, u32[]{:S(2)}) collective-permute-start(bf16[128,512]{1,0:T(8,128)(2,1)S(1)} %get-tuple-element.76), channel_id=1, source_target_pairs={{0,24},{8,16},{16,8},{24,0},{1,25},{9,17},{17,9},{25,1},{2,26},{10... | collective-permute-start | bytes 393224 | tf_op jit(solution)/shard_map/ppermute | solution.py:31
  36.4 3.4 %shard_map.116 = (bf16[512,1024]{1,0:T(8,128)(2,1)S(1)}, bf16[512,512]{1,0:T(8,128)(2,1)S(1)}, f32[512,512]{1,0:T(8,128)S(1)}, bf16[128,512]{1,0:T(8,128)(2,1)S(...) custom-call(bf16[256,256]{1,0:T(8,128)(2,1)S(1)} %get-tuple-element., ...), custom_call_target="tpu_custom_call" | custom-call | flops 4875878400 | bytes 5369856 | tf_op jit(solution)/shard_map/pallas_call | solution.py:55
  42.2 5.4 %shard_map.121 = (bf16[512,512]{1,0:T(8,128)(2,1)S(1)}, f32[32,512]{1,0:T(8,128)S(1)}, bf16[512,256]{1,0:T(8,128)(2,1)S(1)}, bf16[512,256]{1,0:T(8,128)(2,1)S(1)...) custom-call(bf16[128,512]{1,0:T(8,128)(2,1)S(1)} %get-tuple-element.75.refs_0_, ...), custom_call_target="tpu_custom_call" | custom-call | flops 7313817600 | bytes 4911104 | tf_op jit(solution)/shard_map/pallas_call | solution.py:55
  52.5 1.8 %collective-permute-start.16 = (bf16[128,512]{1,0:T(8,128)(2,1)S(1)}, bf16[128,512]{1,0:T(8,128)(2,1)S(1)}, u32[]{:S(2)}, u32[]{:S(2)}) collective-permute-start(bf16[128,512]{1,0:T(8,128)(2,1)S(1)} %shard_map.119), channel_id=1, source_target_pairs={{0,8},{8,0},{16,24},{24,16},{1,9},{9,1},{17,25},{25,17},{2,10},{10... | collective-permute-start | bytes 393224 | tf_op jit(solution)/shard_map/ppermute | solution.py:31
  54.6 3.1 %collective-permute-done.20.refs_1_ = bf16[512,256]{1,0:T(8,128)(2,1)S(1)} collective-permute-done((bf16[512,256]{1,0:T(8,128)(2,1)S(1)}, bf16[512,256]{1,0:T(8,128)(2,1)S(1)}, u32[]{:S(2)}, u32[]{:S(2)}) %collective-permute-start.20) | collective-permute-done | bytes 262176 | tf_op jit(solution)/shard_map/ppermute | solution.py:31
  60.0 2.1 %collective-permute-start.27 = (bf16[208,512]{1,0:T(8,128)(2,1)S(1)}, bf16[208,512]{1,0:T(8,128)(2,1)S(1)}, u32[]{:S(2)}, u32[]{:S(2)}) collective-permute-start(bf16[208,512]{1,0:T(8,128)(2,1)S(1)} %get-tuple-element.94.refs_6_), channel_id=1, source_target_pairs={{0,4},{1,5},{2,6},{3,7},{4,0},{5,1},{6,2},{7,3},{8,12},{9,13},{10,... | collective-permute-start | bytes 638984 | tf_op jit(solution)/shard_map/ppermute | solution.py:31
  62.0 1.4 %collective-permute-done.21.refs_5_ = bf16[256,256]{1,0:T(8,128)(2,1)S(1)} collective-permute-done((bf16[256,256]{1,0:T(8,128)(2,1)S(1)}, bf16[256,256]{1,0:T(8,128)(2,1)S(1)}, u32[]{:S(2)}, u32[]{:S(2)}) %collective-permute-start.21) | collective-permute-done | bytes 131104 | tf_op jit(solution)/shard_map/ppermute | solution.py:31
  63.7 1.9 %shard_map.127 = (bf16[128,768]{1,0:T(8,128)(2,1)S(1)}, bf16[128,768]{1,0:T(8,128)(2,1)S(1)}, bf16[128,768]{1,0:T(8,128)(2,1)S(1)}, bf16[128,768]{1,0:T(8,128)(2,1)S(1)}) custom-call(bf16[512,768]{1,0:T(8,128)(2,1)S(1)} %get-tuple-element.71.refs_0_, f32[2,512,512]{2,1,0:T(8,128)S(1)} %shard_map.117.refs_2_.refs_1_, ...), custom_call_target="tpu_custom_call" | custom-call | flops 3221225472 | bytes 4194304 | tf_op jit(solution)/shard_map/pallas_call | solution.py:55
  67.7 1.4 %collective-permute-start.26 = (bf16[128,768]{1,0:T(8,128)(2,1)S(1)}, bf16[128,768]{1,0:T(8,128)(2,1)S(1)}, u32[]{:S(2)}, u32[]{:S(2)}) collective-permute-start(bf16[128,768]{1,0:T(8,128)(2,1)S(1)} %get-tuple-element.98), channel_id=1, source_target_pairs={{0,24},{8,16},{16,8},{24,0},{1,25},{9,17},{17,9},{25,1},{2,26},{10... | collective-permute-start | bytes 589832 | tf_op jit(solution)/shard_map/ppermute | solution.py:31
  70.0 1.8 %collective-permute-done.27.refs_1_ = bf16[208,512]{1,0:T(8,128)(2,1)S(1)} collective-permute-done((bf16[208,512]{1,0:T(8,128)(2,1)S(1)}, bf16[208,512]{1,0:T(8,128)(2,1)S(1)}, u32[]{:S(2)}, u32[]{:S(2)}) %collective-permute-start.27) | collective-permute-done | bytes 213024 | tf_op jit(solution)/shard_map/ppermute | solution.py:31
  72.6 1.8 %collective-permute-start.30 = (bf16[64,512]{1,0:T(8,128)(2,1)S(1)}, bf16[64,512]{1,0:T(8,128)(2,1)S(1)}, u32[]{:S(2)}, u32[]{:S(2)}) collective-permute-start(bf16[64,512]{1,0:T(8,128)(2,1)S(1)} %shard_map.129), channel_id=1, source_target_pairs={{0,24},{8,16},{16,8},{24,0},{1,25},{9,17},{17,9},{25,1},{2,26},{10... | collective-permute-start | bytes 196616 | tf_op jit(solution)/shard_map/ppermute | solution.py:31
  76.0 2.9 %collective-permute-done.30.refs_3_ = bf16[64,512]{1,0:T(8,128)(2,1)S(1)} collective-permute-done((bf16[64,512]{1,0:T(8,128)(2,1)S(1)}, bf16[64,512]{1,0:T(8,128)(2,1)S(1)}, u32[]{:S(2)}, u32[]{:S(2)}) %collective-permute-start.30) | collective-permute-done | bytes 65568 | tf_op jit(solution)/shard_map/ppermute | solution.py:31
  79.7 1.4 %shard_map.131 = (bf16[1,128,1024]{2,1,0:T(8,128)(2,1)}, bf16[1,128,1024]{2,1,0:T(8,128)(2,1)}, bf16[1,128,1024]{2,1,0:T(8,128)(2,1)}, f32[32,2048]{1,0:T(8,128)}, f32[31,2048]{1,0:T(8,128)}) custom-call(bf16[128,768]{1,0:T(8,128)(2,1)S(1)} %get-tuple-element.95.refs_0_, bf16[128,768]{1,0:T(8,128)(2,1)S(1)} %collective-permute-done.24.refs_1_, ...), custom_call_target="tpu_custom_call" | custom-call | bytes 2605056 | tf_op jit(solution)/shard_map/pallas_call | solution.py:55
  (65 shorter events, 21.8 us)
Async XLA Ops:
  1.9 9.4 %collective-permute-start = (bf16[112,1024]{1,0:T(8,128)(2,1)S(1)}, bf16[112,1024]{1,0:T(8,128)(2,1)S(1)}, u32[]{:S(2)}, u32[]{:S(2)}) collective-permute-start(bf16[112,1024]{1,0:T(8,128)(2,1)S(1)} %get-tuple-element.60), channel_id=1, source_target_pairs={{0,8},{8,0},{16,24},{24,16},{1,9},{9,1},{17,25},{25,17},{2,10},{10... | collective-permute-start | bytes 688136 | tf_op jit(solution)/shard_map/ppermute | solution.py:31
  4.9 12.0 %collective-permute-start.1 = (bf16[112,1024]{1,0:T(8,128)(2,1)S(1)}, bf16[112,1024]{1,0:T(8,128)(2,1)S(1)}, u32[]{:S(2)}, u32[]{:S(2)}) collective-permute-start(bf16[112,1024]{1,0:T(8,128)(2,1)S(1)} %get-tuple-element.61), channel_id=1, source_target_pairs={{0,16},{8,24},{16,0},{24,8},{1,17},{9,25},{17,1},{25,9},{2,18},{10... | collective-permute-start | bytes 688136 | tf_op jit(solution)/shard_map/ppermute | solution.py:31
  6.5 10.5 %collective-permute-start.2 = (bf16[112,1024]{1,0:T(8,128)(2,1)S(1)}, bf16[112,1024]{1,0:T(8,128)(2,1)S(1)}, u32[]{:S(2)}, u32[]{:S(2)}) collective-permute-start(bf16[112,1024]{1,0:T(8,128)(2,1)S(1)} %get-tuple-element.62), channel_id=1, source_target_pairs={{0,24},{8,16},{16,8},{24,0},{1,25},{9,17},{17,9},{25,1},{2,26},{10... | collective-permute-start | bytes 688136 | tf_op jit(solution)/shard_map/ppermute | solution.py:31
  18.3 6.3 %collective-permute-start.5 = (bf16[256,256]{1,0:T(8,128)(2,1)S(1)}, bf16[256,256]{1,0:T(8,128)(2,1)S(1)}, u32[]{:S(2)}, u32[]{:S(2)}) collective-permute-start(bf16[256,256]{1,0:T(8,128)(2,1)S(1)} %get-tuple-element.64.refs_0_.refs_3_), channel_id=1, source_target_pairs={{0,16},{8,24},{16,0},{24,8},{1,17},{9,25},{17,1},{25,9},{2,18},{10... | collective-permute-start | bytes 393224 | tf_op jit(solution)/shard_map/ppermute | solution.py:31
  19.9 6.3 %collective-permute-start.3 = (bf16[256,256]{1,0:T(8,128)(2,1)S(1)}, bf16[256,256]{1,0:T(8,128)(2,1)S(1)}, u32[]{:S(2)}, u32[]{:S(2)}) collective-permute-start(bf16[256,256]{1,0:T(8,128)(2,1)S(1)} %get-tuple-element.63.refs_0_), channel_id=1, source_target_pairs={{0,8},{8,0},{16,24},{24,16},{1,9},{9,1},{17,25},{25,17},{2,10},{10... | collective-permute-start | bytes 393224 | tf_op jit(solution)/shard_map/ppermute | solution.py:31
  20.4 7.7 %collective-permute-start.7 = (bf16[128,512]{1,0:T(8,128)(2,1)S(1)}, bf16[128,512]{1,0:T(8,128)(2,1)S(1)}, u32[]{:S(2)}, u32[]{:S(2)}) collective-permute-start(bf16[128,512]{1,0:T(8,128)(2,1)S(1)} %get-tuple-element.65.refs_0_), channel_id=1, source_target_pairs={{0,4},{1,5},{2,6},{3,7},{4,0},{5,1},{6,2},{7,3},{8,12},{9,13},{10,... | collective-permute-start | bytes 393224 | tf_op jit(solution)/shard_map/ppermute | solution.py:31
  23.0 6.3 %collective-permute-start.8 = (bf16[128,512]{1,0:T(8,128)(2,1)S(1)}, bf16[128,512]{1,0:T(8,128)(2,1)S(1)}, u32[]{:S(2)}, u32[]{:S(2)}) collective-permute-start(bf16[128,512]{1,0:T(8,128)(2,1)S(1)} %get-tuple-element.65.refs_0_), channel_id=1, source_target_pairs={{0,2},{1,3},{2,0},{3,1},{4,6},{5,7},{6,4},{7,5},{8,10},{9,11},{10,... | collective-permute-start | bytes 393224 | tf_op jit(solution)/shard_map/ppermute | solution.py:31
  24.6 9.7 %collective-permute-start.6 = (bf16[512,256]{1,0:T(8,128)(2,1)S(1)}, bf16[512,256]{1,0:T(8,128)(2,1)S(1)}, u32[]{:S(2)}, u32[]{:S(2)}) collective-permute-start(bf16[512,256]{1,0:T(8,128)(2,1)S(1)} %shard_map.112), channel_id=1, source_target_pairs={{0,8},{8,0},{16,24},{24,16},{1,9},{9,1},{17,25},{25,17},{2,10},{10... | collective-permute-start | bytes 786440 | tf_op jit(solution)/shard_map/ppermute | solution.py:31
  26.2 8.1 %collective-permute-start.4 = (bf16[512,256]{1,0:T(8,128)(2,1)S(1)}, bf16[512,256]{1,0:T(8,128)(2,1)S(1)}, u32[]{:S(2)}, u32[]{:S(2)}) collective-permute-start(bf16[512,256]{1,0:T(8,128)(2,1)S(1)} %shard_map.111), channel_id=1, source_target_pairs={{0,16},{8,24},{16,0},{24,8},{1,17},{9,25},{17,1},{25,9},{2,18},{10... | collective-permute-start | bytes 786440 | tf_op jit(solution)/shard_map/ppermute | solution.py:31
  26.8 6.5 %collective-permute-start.10 = (bf16[128,512]{1,0:T(8,128)(2,1)S(1)}, bf16[128,512]{1,0:T(8,128)(2,1)S(1)}, u32[]{:S(2)}, u32[]{:S(2)}) collective-permute-start(bf16[128,512]{1,0:T(8,128)(2,1)S(1)} %get-tuple-element.66), channel_id=1, source_target_pairs={{0,8},{8,0},{16,24},{24,16},{1,9},{9,1},{17,25},{25,17},{2,10},{10... | collective-permute-start | bytes 393224 | tf_op jit(solution)/shard_map/ppermute | solution.py:31
  28.1 5.9 %collective-permute-start.11 = (bf16[128,512]{1,0:T(8,128)(2,1)S(1)}, bf16[128,512]{1,0:T(8,128)(2,1)S(1)}, u32[]{:S(2)}, u32[]{:S(2)}) collective-permute-start(bf16[128,512]{1,0:T(8,128)(2,1)S(1)} %get-tuple-element.67), channel_id=1, source_target_pairs={{0,16},{8,24},{16,0},{24,8},{1,17},{9,25},{17,1},{25,9},{2,18},{10... | collective-permute-start | bytes 393224 | tf_op jit(solution)/shard_map/ppermute | solution.py:31
  34.4 7.8 %collective-permute-start.17 = (bf16[128,512]{1,0:T(8,128)(2,1)S(1)}, bf16[128,512]{1,0:T(8,128)(2,1)S(1)}, u32[]{:S(2)}, u32[]{:S(2)}) collective-permute-start(bf16[128,512]{1,0:T(8,128)(2,1)S(1)} %get-tuple-element.76), channel_id=1, source_target_pairs={{0,24},{8,16},{16,8},{24,0},{1,25},{9,17},{17,9},{25,1},{2,26},{10... | collective-permute-start | bytes 393224 | tf_op jit(solution)/shard_map/ppermute | solution.py:31
  39.8 7.8 %collective-permute-start.13 = (bf16[128,512]{1,0:T(8,128)(2,1)S(1)}, bf16[128,512]{1,0:T(8,128)(2,1)S(1)}, u32[]{:S(2)}, u32[]{:S(2)}) collective-permute-start(bf16[128,512]{1,0:T(8,128)(2,1)S(1)} %get-tuple-element.69), channel_id=1, source_target_pairs={{0,8},{8,0},{16,24},{24,16},{1,9},{9,1},{17,25},{25,17},{2,10},{10... | collective-permute-start | bytes 393224 | tf_op jit(solution)/shard_map/ppermute | solution.py:31
  41.0 6.6 %collective-permute-start.15 = (bf16[128,512]{1,0:T(8,128)(2,1)S(1)}, bf16[128,512]{1,0:T(8,128)(2,1)S(1)}, u32[]{:S(2)}, u32[]{:S(2)}) collective-permute-start(bf16[128,512]{1,0:T(8,128)(2,1)S(1)} %get-tuple-element.72), channel_id=1, source_target_pairs={{0,16},{8,24},{16,0},{24,8},{1,17},{9,25},{17,1},{25,9},{2,18},{10... | collective-permute-start | bytes 393224 | tf_op jit(solution)/shard_map/ppermute | solution.py:31
  48.5 9.2 %collective-permute-start.20 = (bf16[512,256]{1,0:T(8,128)(2,1)S(1)}, bf16[512,256]{1,0:T(8,128)(2,1)S(1)}, u32[]{:S(2)}, u32[]{:S(2)}) collective-permute-start(bf16[512,256]{1,0:T(8,128)(2,1)S(1)} %get-tuple-element.84), channel_id=1, source_target_pairs={{0,16},{8,24},{16,0},{24,8},{1,17},{9,25},{17,1},{25,9},{2,18},{10... | collective-permute-start | bytes 786440 | tf_op jit(solution)/shard_map/ppermute | solution.py:31
  49.4 9.2 %collective-permute-start.18 = (bf16[512,256]{1,0:T(8,128)(2,1)S(1)}, bf16[512,256]{1,0:T(8,128)(2,1)S(1)}, u32[]{:S(2)}, u32[]{:S(2)}) collective-permute-start(bf16[512,256]{1,0:T(8,128)(2,1)S(1)} %get-tuple-element.80), channel_id=1, source_target_pairs={{0,8},{8,0},{16,24},{24,16},{1,9},{9,1},{17,25},{25,17},{2,10},{10... | collective-permute-start | bytes 786440 | tf_op jit(solution)/shard_map/ppermute | solution.py:31
  50.6 9.3 %collective-permute-start.23 = (bf16[288,512]{1,0:T(8,128)(2,1)S(1)}, bf16[288,512]{1,0:T(8,128)(2,1)S(1)}, u32[]{:S(2)}, u32[]{:S(2)}) collective-permute-start(bf16[288,512]{1,0:T(8,128)(2,1)S(1)} %get-tuple-element.93), channel_id=1, source_target_pairs={{0,2},{1,3},{2,0},{3,1},{4,6},{5,7},{6,4},{7,5},{8,10},{9,11},{10,... | collective-permute-start | bytes 884744 | tf_op jit(solution)/shard_map/ppermute | solution.py:31
  52.5 9.5 %collective-permute-start.16 = (bf16[128,512]{1,0:T(8,128)(2,1)S(1)}, bf16[128,512]{1,0:T(8,128)(2,1)S(1)}, u32[]{:S(2)}, u32[]{:S(2)}) collective-permute-start(bf16[128,512]{1,0:T(8,128)(2,1)S(1)} %shard_map.119), channel_id=1, source_target_pairs={{0,8},{8,0},{16,24},{24,16},{1,9},{9,1},{17,25},{25,17},{2,10},{10... | collective-permute-start | bytes 393224 | tf_op jit(solution)/shard_map/ppermute | solution.py:31
  54.3 7.7 %collective-permute-start.14 = (bf16[128,512]{1,0:T(8,128)(2,1)S(1)}, bf16[128,512]{1,0:T(8,128)(2,1)S(1)}, u32[]{:S(2)}, u32[]{:S(2)}) collective-permute-start(bf16[128,512]{1,0:T(8,128)(2,1)S(1)} %shard_map.118), channel_id=1, source_target_pairs={{0,16},{8,24},{16,0},{24,8},{1,17},{9,25},{17,1},{25,9},{2,18},{10... | collective-permute-start | bytes 393224 | tf_op jit(solution)/shard_map/ppermute | solution.py:31
  60.0 11.8 %collective-permute-start.27 = (bf16[208,512]{1,0:T(8,128)(2,1)S(1)}, bf16[208,512]{1,0:T(8,128)(2,1)S(1)}, u32[]{:S(2)}, u32[]{:S(2)}) collective-permute-start(bf16[208,512]{1,0:T(8,128)(2,1)S(1)} %get-tuple-element.94.refs_6_), channel_id=1, source_target_pairs={{0,4},{1,5},{2,6},{3,7},{4,0},{5,1},{6,2},{7,3},{8,12},{9,13},{10,... | collective-permute-start | bytes 638984 | tf_op jit(solution)/shard_map/ppermute | solution.py:31
  65.6 7.0 %collective-permute-start.25 = (bf16[128,768]{1,0:T(8,128)(2,1)S(1)}, bf16[128,768]{1,0:T(8,128)(2,1)S(1)}, u32[]{:S(2)}, u32[]{:S(2)}) collective-permute-start(bf16[128,768]{1,0:T(8,128)(2,1)S(1)} %get-tuple-element.97), channel_id=1, source_target_pairs={{0,16},{8,24},{16,0},{24,8},{1,17},{9,25},{17,1},{25,9},{2,18},{10... | collective-permute-start | bytes 589832 | tf_op jit(solution)/shard_map/ppermute | solution.py:31
  66.8 12.9 %collective-permute-start.24 = (bf16[128,768]{1,0:T(8,128)(2,1)S(1)}, bf16[128,768]{1,0:T(8,128)(2,1)S(1)}, u32[]{:S(2)}, u32[]{:S(2)}) collective-permute-start(bf16[128,768]{1,0:T(8,128)(2,1)S(1)} %get-tuple-element.96), channel_id=1, source_target_pairs={{0,8},{8,0},{16,24},{24,16},{1,9},{9,1},{17,25},{25,17},{2,10},{10... | collective-permute-start | bytes 589832 | tf_op jit(solution)/shard_map/ppermute | solution.py:31
  67.7 12.0 %collective-permute-start.26 = (bf16[128,768]{1,0:T(8,128)(2,1)S(1)}, bf16[128,768]{1,0:T(8,128)(2,1)S(1)}, u32[]{:S(2)}, u32[]{:S(2)}) collective-permute-start(bf16[128,768]{1,0:T(8,128)(2,1)S(1)} %get-tuple-element.98), channel_id=1, source_target_pairs={{0,24},{8,16},{16,8},{24,0},{1,25},{9,17},{17,9},{25,1},{2,26},{10... | collective-permute-start | bytes 589832 | tf_op jit(solution)/shard_map/ppermute | solution.py:31
  72.6 6.4 %collective-permute-start.30 = (bf16[64,512]{1,0:T(8,128)(2,1)S(1)}, bf16[64,512]{1,0:T(8,128)(2,1)S(1)}, u32[]{:S(2)}, u32[]{:S(2)}) collective-permute-start(bf16[64,512]{1,0:T(8,128)(2,1)S(1)} %shard_map.129), channel_id=1, source_target_pairs={{0,24},{8,16},{16,8},{24,0},{1,25},{9,17},{17,9},{25,1},{2,26},{10... | collective-permute-start | bytes 196616 | tf_op jit(solution)/shard_map/ppermute | solution.py:31
  (9 other events, 48.6 us)

commit v7 on v6

--- a/solution.py
+++ b/solution.py
@@ -19,7 +19,7 @@
 ATTEND_COST = 24
 BACK_COST = 48
 SPLIT_BACK = False
-PAD = 48
+PAD = 0
 PACK_LIMIT = 60
 F32 = jnp.float32
 BF16 = jnp.bfloat16
@@ -680,7 +680,8 @@
     shapes = [((TAPS + rows, channels), BF16)] * groups
     other = swap(halves[1], "frame", masks[-1])
     sums = list(call(add_halves, shapes, halves[0], other, after=[written]))
-    sums[-1] = stack(sums[-1], after=pieces[2:3])
+    first = swap(sums[0], "frame", 1)
+    sums[-1] = stack(sums[-1], after=[first, pieces[2]])
     sums = exchange(sums)
     shapes = [((rows, model), F32), ((KERNEL, model), F32)]
     sums = call(functools.partial(scale_sums, groups, scale), shapes, *sums)

time: 81.2 us -> 81.2 us (level)
  starting transfers between devices: 36.3 us -> 37.4 us
  waiting for transfers between devices: 26.1 us -> 25 us
    ppermute x31 -> x32, waiting for transfers between devices: 26.1 us -> 25 us  [swap(): return lax.ppermute(cells, axis, [(i, i ^ mask) for i in range(count)])]
    ppermute x31 -> x32, starting transfers between devices: 36.3 us -> 37.4 us  [swap(): return lax.ppermute(cells, axis, [(i, i ^ mask) for i in range(count)])]
  transfers between devices with their start and end apart: 31 -> 32, of which waited for: 16 -> 15; matrix products, arithmetic and copies ran while one was open for 0% -> 0% of each run, Pallas kernels for 16% -> 16%
where the time goes in v7:
time: 81.2 us; the launch traced here: 81.1 us
  starting transfers between devices  37.4 us (46%)
  waiting for transfers between devices  25 us (31%)
  Pallas kernels  17.8 us (22%)
  between operations  0.86 us (1%)
    ppermute x32, starting transfers between devices, swap(): return lax.ppermute(cells, axis, [(i, i ^ mask) for i in range(count)])  37.4 us
    ppermute x32, waiting for transfers between devices, swap(): return lax.ppermute(cells, axis, [(i, i ^ mask) for i in range(count)])  25 us
    pallas_call x23, Pallas kernels, call(): pl.pallas_call(lambda *refs: body(*refs[:count], *refs[count + len(after)...  17.8 us
  transfers between devices with their start and end apart: 32, of which 15 were waited for; matrix products, arithmetic and copies ran while one was open for 0% of the time, Pallas kernels for 16%

profile of v7, /device:TPU:0, one launch (start us, length us, event | category | flops | bytes accessed | tf_op | source)
XLA Modules:
  0.0 81.1 jit_solution(16291846425086212241)
XLA Ops:
  1.9 3.0 %collective-permute-start = (bf16[112,1024]{1,0:T(8,128)(2,1)S(1)}, bf16[112,1024]{1,0:T(8,128)(2,1)S(1)}, u32[]{:S(2)}, u32[]{:S(2)}) collective-permute-start(bf16[112,1024]{1,0:T(8,128)(2,1)S(1)} %get-tuple-element.60), channel_id=1, source_target_pairs={{0,8},{8,0},{16,24},{24,16},{1,9},{9,1},{17,25},{25,17},{2,10},{10... | collective-permute-start | bytes 688136 | tf_op jit(solution)/shard_map/ppermute | solution.py:31
  4.9 1.5 %collective-permute-start.1 = (bf16[112,1024]{1,0:T(8,128)(2,1)S(1)}, bf16[112,1024]{1,0:T(8,128)(2,1)S(1)}, u32[]{:S(2)}, u32[]{:S(2)}) collective-permute-start(bf16[112,1024]{1,0:T(8,128)(2,1)S(1)} %get-tuple-element.61), channel_id=1, source_target_pairs={{0,16},{8,24},{16,0},{24,8},{1,17},{9,25},{17,1},{25,9},{2,18},{10... | collective-permute-start | bytes 688136 | tf_op jit(solution)/shard_map/ppermute | solution.py:31
  6.5 4.9 %collective-permute-done.refs_1_ = bf16[112,1024]{1,0:T(8,128)(2,1)S(1)} collective-permute-done((bf16[112,1024]{1,0:T(8,128)(2,1)S(1)}, bf16[112,1024]{1,0:T(8,128)(2,1)S(1)}, u32[]{:S(2)}, u32[]{:S(2)}) %collective-permute-start) | collective-permute-done | bytes 229408 | tf_op jit(solution)/shard_map/ppermute | solution.py:31
  11.4 5.5 %collective-permute-done.1.refs_2_ = bf16[112,1024]{1,0:T(8,128)(2,1)S(1)} collective-permute-done((bf16[112,1024]{1,0:T(8,128)(2,1)S(1)}, bf16[112,1024]{1,0:T(8,128)(2,1)S(1)}, u32[]{:S(2)}, u32[]{:S(2)}) %collective-permute-start.1) | collective-permute-done | bytes 229408 | tf_op jit(solution)/shard_map/ppermute | solution.py:31
  16.9 1.4 %shard_map.110 = (bf16[512,768]{1,0:T(8,128)(2,1)S(1)}, bf16[256,256]{1,0:T(8,128)(2,1)S(1)}, bf16[256,256]{1,0:T(8,128)(2,1)S(1)}, bf16[128,512]{1,0:T(8,128)(2,1)S(1)}) custom-call(bf16[112,1024]{1,0:T(8,128)(2,1)S(1)} %get-tuple-element.59.refs_0_, bf16[112,1024]{1,0:T(8,128)(2,1)S(1)} %collective-permute-done.refs_1_, ...), custom_call_target="tpu_custom_call" | custom-call | flops 1610612736 | bytes 2097152 | tf_op jit(solution)/shard_map/pallas_call | solution.py:55
  18.3 1.6 %collective-permute-start.5 = (bf16[256,256]{1,0:T(8,128)(2,1)S(1)}, bf16[256,256]{1,0:T(8,128)(2,1)S(1)}, u32[]{:S(2)}, u32[]{:S(2)}) collective-permute-start(bf16[256,256]{1,0:T(8,128)(2,1)S(1)} %get-tuple-element.64.refs_0_.refs_3_), channel_id=1, source_target_pairs={{0,16},{8,24},{16,0},{24,8},{1,17},{9,25},{17,1},{25,9},{2,18},{10... | collective-permute-start | bytes 393224 | tf_op jit(solution)/shard_map/ppermute | solution.py:31
  20.4 2.6 %collective-permute-start.7 = (bf16[128,512]{1,0:T(8,128)(2,1)S(1)}, bf16[128,512]{1,0:T(8,128)(2,1)S(1)}, u32[]{:S(2)}, u32[]{:S(2)}) collective-permute-start(bf16[128,512]{1,0:T(8,128)(2,1)S(1)} %get-tuple-element.65.refs_0_), channel_id=1, source_target_pairs={{0,4},{1,5},{2,6},{3,7},{4,0},{5,1},{6,2},{7,3},{8,12},{9,13},{10,... | collective-permute-start | bytes 393224 | tf_op jit(solution)/shard_map/ppermute | solution.py:31
  23.0 1.6 %collective-permute-start.8 = (bf16[128,512]{1,0:T(8,128)(2,1)S(1)}, bf16[128,512]{1,0:T(8,128)(2,1)S(1)}, u32[]{:S(2)}, u32[]{:S(2)}) collective-permute-start(bf16[128,512]{1,0:T(8,128)(2,1)S(1)} %get-tuple-element.65.refs_0_), channel_id=1, source_target_pairs={{0,2},{1,3},{2,0},{3,1},{4,6},{5,7},{6,4},{7,5},{8,10},{9,11},{10,... | collective-permute-start | bytes 393224 | tf_op jit(solution)/shard_map/ppermute | solution.py:31
  24.6 1.6 %collective-permute-start.6 = (bf16[512,256]{1,0:T(8,128)(2,1)S(1)}, bf16[512,256]{1,0:T(8,128)(2,1)S(1)}, u32[]{:S(2)}, u32[]{:S(2)}) collective-permute-start(bf16[512,256]{1,0:T(8,128)(2,1)S(1)} %shard_map.112), channel_id=1, source_target_pairs={{0,8},{8,0},{16,24},{24,16},{1,9},{9,1},{17,25},{25,17},{2,10},{10... | collective-permute-start | bytes 786440 | tf_op jit(solution)/shard_map/ppermute | solution.py:31
  26.8 1.3 %collective-permute-start.10 = (bf16[128,512]{1,0:T(8,128)(2,1)S(1)}, bf16[128,512]{1,0:T(8,128)(2,1)S(1)}, u32[]{:S(2)}, u32[]{:S(2)}) collective-permute-start(bf16[128,512]{1,0:T(8,128)(2,1)S(1)} %get-tuple-element.66), channel_id=1, source_target_pairs={{0,8},{8,0},{16,24},{24,16},{1,9},{9,1},{17,25},{25,17},{2,10},{10... | collective-permute-start | bytes 393224 | tf_op jit(solution)/shard_map/ppermute | solution.py:31
  29.9 3.4 %collective-permute-done.10.refs_6_.refs_1_ = bf16[128,512]{1,0:T(8,128)(2,1)S(1)} collective-permute-done((bf16[128,512]{1,0:T(8,128)(2,1)S(1)}, bf16[128,512]{1,0:T(8,128)(2,1)S(1)}, u32[]{:S(2)}, u32[]{:S(2)}) %collective-permute-start.10) | collective-permute-done | bytes 131104 | tf_op jit(solution)/shard_map/ppermute | solution.py:31
  34.4 1.8 %collective-permute-start.17 = (bf16[128,512]{1,0:T(8,128)(2,1)S(1)}, bf16[128,512]{1,0:T(8,128)(2,1)S(1)}, u32[]{:S(2)}, u32[]{:S(2)}) collective-permute-start(bf16[128,512]{1,0:T(8,128)(2,1)S(1)} %get-tuple-element.76), channel_id=1, source_target_pairs={{0,24},{8,16},{16,8},{24,0},{1,25},{9,17},{17,9},{25,1},{2,26},{10... | collective-permute-start | bytes 393224 | tf_op jit(solution)/shard_map/ppermute | solution.py:31
  36.4 3.4 %shard_map.116 = (bf16[512,1024]{1,0:T(8,128)(2,1)S(1)}, bf16[512,512]{1,0:T(8,128)(2,1)S(1)}, f32[512,512]{1,0:T(8,128)S(1)}, bf16[128,512]{1,0:T(8,128)(2,1)S(...) custom-call(bf16[256,256]{1,0:T(8,128)(2,1)S(1)} %get-tuple-element., ...), custom_call_target="tpu_custom_call" | custom-call | flops 4875878400 | bytes 5369856 | tf_op jit(solution)/shard_map/pallas_call | solution.py:55
  42.2 5.4 %shard_map.121 = (bf16[512,512]{1,0:T(8,128)(2,1)S(1)}, f32[32,512]{1,0:T(8,128)S(1)}, bf16[512,256]{1,0:T(8,128)(2,1)S(1)}, bf16[512,256]{1,0:T(8,128)(2,1)S(1)...) custom-call(bf16[128,512]{1,0:T(8,128)(2,1)S(1)} %get-tuple-element.75.refs_0_, ...), custom_call_target="tpu_custom_call" | custom-call | flops 7313817600 | bytes 4911104 | tf_op jit(solution)/shard_map/pallas_call | solution.py:55
  52.5 1.8 %collective-permute-start.16 = (bf16[128,512]{1,0:T(8,128)(2,1)S(1)}, bf16[128,512]{1,0:T(8,128)(2,1)S(1)}, u32[]{:S(2)}, u32[]{:S(2)}) collective-permute-start(bf16[128,512]{1,0:T(8,128)(2,1)S(1)} %shard_map.119), channel_id=1, source_target_pairs={{0,8},{8,0},{16,24},{24,16},{1,9},{9,1},{17,25},{25,17},{2,10},{10... | collective-permute-start | bytes 393224 | tf_op jit(solution)/shard_map/ppermute | solution.py:31
  54.6 3.1 %collective-permute-done.20.refs_1_ = bf16[512,256]{1,0:T(8,128)(2,1)S(1)} collective-permute-done((bf16[512,256]{1,0:T(8,128)(2,1)S(1)}, bf16[512,256]{1,0:T(8,128)(2,1)S(1)}, u32[]{:S(2)}, u32[]{:S(2)}) %collective-permute-start.20) | collective-permute-done | bytes 262176 | tf_op jit(solution)/shard_map/ppermute | solution.py:31
  60.0 2.1 %collective-permute-start.27 = (bf16[160,512]{1,0:T(8,128)(2,1)S(1)}, bf16[160,512]{1,0:T(8,128)(2,1)S(1)}, u32[]{:S(2)}, u32[]{:S(2)}) collective-permute-start(bf16[160,512]{1,0:T(8,128)(2,1)S(1)} %get-tuple-element.94.refs_6_), channel_id=1, source_target_pairs={{0,4},{1,5},{2,6},{3,7},{4,0},{5,1},{6,2},{7,3},{8,12},{9,13},{10,... | collective-permute-start | bytes 491528 | tf_op jit(solution)/shard_map/ppermute | solution.py:31
  62.1 1.3 %collective-permute-done.21.refs_5_ = bf16[256,256]{1,0:T(8,128)(2,1)S(1)} collective-permute-done((bf16[256,256]{1,0:T(8,128)(2,1)S(1)}, bf16[256,256]{1,0:T(8,128)(2,1)S(1)}, u32[]{:S(2)}, u32[]{:S(2)}) %collective-permute-start.21) | collective-permute-done | bytes 131104 | tf_op jit(solution)/shard_map/ppermute | solution.py:31
  63.7 1.9 %shard_map.127 = (bf16[128,768]{1,0:T(8,128)(2,1)S(1)}, bf16[128,768]{1,0:T(8,128)(2,1)S(1)}, bf16[128,768]{1,0:T(8,128)(2,1)S(1)}, bf16[128,768]{1,0:T(8,128)(2,1)S(1)}) custom-call(bf16[512,768]{1,0:T(8,128)(2,1)S(1)} %get-tuple-element.71.refs_0_, f32[2,512,512]{2,1,0:T(8,128)S(1)} %shard_map.117.refs_2_.refs_1_, ...), custom_call_target="tpu_custom_call" | custom-call | flops 3221225472 | bytes 4194304 | tf_op jit(solution)/shard_map/pallas_call | solution.py:55
  67.7 1.4 %collective-permute-start.26 = (bf16[128,768]{1,0:T(8,128)(2,1)S(1)}, bf16[128,768]{1,0:T(8,128)(2,1)S(1)}, u32[]{:S(2)}, u32[]{:S(2)}) collective-permute-start(bf16[128,768]{1,0:T(8,128)(2,1)S(1)} %get-tuple-element.98), channel_id=1, source_target_pairs={{0,24},{8,16},{16,8},{24,0},{1,25},{9,17},{17,9},{25,1},{2,26},{10... | collective-permute-start | bytes 589832 | tf_op jit(solution)/shard_map/ppermute | solution.py:31
  70.1 1.3 %collective-permute-start.28 = (bf16[64,512]{1,0:T(8,128)(2,1)S(1)}, bf16[64,512]{1,0:T(8,128)(2,1)S(1)}, u32[]{:S(2)}, u32[]{:S(2)}) collective-permute-start(bf16[64,512]{1,0:T(8,128)(2,1)S(1)} %get-tuple-element.102), channel_id=1, source_target_pairs={{0,8},{8,0},{16,24},{24,16},{1,9},{9,1},{17,25},{25,17},{2,10},{10... | collective-permute-start | bytes 196616 | tf_op jit(solution)/shard_map/ppermute | solution.py:31
  73.8 2.0 %collective-permute-start.31 = (bf16[64,512]{1,0:T(8,128)(2,1)S(1)}, bf16[64,512]{1,0:T(8,128)(2,1)S(1)}, u32[]{:S(2)}, u32[]{:S(2)}) collective-permute-start(bf16[64,512]{1,0:T(8,128)(2,1)S(1)} %shard_map.129), channel_id=1, source_target_pairs={{0,24},{8,16},{16,8},{24,0},{1,25},{9,17},{17,9},{25,1},{2,26},{10... | collective-permute-start | bytes 196616 | tf_op jit(solution)/shard_map/ppermute | solution.py:31
  75.7 3.0 %collective-permute-done.28.refs_1_ = bf16[64,512]{1,0:T(8,128)(2,1)S(1)} collective-permute-done((bf16[64,512]{1,0:T(8,128)(2,1)S(1)}, bf16[64,512]{1,0:T(8,128)(2,1)S(1)}, u32[]{:S(2)}, u32[]{:S(2)}) %collective-permute-start.28) | collective-permute-done | bytes 65568 | tf_op jit(solution)/shard_map/ppermute | solution.py:31
  79.7 1.4 %shard_map.131 = (bf16[1,128,1024]{2,1,0:T(8,128)(2,1)}, bf16[1,128,1024]{2,1,0:T(8,128)(2,1)}, bf16[1,128,1024]{2,1,0:T(8,128)(2,1)}, f32[32,2048]{1,0:T(8,128)}, f32[31,2048]{1,0:T(8,128)}) custom-call(bf16[128,768]{1,0:T(8,128)(2,1)S(1)} %get-tuple-element.95.refs_0_, bf16[128,768]{1,0:T(8,128)(2,1)S(1)} %collective-permute-done.24.refs_1_, ...), custom_call_target="tpu_custom_call" | custom-call | bytes 2605056 | tf_op jit(solution)/shard_map/pallas_call | solution.py:55
  (67 shorter events, 22.0 us)
Async XLA Ops:
  1.9 9.4 %collective-permute-start = (bf16[112,1024]{1,0:T(8,128)(2,1)S(1)}, bf16[112,1024]{1,0:T(8,128)(2,1)S(1)}, u32[]{:S(2)}, u32[]{:S(2)}) collective-permute-start(bf16[112,1024]{1,0:T(8,128)(2,1)S(1)} %get-tuple-element.60), channel_id=1, source_target_pairs={{0,8},{8,0},{16,24},{24,16},{1,9},{9,1},{17,25},{25,17},{2,10},{10... | collective-permute-start | bytes 688136 | tf_op jit(solution)/shard_map/ppermute | solution.py:31
  4.9 12.0 %collective-permute-start.1 = (bf16[112,1024]{1,0:T(8,128)(2,1)S(1)}, bf16[112,1024]{1,0:T(8,128)(2,1)S(1)}, u32[]{:S(2)}, u32[]{:S(2)}) collective-permute-start(bf16[112,1024]{1,0:T(8,128)(2,1)S(1)} %get-tuple-element.61), channel_id=1, source_target_pairs={{0,16},{8,24},{16,0},{24,8},{1,17},{9,25},{17,1},{25,9},{2,18},{10... | collective-permute-start | bytes 688136 | tf_op jit(solution)/shard_map/ppermute | solution.py:31
  6.5 10.5 %collective-permute-start.2 = (bf16[112,1024]{1,0:T(8,128)(2,1)S(1)}, bf16[112,1024]{1,0:T(8,128)(2,1)S(1)}, u32[]{:S(2)}, u32[]{:S(2)}) collective-permute-start(bf16[112,1024]{1,0:T(8,128)(2,1)S(1)} %get-tuple-element.62), channel_id=1, source_target_pairs={{0,24},{8,16},{16,8},{24,0},{1,25},{9,17},{17,9},{25,1},{2,26},{10... | collective-permute-start | bytes 688136 | tf_op jit(solution)/shard_map/ppermute | solution.py:31
  18.3 6.3 %collective-permute-start.5 = (bf16[256,256]{1,0:T(8,128)(2,1)S(1)}, bf16[256,256]{1,0:T(8,128)(2,1)S(1)}, u32[]{:S(2)}, u32[]{:S(2)}) collective-permute-start(bf16[256,256]{1,0:T(8,128)(2,1)S(1)} %get-tuple-element.64.refs_0_.refs_3_), channel_id=1, source_target_pairs={{0,16},{8,24},{16,0},{24,8},{1,17},{9,25},{17,1},{25,9},{2,18},{10... | collective-permute-start | bytes 393224 | tf_op jit(solution)/shard_map/ppermute | solution.py:31
  19.9 6.3 %collective-permute-start.3 = (bf16[256,256]{1,0:T(8,128)(2,1)S(1)}, bf16[256,256]{1,0:T(8,128)(2,1)S(1)}, u32[]{:S(2)}, u32[]{:S(2)}) collective-permute-start(bf16[256,256]{1,0:T(8,128)(2,1)S(1)} %get-tuple-element.63.refs_0_), channel_id=1, source_target_pairs={{0,8},{8,0},{16,24},{24,16},{1,9},{9,1},{17,25},{25,17},{2,10},{10... | collective-permute-start | bytes 393224 | tf_op jit(solution)/shard_map/ppermute | solution.py:31
  20.4 7.7 %collective-permute-start.7 = (bf16[128,512]{1,0:T(8,128)(2,1)S(1)}, bf16[128,512]{1,0:T(8,128)(2,1)S(1)}, u32[]{:S(2)}, u32[]{:S(2)}) collective-permute-start(bf16[128,512]{1,0:T(8,128)(2,1)S(1)} %get-tuple-element.65.refs_0_), channel_id=1, source_target_pairs={{0,4},{1,5},{2,6},{3,7},{4,0},{5,1},{6,2},{7,3},{8,12},{9,13},{10,... | collective-permute-start | bytes 393224 | tf_op jit(solution)/shard_map/ppermute | solution.py:31
  23.0 6.3 %collective-permute-start.8 = (bf16[128,512]{1,0:T(8,128)(2,1)S(1)}, bf16[128,512]{1,0:T(8,128)(2,1)S(1)}, u32[]{:S(2)}, u32[]{:S(2)}) collective-permute-start(bf16[128,512]{1,0:T(8,128)(2,1)S(1)} %get-tuple-element.65.refs_0_), channel_id=1, source_target_pairs={{0,2},{1,3},{2,0},{3,1},{4,6},{5,7},{6,4},{7,5},{8,10},{9,11},{10,... | collective-permute-start | bytes 393224 | tf_op jit(solution)/shard_map/ppermute | solution.py:31
  24.6 9.7 %collective-permute-start.6 = (bf16[512,256]{1,0:T(8,128)(2,1)S(1)}, bf16[512,256]{1,0:T(8,128)(2,1)S(1)}, u32[]{:S(2)}, u32[]{:S(2)}) collective-permute-start(bf16[512,256]{1,0:T(8,128)(2,1)S(1)} %shard_map.112), channel_id=1, source_target_pairs={{0,8},{8,0},{16,24},{24,16},{1,9},{9,1},{17,25},{25,17},{2,10},{10... | collective-permute-start | bytes 786440 | tf_op jit(solution)/shard_map/ppermute | solution.py:31
  26.2 8.1 %collective-permute-start.4 = (bf16[512,256]{1,0:T(8,128)(2,1)S(1)}, bf16[512,256]{1,0:T(8,128)(2,1)S(1)}, u32[]{:S(2)}, u32[]{:S(2)}) collective-permute-start(bf16[512,256]{1,0:T(8,128)(2,1)S(1)} %shard_map.111), channel_id=1, source_target_pairs={{0,16},{8,24},{16,0},{24,8},{1,17},{9,25},{17,1},{25,9},{2,18},{10... | collective-permute-start | bytes 786440 | tf_op jit(solution)/shard_map/ppermute | solution.py:31
  26.8 6.5 %collective-permute-start.10 = (bf16[128,512]{1,0:T(8,128)(2,1)S(1)}, bf16[128,512]{1,0:T(8,128)(2,1)S(1)}, u32[]{:S(2)}, u32[]{:S(2)}) collective-permute-start(bf16[128,512]{1,0:T(8,128)(2,1)S(1)} %get-tuple-element.66), channel_id=1, source_target_pairs={{0,8},{8,0},{16,24},{24,16},{1,9},{9,1},{17,25},{25,17},{2,10},{10... | collective-permute-start | bytes 393224 | tf_op jit(solution)/shard_map/ppermute | solution.py:31
  34.4 7.8 %collective-permute-start.17 = (bf16[128,512]{1,0:T(8,128)(2,1)S(1)}, bf16[128,512]{1,0:T(8,128)(2,1)S(1)}, u32[]{:S(2)}, u32[]{:S(2)}) collective-permute-start(bf16[128,512]{1,0:T(8,128)(2,1)S(1)} %get-tuple-element.76), channel_id=1, source_target_pairs={{0,24},{8,16},{16,8},{24,0},{1,25},{9,17},{17,9},{25,1},{2,26},{10... | collective-permute-start | bytes 393224 | tf_op jit(solution)/shard_map/ppermute | solution.py:31
  39.8 7.8 %collective-permute-start.13 = (bf16[128,512]{1,0:T(8,128)(2,1)S(1)}, bf16[128,512]{1,0:T(8,128)(2,1)S(1)}, u32[]{:S(2)}, u32[]{:S(2)}) collective-permute-start(bf16[128,512]{1,0:T(8,128)(2,1)S(1)} %get-tuple-element.69), channel_id=1, source_target_pairs={{0,8},{8,0},{16,24},{24,16},{1,9},{9,1},{17,25},{25,17},{2,10},{10... | collective-permute-start | bytes 393224 | tf_op jit(solution)/shard_map/ppermute | solution.py:31
  41.0 6.6 %collective-permute-start.15 = (bf16[128,512]{1,0:T(8,128)(2,1)S(1)}, bf16[128,512]{1,0:T(8,128)(2,1)S(1)}, u32[]{:S(2)}, u32[]{:S(2)}) collective-permute-start(bf16[128,512]{1,0:T(8,128)(2,1)S(1)} %get-tuple-element.72), channel_id=1, source_target_pairs={{0,16},{8,24},{16,0},{24,8},{1,17},{9,25},{17,1},{25,9},{2,18},{10... | collective-permute-start | bytes 393224 | tf_op jit(solution)/shard_map/ppermute | solution.py:31
  48.5 9.2 %collective-permute-start.20 = (bf16[512,256]{1,0:T(8,128)(2,1)S(1)}, bf16[512,256]{1,0:T(8,128)(2,1)S(1)}, u32[]{:S(2)}, u32[]{:S(2)}) collective-permute-start(bf16[512,256]{1,0:T(8,128)(2,1)S(1)} %get-tuple-element.84), channel_id=1, source_target_pairs={{0,16},{8,24},{16,0},{24,8},{1,17},{9,25},{17,1},{25,9},{2,18},{10... | collective-permute-start | bytes 786440 | tf_op jit(solution)/shard_map/ppermute | solution.py:31
  49.4 9.2 %collective-permute-start.18 = (bf16[512,256]{1,0:T(8,128)(2,1)S(1)}, bf16[512,256]{1,0:T(8,128)(2,1)S(1)}, u32[]{:S(2)}, u32[]{:S(2)}) collective-permute-start(bf16[512,256]{1,0:T(8,128)(2,1)S(1)} %get-tuple-element.80), channel_id=1, source_target_pairs={{0,8},{8,0},{16,24},{24,16},{1,9},{9,1},{17,25},{25,17},{2,10},{10... | collective-permute-start | bytes 786440 | tf_op jit(solution)/shard_map/ppermute | solution.py:31
  50.6 9.3 %collective-permute-start.23 = (bf16[288,512]{1,0:T(8,128)(2,1)S(1)}, bf16[288,512]{1,0:T(8,128)(2,1)S(1)}, u32[]{:S(2)}, u32[]{:S(2)}) collective-permute-start(bf16[288,512]{1,0:T(8,128)(2,1)S(1)} %get-tuple-element.93), channel_id=1, source_target_pairs={{0,2},{1,3},{2,0},{3,1},{4,6},{5,7},{6,4},{7,5},{8,10},{9,11},{10,... | collective-permute-start | bytes 884744 | tf_op jit(solution)/shard_map/ppermute | solution.py:31
  52.5 9.6 %collective-permute-start.16 = (bf16[128,512]{1,0:T(8,128)(2,1)S(1)}, bf16[128,512]{1,0:T(8,128)(2,1)S(1)}, u32[]{:S(2)}, u32[]{:S(2)}) collective-permute-start(bf16[128,512]{1,0:T(8,128)(2,1)S(1)} %shard_map.119), channel_id=1, source_target_pairs={{0,8},{8,0},{16,24},{24,16},{1,9},{9,1},{17,25},{25,17},{2,10},{10... | collective-permute-start | bytes 393224 | tf_op jit(solution)/shard_map/ppermute | solution.py:31
  54.3 7.8 %collective-permute-start.14 = (bf16[128,512]{1,0:T(8,128)(2,1)S(1)}, bf16[128,512]{1,0:T(8,128)(2,1)S(1)}, u32[]{:S(2)}, u32[]{:S(2)}) collective-permute-start(bf16[128,512]{1,0:T(8,128)(2,1)S(1)} %shard_map.118), channel_id=1, source_target_pairs={{0,16},{8,24},{16,0},{24,8},{1,17},{9,25},{17,1},{25,9},{2,18},{10... | collective-permute-start | bytes 393224 | tf_op jit(solution)/shard_map/ppermute | solution.py:31
  60.0 10.0 %collective-permute-start.27 = (bf16[160,512]{1,0:T(8,128)(2,1)S(1)}, bf16[160,512]{1,0:T(8,128)(2,1)S(1)}, u32[]{:S(2)}, u32[]{:S(2)}) collective-permute-start(bf16[160,512]{1,0:T(8,128)(2,1)S(1)} %get-tuple-element.94.refs_6_), channel_id=1, source_target_pairs={{0,4},{1,5},{2,6},{3,7},{4,0},{5,1},{6,2},{7,3},{8,12},{9,13},{10,... | collective-permute-start | bytes 491528 | tf_op jit(solution)/shard_map/ppermute | solution.py:31
  65.6 7.0 %collective-permute-start.25 = (bf16[128,768]{1,0:T(8,128)(2,1)S(1)}, bf16[128,768]{1,0:T(8,128)(2,1)S(1)}, u32[]{:S(2)}, u32[]{:S(2)}) collective-permute-start(bf16[128,768]{1,0:T(8,128)(2,1)S(1)} %get-tuple-element.97), channel_id=1, source_target_pairs={{0,16},{8,24},{16,0},{24,8},{1,17},{9,25},{17,1},{25,9},{2,18},{10... | collective-permute-start | bytes 589832 | tf_op jit(solution)/shard_map/ppermute | solution.py:31
  66.8 12.9 %collective-permute-start.24 = (bf16[128,768]{1,0:T(8,128)(2,1)S(1)}, bf16[128,768]{1,0:T(8,128)(2,1)S(1)}, u32[]{:S(2)}, u32[]{:S(2)}) collective-permute-start(bf16[128,768]{1,0:T(8,128)(2,1)S(1)} %get-tuple-element.96), channel_id=1, source_target_pairs={{0,8},{8,0},{16,24},{24,16},{1,9},{9,1},{17,25},{25,17},{2,10},{10... | collective-permute-start | bytes 589832 | tf_op jit(solution)/shard_map/ppermute | solution.py:31
  67.7 12.0 %collective-permute-start.26 = (bf16[128,768]{1,0:T(8,128)(2,1)S(1)}, bf16[128,768]{1,0:T(8,128)(2,1)S(1)}, u32[]{:S(2)}, u32[]{:S(2)}) collective-permute-start(bf16[128,768]{1,0:T(8,128)(2,1)S(1)} %get-tuple-element.98), channel_id=1, source_target_pairs={{0,24},{8,16},{16,8},{24,0},{1,25},{9,17},{17,9},{25,1},{2,26},{10... | collective-permute-start | bytes 589832 | tf_op jit(solution)/shard_map/ppermute | solution.py:31
  70.1 8.6 %collective-permute-start.28 = (bf16[64,512]{1,0:T(8,128)(2,1)S(1)}, bf16[64,512]{1,0:T(8,128)(2,1)S(1)}, u32[]{:S(2)}, u32[]{:S(2)}) collective-permute-start(bf16[64,512]{1,0:T(8,128)(2,1)S(1)} %get-tuple-element.102), channel_id=1, source_target_pairs={{0,8},{8,0},{16,24},{24,16},{1,9},{9,1},{17,25},{25,17},{2,10},{10... | collective-permute-start | bytes 196616 | tf_op jit(solution)/shard_map/ppermute | solution.py:31
  72.6 6.4 %collective-permute-start.29 = (bf16[64,512]{1,0:T(8,128)(2,1)S(1)}, bf16[64,512]{1,0:T(8,128)(2,1)S(1)}, u32[]{:S(2)}, u32[]{:S(2)}) collective-permute-start(bf16[64,512]{1,0:T(8,128)(2,1)S(1)} %get-tuple-element.103), channel_id=1, source_target_pairs={{0,16},{8,24},{16,0},{24,8},{1,17},{9,25},{17,1},{25,9},{2,18},{10... | collective-permute-start | bytes 196616 | tf_op jit(solution)/shard_map/ppermute | solution.py:31
  (10 other events, 54.7 us)

commit v8 on v7

--- a/solution.py
+++ b/solution.py
@@ -357,7 +357,7 @@
     goes[...] = total[half:, :]
 
 
-def weigh(rows_ref, out):
+def weigh(rows_ref, out, rounded):
     width = rows_ref.shape[1] // 3
     for head in range(width // HDIM):
         at = head * HDIM
@@ -365,13 +365,15 @@
         keys = rows_ref[:, width + at : width + at + HDIM]
         scores = product(queries, keys, 1, 1) * ROOT
         exponent = jnp.exp(scores - jnp.max(scores, axis=1, keepdims=True))
-        out[head] = exponent * (1.0 / jnp.sum(exponent, axis=1, keepdims=True))
+        weights = exponent * (1.0 / jnp.sum(exponent, axis=1, keepdims=True))
+        out[head] = weights
+        rounded[head] = weights.astype(BF16)
 
 
 def attend_back(groups, *refs):
-    rows_ref, weights_ref = refs[:2]
-    upstream = refs[2 : groups + 2]
-    outs = refs[groups + 2 : -2]
+    rows_ref, weights_ref, probs_ref = refs[:3]
+    upstream = refs[3 : groups + 3]
+    outs = refs[groups + 3 : -2]
     grads, result = refs[-2:]
     me = lax.axis_index("fsdp")
     width = upstream[0].shape[1]
@@ -398,7 +400,7 @@
             product(grad_scores, queries, 0, 0) * ROOT
         ).astype(BF16)
         result[:, 2 * width + at : 2 * width + at + HDIM] = product(
-            weights.astype(BF16), above, 0, 0
+            probs_ref[head], above, 0, 0
         ).astype(BF16)
     for k in range(groups):
         piece = result[block(me ^ k, local, local), :]
@@ -627,7 +629,8 @@
         flops=conv_flops,
     )
     whole, projected, slope = outs[:3]
-    (weights,) = call(weigh, [((width // HDIM, frames, frames), F32)], held)
+    square = (width // HDIM, frames, frames)
+    weights, probs = call(weigh, [(square, F32), (square, BF16)], held)
     ahead = exchange_split(outs[3:], after=[weights])
 
     outs = call(
@@ -664,6 +667,7 @@
         split(3 * width) if SPLIT_BACK else [((local, 3 * width), BF16)] * groups,
         held,
         weights,
+        probs,
         *above,
         scratch=[pltpu.VMEM((frames, width), BF16), pltpu.VMEM((frames, 3 * width), BF16)],
         flops=BACK_COST * frames * frames * width,

time: 81.2 us -> 81.8 us (level)
  waiting for transfers between devices: 25 us -> 26.2 us
    ppermute x32, waiting for transfers between devices: 25 us -> 26.2 us  [swap(): return lax.ppermute(cells, axis, [(i, i ^ mask) for i in range(count)])]
  transfers between devices with their start and end apart: 32 -> 32, of which waited for: 15 -> 13; matrix products, arithmetic and copies ran while one was open for 0% -> 0% of each run, Pallas kernels for 16% -> 16%
where the time goes in v8:
time: 81.8 us; the launch traced here: 81.7 us
  starting transfers between devices  36.7 us (45%)
  waiting for transfers between devices  26.2 us (32%)
  Pallas kernels  17.8 us (22%)
  between operations  0.87 us (1%)
    ppermute x32, starting transfers between devices, swap(): return lax.ppermute(cells, axis, [(i, i ^ mask) for i in range(count)])  36.7 us
    ppermute x32, waiting for transfers between devices, swap(): return lax.ppermute(cells, axis, [(i, i ^ mask) for i in range(count)])  26.2 us
    pallas_call x23, Pallas kernels, call(): pl.pallas_call(lambda *refs: body(*refs[:count], *refs[count + len(after)...  17.8 us
  transfers between devices with their start and end apart: 32, of which 13 were waited for; matrix products, arithmetic and copies ran while one was open for 0% of the time, Pallas kernels for 16%

profile of v8, /device:TPU:0, one launch (start us, length us, event | category | flops | bytes accessed | tf_op | source)
XLA Modules:
  0.0 81.7 jit_solution(4610856918607377495)
XLA Ops:
  1.9 3.0 %collective-permute-start = (bf16[112,1024]{1,0:T(8,128)(2,1)S(1)}, bf16[112,1024]{1,0:T(8,128)(2,1)S(1)}, u32[]{:S(2)}, u32[]{:S(2)}) collective-permute-start(bf16[112,1024]{1,0:T(8,128)(2,1)S(1)} %get-tuple-element.62), channel_id=1, source_target_pairs={{0,8},{8,0},{16,24},{24,16},{1,9},{9,1},{17,25},{25,17},{2,10},{10... | collective-permute-start | bytes 688136 | tf_op jit(solution)/shard_map/ppermute | solution.py:31
  4.9 1.5 %collective-permute-start.1 = (bf16[112,1024]{1,0:T(8,128)(2,1)S(1)}, bf16[112,1024]{1,0:T(8,128)(2,1)S(1)}, u32[]{:S(2)}, u32[]{:S(2)}) collective-permute-start(bf16[112,1024]{1,0:T(8,128)(2,1)S(1)} %get-tuple-element.63), channel_id=1, source_target_pairs={{0,16},{8,24},{16,0},{24,8},{1,17},{9,25},{17,1},{25,9},{2,18},{10... | collective-permute-start | bytes 688136 | tf_op jit(solution)/shard_map/ppermute | solution.py:31
  6.5 4.9 %collective-permute-done.refs_1_ = bf16[112,1024]{1,0:T(8,128)(2,1)S(1)} collective-permute-done((bf16[112,1024]{1,0:T(8,128)(2,1)S(1)}, bf16[112,1024]{1,0:T(8,128)(2,1)S(1)}, u32[]{:S(2)}, u32[]{:S(2)}) %collective-permute-start) | collective-permute-done | bytes 229408 | tf_op jit(solution)/shard_map/ppermute | solution.py:31
  11.4 5.5 %collective-permute-done.1.refs_2_ = bf16[112,1024]{1,0:T(8,128)(2,1)S(1)} collective-permute-done((bf16[112,1024]{1,0:T(8,128)(2,1)S(1)}, bf16[112,1024]{1,0:T(8,128)(2,1)S(1)}, u32[]{:S(2)}, u32[]{:S(2)}) %collective-permute-start.1) | collective-permute-done | bytes 229408 | tf_op jit(solution)/shard_map/ppermute | solution.py:31
  16.9 1.4 %shard_map.110 = (bf16[512,768]{1,0:T(8,128)(2,1)S(1)}, bf16[256,256]{1,0:T(8,128)(2,1)S(1)}, bf16[256,256]{1,0:T(8,128)(2,1)S(1)}, bf16[128,512]{1,0:T(8,128)(2,1)S(1)}) custom-call(bf16[112,1024]{1,0:T(8,128)(2,1)S(1)} %get-tuple-element.61.refs_0_, bf16[112,1024]{1,0:T(8,128)(2,1)S(1)} %collective-permute-done.refs_1_, ...), custom_call_target="tpu_custom_call" | custom-call | flops 1610612736 | bytes 2097152 | tf_op jit(solution)/shard_map/pallas_call | solution.py:55
  20.4 1.6 %collective-permute-start.8 = (bf16[128,512]{1,0:T(8,128)(2,1)S(1)}, bf16[128,512]{1,0:T(8,128)(2,1)S(1)}, u32[]{:S(2)}, u32[]{:S(2)}) collective-permute-start(bf16[128,512]{1,0:T(8,128)(2,1)S(1)} %get-tuple-element.67.refs_0_), channel_id=1, source_target_pairs={{0,2},{1,3},{2,0},{3,1},{4,6},{5,7},{6,4},{7,5},{8,10},{9,11},{10,... | collective-permute-start | bytes 393224 | tf_op jit(solution)/shard_map/ppermute | solution.py:31
  22.0 2.6 %collective-permute-start.7 = (bf16[128,512]{1,0:T(8,128)(2,1)S(1)}, bf16[128,512]{1,0:T(8,128)(2,1)S(1)}, u32[]{:S(2)}, u32[]{:S(2)}) collective-permute-start(bf16[128,512]{1,0:T(8,128)(2,1)S(1)} %get-tuple-element.67.refs_0_), channel_id=1, source_target_pairs={{0,4},{1,5},{2,6},{3,7},{4,0},{5,1},{6,2},{7,3},{8,12},{9,13},{10,... | collective-permute-start | bytes 393224 | tf_op jit(solution)/shard_map/ppermute | solution.py:31
  29.5 1.5 %collective-permute-start.11 = (bf16[128,512]{1,0:T(8,128)(2,1)S(1)}, bf16[128,512]{1,0:T(8,128)(2,1)S(1)}, u32[]{:S(2)}, u32[]{:S(2)}) collective-permute-start(bf16[128,512]{1,0:T(8,128)(2,1)S(1)} %get-tuple-element.69), channel_id=1, source_target_pairs={{0,16},{8,24},{16,0},{24,8},{1,17},{9,25},{17,1},{25,9},{2,18},{10... | collective-permute-start | bytes 393224 | tf_op jit(solution)/shard_map/ppermute | solution.py:31
  31.0 3.4 %collective-permute-done.9.refs_3_ = bf16[128,512]{1,0:T(8,128)(2,1)S(1)} collective-permute-done((bf16[128,512]{1,0:T(8,128)(2,1)S(1)}, bf16[128,512]{1,0:T(8,128)(2,1)S(1)}, u32[]{:S(2)}, u32[]{:S(2)}) %collective-permute-start.9) | collective-permute-done | bytes 131104 | tf_op jit(solution)/shard_map/ppermute | solution.py:31
  34.7 1.7 %collective-permute-start.17 = (bf16[128,512]{1,0:T(8,128)(2,1)S(1)}, bf16[128,512]{1,0:T(8,128)(2,1)S(1)}, u32[]{:S(2)}, u32[]{:S(2)}) collective-permute-start(bf16[128,512]{1,0:T(8,128)(2,1)S(1)} %get-tuple-element.80), channel_id=1, source_target_pairs={{0,24},{8,16},{16,8},{24,0},{1,25},{9,17},{17,9},{25,1},{2,26},{10... | collective-permute-start | bytes 393224 | tf_op jit(solution)/shard_map/ppermute | solution.py:31
  36.7 3.4 %shard_map.116 = (bf16[512,1024]{1,0:T(8,128)(2,1)S(1)}, bf16[512,512]{1,0:T(8,128)(2,1)S(1)}, f32[512,512]{1,0:T(8,128)S(1)}, bf16[128,512]{1,0:T(8,128)(2,1)S(...) custom-call(bf16[256,256]{1,0:T(8,128)(2,1)S(1)} %get-tuple-element., ...), custom_call_target="tpu_custom_call" | custom-call | flops 4875878400 | bytes 5369856 | tf_op jit(solution)/shard_map/pallas_call | solution.py:55
  40.1 1.8 %collective-permute-start.13 = (bf16[128,512]{1,0:T(8,128)(2,1)S(1)}, bf16[128,512]{1,0:T(8,128)(2,1)S(1)}, u32[]{:S(2)}, u32[]{:S(2)}) collective-permute-start(bf16[128,512]{1,0:T(8,128)(2,1)S(1)} %get-tuple-element.71), channel_id=1, source_target_pairs={{0,8},{8,0},{16,24},{24,16},{1,9},{9,1},{17,25},{25,17},{2,10},{10... | collective-permute-start | bytes 393224 | tf_op jit(solution)/shard_map/ppermute | solution.py:31
  42.4 5.4 %shard_map.121 = (bf16[512,512]{1,0:T(8,128)(2,1)S(1)}, f32[32,512]{1,0:T(8,128)S(1)}, bf16[512,256]{1,0:T(8,128)(2,1)S(1)}, bf16[512,256]{1,0:T(8,128)(2,1)S(1)...) custom-call(bf16[128,512]{1,0:T(8,128)(2,1)S(1)} %get-tuple-element.79.refs_0_, ...), custom_call_target="tpu_custom_call" | custom-call | flops 7313817600 | bytes 4911104 | tf_op jit(solution)/shard_map/pallas_call | solution.py:55
  50.8 1.8 %collective-permute-start.23 = (bf16[288,512]{1,0:T(8,128)(2,1)S(1)}, bf16[288,512]{1,0:T(8,128)(2,1)S(1)}, u32[]{:S(2)}, u32[]{:S(2)}) collective-permute-start(bf16[288,512]{1,0:T(8,128)(2,1)S(1)} %get-tuple-element.97), channel_id=1, source_target_pairs={{0,2},{1,3},{2,0},{3,1},{4,6},{5,7},{6,4},{7,5},{8,10},{9,11},{10,... | collective-permute-start | bytes 884744 | tf_op jit(solution)/shard_map/ppermute | solution.py:31
  53.5 1.4 %collective-permute-start.14 = (bf16[128,512]{1,0:T(8,128)(2,1)S(1)}, bf16[128,512]{1,0:T(8,128)(2,1)S(1)}, u32[]{:S(2)}, u32[]{:S(2)}) collective-permute-start(bf16[128,512]{1,0:T(8,128)(2,1)S(1)} %shard_map.118), channel_id=1, source_target_pairs={{0,16},{8,24},{16,0},{24,8},{1,17},{9,25},{17,1},{25,9},{2,18},{10... | collective-permute-start | bytes 393224 | tf_op jit(solution)/shard_map/ppermute | solution.py:31
  55.6 2.0 %collective-permute-done.18.refs_1_ = bf16[512,256]{1,0:T(8,128)(2,1)S(1)} collective-permute-done((bf16[512,256]{1,0:T(8,128)(2,1)S(1)}, bf16[512,256]{1,0:T(8,128)(2,1)S(1)}, u32[]{:S(2)}, u32[]{:S(2)}) %collective-permute-start.18) | collective-permute-done | bytes 262176 | tf_op jit(solution)/shard_map/ppermute | solution.py:31
  57.7 1.8 %collective-permute-start.19 = (bf16[256,256]{1,0:T(8,128)(2,1)S(1)}, bf16[256,256]{1,0:T(8,128)(2,1)S(1)}, u32[]{:S(2)}, u32[]{:S(2)}) collective-permute-start(bf16[256,256]{1,0:T(8,128)(2,1)S(1)} %get-tuple-element.86), channel_id=1, source_target_pairs={{0,16},{8,24},{16,0},{24,8},{1,17},{9,25},{17,1},{25,9},{2,18},{10... | collective-permute-start | bytes 393224 | tf_op jit(solution)/shard_map/ppermute | solution.py:31
  60.1 2.9 %collective-permute-start.27 = (bf16[160,512]{1,0:T(8,128)(2,1)S(1)}, bf16[160,512]{1,0:T(8,128)(2,1)S(1)}, u32[]{:S(2)}, u32[]{:S(2)}) collective-permute-start(bf16[160,512]{1,0:T(8,128)(2,1)S(1)} %get-tuple-element.98.refs_7_), channel_id=1, source_target_pairs={{0,4},{1,5},{2,6},{3,7},{4,0},{5,1},{6,2},{7,3},{8,12},{9,13},{10,... | collective-permute-start | bytes 491528 | tf_op jit(solution)/shard_map/ppermute | solution.py:31
  64.6 1.9 %shard_map.127 = (bf16[128,768]{1,0:T(8,128)(2,1)S(1)}, bf16[128,768]{1,0:T(8,128)(2,1)S(1)}, bf16[128,768]{1,0:T(8,128)(2,1)S(1)}, bf16[128,768]{1,0:T(8,128)(2,1)S(1)}) custom-call(bf16[512,768]{1,0:T(8,128)(2,1)S(1)} %get-tuple-element.73.refs_0_, f32[2,512,512]{2,1,0:T(8,128)S(1)} %get-tuple-element.74.refs_2_.refs_1_, ...), custom_call_target="tpu_custom_call" | custom-call | flops 3221225472 | bytes 5242880 | tf_op jit(solution)/shard_map/pallas_call | solution.py:55
  66.8 1.7 %collective-permute-start.24 = (bf16[128,768]{1,0:T(8,128)(2,1)S(1)}, bf16[128,768]{1,0:T(8,128)(2,1)S(1)}, u32[]{:S(2)}, u32[]{:S(2)}) collective-permute-start(bf16[128,768]{1,0:T(8,128)(2,1)S(1)} %get-tuple-element.100), channel_id=1, source_target_pairs={{0,8},{8,0},{16,24},{24,16},{1,9},{9,1},{17,25},{25,17},{2,10},{10... | collective-permute-start | bytes 589832 | tf_op jit(solution)/shard_map/ppermute | solution.py:31
  68.5 1.5 %collective-permute-start.26 = (bf16[128,768]{1,0:T(8,128)(2,1)S(1)}, bf16[128,768]{1,0:T(8,128)(2,1)S(1)}, u32[]{:S(2)}, u32[]{:S(2)}) collective-permute-start(bf16[128,768]{1,0:T(8,128)(2,1)S(1)} %get-tuple-element.102), channel_id=1, source_target_pairs={{0,24},{8,16},{16,8},{24,0},{1,25},{9,17},{17,9},{25,1},{2,26},{10... | collective-permute-start | bytes 589832 | tf_op jit(solution)/shard_map/ppermute | solution.py:31
  71.6 2.3 %collective-permute-done.25.refs_2_ = bf16[128,768]{1,0:T(8,128)(2,1)S(1)} collective-permute-done((bf16[128,768]{1,0:T(8,128)(2,1)S(1)}, bf16[128,768]{1,0:T(8,128)(2,1)S(1)}, u32[]{:S(2)}, u32[]{:S(2)}) %collective-permute-start.25) | collective-permute-done | bytes 196640 | tf_op jit(solution)/shard_map/ppermute | solution.py:31
  73.9 1.5 %collective-permute-start.31 = (bf16[64,512]{1,0:T(8,128)(2,1)S(1)}, bf16[64,512]{1,0:T(8,128)(2,1)S(1)}, u32[]{:S(2)}, u32[]{:S(2)}) collective-permute-start(bf16[64,512]{1,0:T(8,128)(2,1)S(1)} %shard_map.129), channel_id=1, source_target_pairs={{0,24},{8,16},{16,8},{24,0},{1,25},{9,17},{17,9},{25,1},{2,26},{10... | collective-permute-start | bytes 196616 | tf_op jit(solution)/shard_map/ppermute | solution.py:31
  75.4 3.3 %collective-permute-done.28.refs_1_ = bf16[64,512]{1,0:T(8,128)(2,1)S(1)} collective-permute-done((bf16[64,512]{1,0:T(8,128)(2,1)S(1)}, bf16[64,512]{1,0:T(8,128)(2,1)S(1)}, u32[]{:S(2)}, u32[]{:S(2)}) %collective-permute-start.28) | collective-permute-done | bytes 65568 | tf_op jit(solution)/shard_map/ppermute | solution.py:31
  (67 shorter events, 21.1 us)
Async XLA Ops:
  1.9 9.4 %collective-permute-start = (bf16[112,1024]{1,0:T(8,128)(2,1)S(1)}, bf16[112,1024]{1,0:T(8,128)(2,1)S(1)}, u32[]{:S(2)}, u32[]{:S(2)}) collective-permute-start(bf16[112,1024]{1,0:T(8,128)(2,1)S(1)} %get-tuple-element.62), channel_id=1, source_target_pairs={{0,8},{8,0},{16,24},{24,16},{1,9},{9,1},{17,25},{25,17},{2,10},{10... | collective-permute-start | bytes 688136 | tf_op jit(solution)/shard_map/ppermute | solution.py:31
  4.9 12.0 %collective-permute-start.1 = (bf16[112,1024]{1,0:T(8,128)(2,1)S(1)}, bf16[112,1024]{1,0:T(8,128)(2,1)S(1)}, u32[]{:S(2)}, u32[]{:S(2)}) collective-permute-start(bf16[112,1024]{1,0:T(8,128)(2,1)S(1)} %get-tuple-element.63), channel_id=1, source_target_pairs={{0,16},{8,24},{16,0},{24,8},{1,17},{9,25},{17,1},{25,9},{2,18},{10... | collective-permute-start | bytes 688136 | tf_op jit(solution)/shard_map/ppermute | solution.py:31
  6.5 10.5 %collective-permute-start.2 = (bf16[112,1024]{1,0:T(8,128)(2,1)S(1)}, bf16[112,1024]{1,0:T(8,128)(2,1)S(1)}, u32[]{:S(2)}, u32[]{:S(2)}) collective-permute-start(bf16[112,1024]{1,0:T(8,128)(2,1)S(1)} %get-tuple-element.64), channel_id=1, source_target_pairs={{0,24},{8,16},{16,8},{24,0},{1,25},{9,17},{17,9},{25,1},{2,26},{10... | collective-permute-start | bytes 688136 | tf_op jit(solution)/shard_map/ppermute | solution.py:31
  18.3 6.3 %collective-permute-start.3 = (bf16[256,256]{1,0:T(8,128)(2,1)S(1)}, bf16[256,256]{1,0:T(8,128)(2,1)S(1)}, u32[]{:S(2)}, u32[]{:S(2)}) collective-permute-start(bf16[256,256]{1,0:T(8,128)(2,1)S(1)} %get-tuple-element.65.refs_0_), channel_id=1, source_target_pairs={{0,8},{8,0},{16,24},{24,16},{1,9},{9,1},{17,25},{25,17},{2,10},{10... | collective-permute-start | bytes 393224 | tf_op jit(solution)/shard_map/ppermute | solution.py:31
  19.6 6.3 %collective-permute-start.5 = (bf16[256,256]{1,0:T(8,128)(2,1)S(1)}, bf16[256,256]{1,0:T(8,128)(2,1)S(1)}, u32[]{:S(2)}, u32[]{:S(2)}) collective-permute-start(bf16[256,256]{1,0:T(8,128)(2,1)S(1)} %get-tuple-element.66.refs_0_.refs_3_), channel_id=1, source_target_pairs={{0,16},{8,24},{16,0},{24,8},{1,17},{9,25},{17,1},{25,9},{2,18},{10... | collective-permute-start | bytes 393224 | tf_op jit(solution)/shard_map/ppermute | solution.py:31
  20.4 9.1 %collective-permute-start.8 = (bf16[128,512]{1,0:T(8,128)(2,1)S(1)}, bf16[128,512]{1,0:T(8,128)(2,1)S(1)}, u32[]{:S(2)}, u32[]{:S(2)}) collective-permute-start(bf16[128,512]{1,0:T(8,128)(2,1)S(1)} %get-tuple-element.67.refs_0_), channel_id=1, source_target_pairs={{0,2},{1,3},{2,0},{3,1},{4,6},{5,7},{6,4},{7,5},{8,10},{9,11},{10,... | collective-permute-start | bytes 393224 | tf_op jit(solution)/shard_map/ppermute | solution.py:31
  22.0 7.4 %collective-permute-start.7 = (bf16[128,512]{1,0:T(8,128)(2,1)S(1)}, bf16[128,512]{1,0:T(8,128)(2,1)S(1)}, u32[]{:S(2)}, u32[]{:S(2)}) collective-permute-start(bf16[128,512]{1,0:T(8,128)(2,1)S(1)} %get-tuple-element.67.refs_0_), channel_id=1, source_target_pairs={{0,4},{1,5},{2,6},{3,7},{4,0},{5,1},{6,2},{7,3},{8,12},{9,13},{10,... | collective-permute-start | bytes 393224 | tf_op jit(solution)/shard_map/ppermute | solution.py:31
  24.6 10.0 %collective-permute-start.4 = (bf16[512,256]{1,0:T(8,128)(2,1)S(1)}, bf16[512,256]{1,0:T(8,128)(2,1)S(1)}, u32[]{:S(2)}, u32[]{:S(2)}) collective-permute-start(bf16[512,256]{1,0:T(8,128)(2,1)S(1)} %shard_map.111), channel_id=1, source_target_pairs={{0,16},{8,24},{16,0},{24,8},{1,17},{9,25},{17,1},{25,9},{2,18},{10... | collective-permute-start | bytes 786440 | tf_op jit(solution)/shard_map/ppermute | solution.py:31
  25.9 8.7 %collective-permute-start.6 = (bf16[512,256]{1,0:T(8,128)(2,1)S(1)}, bf16[512,256]{1,0:T(8,128)(2,1)S(1)}, u32[]{:S(2)}, u32[]{:S(2)}) collective-permute-start(bf16[512,256]{1,0:T(8,128)(2,1)S(1)} %shard_map.112), channel_id=1, source_target_pairs={{0,8},{8,0},{16,24},{24,16},{1,9},{9,1},{17,25},{25,17},{2,10},{10... | collective-permute-start | bytes 786440 | tf_op jit(solution)/shard_map/ppermute | solution.py:31
  26.8 7.7 %collective-permute-start.10 = (bf16[128,512]{1,0:T(8,128)(2,1)S(1)}, bf16[128,512]{1,0:T(8,128)(2,1)S(1)}, u32[]{:S(2)}, u32[]{:S(2)}) collective-permute-start(bf16[128,512]{1,0:T(8,128)(2,1)S(1)} %get-tuple-element.68), channel_id=1, source_target_pairs={{0,8},{8,0},{16,24},{24,16},{1,9},{9,1},{17,25},{25,17},{2,10},{10... | collective-permute-start | bytes 393224 | tf_op jit(solution)/shard_map/ppermute | solution.py:31
  34.7 7.7 %collective-permute-start.17 = (bf16[128,512]{1,0:T(8,128)(2,1)S(1)}, bf16[128,512]{1,0:T(8,128)(2,1)S(1)}, u32[]{:S(2)}, u32[]{:S(2)}) collective-permute-start(bf16[128,512]{1,0:T(8,128)(2,1)S(1)} %get-tuple-element.80), channel_id=1, source_target_pairs={{0,24},{8,16},{16,8},{24,0},{1,25},{9,17},{17,9},{25,1},{2,26},{10... | collective-permute-start | bytes 393224 | tf_op jit(solution)/shard_map/ppermute | solution.py:31
  40.1 7.7 %collective-permute-start.13 = (bf16[128,512]{1,0:T(8,128)(2,1)S(1)}, bf16[128,512]{1,0:T(8,128)(2,1)S(1)}, u32[]{:S(2)}, u32[]{:S(2)}) collective-permute-start(bf16[128,512]{1,0:T(8,128)(2,1)S(1)} %get-tuple-element.71), channel_id=1, source_target_pairs={{0,8},{8,0},{16,24},{24,16},{1,9},{9,1},{17,25},{25,17},{2,10},{10... | collective-permute-start | bytes 393224 | tf_op jit(solution)/shard_map/ppermute | solution.py:31
  48.7 8.9 %collective-permute-start.18 = (bf16[512,256]{1,0:T(8,128)(2,1)S(1)}, bf16[512,256]{1,0:T(8,128)(2,1)S(1)}, u32[]{:S(2)}, u32[]{:S(2)}) collective-permute-start(bf16[512,256]{1,0:T(8,128)(2,1)S(1)} %get-tuple-element.84), channel_id=1, source_target_pairs={{0,8},{8,0},{16,24},{24,16},{1,9},{9,1},{17,25},{25,17},{2,10},{10... | collective-permute-start | bytes 786440 | tf_op jit(solution)/shard_map/ppermute | solution.py:31
  50.0 9.6 %collective-permute-start.20 = (bf16[512,256]{1,0:T(8,128)(2,1)S(1)}, bf16[512,256]{1,0:T(8,128)(2,1)S(1)}, u32[]{:S(2)}, u32[]{:S(2)}) collective-permute-start(bf16[512,256]{1,0:T(8,128)(2,1)S(1)} %get-tuple-element.88), channel_id=1, source_target_pairs={{0,16},{8,24},{16,0},{24,8},{1,17},{9,25},{17,1},{25,9},{2,18},{10... | collective-permute-start | bytes 786440 | tf_op jit(solution)/shard_map/ppermute | solution.py:31
  50.8 9.3 %collective-permute-start.23 = (bf16[288,512]{1,0:T(8,128)(2,1)S(1)}, bf16[288,512]{1,0:T(8,128)(2,1)S(1)}, u32[]{:S(2)}, u32[]{:S(2)}) collective-permute-start(bf16[288,512]{1,0:T(8,128)(2,1)S(1)} %get-tuple-element.97), channel_id=1, source_target_pairs={{0,2},{1,3},{2,0},{3,1},{4,6},{5,7},{6,4},{7,5},{8,10},{9,11},{10,... | collective-permute-start | bytes 884744 | tf_op jit(solution)/shard_map/ppermute | solution.py:31
  53.5 9.5 %collective-permute-start.14 = (bf16[128,512]{1,0:T(8,128)(2,1)S(1)}, bf16[128,512]{1,0:T(8,128)(2,1)S(1)}, u32[]{:S(2)}, u32[]{:S(2)}) collective-permute-start(bf16[128,512]{1,0:T(8,128)(2,1)S(1)} %shard_map.118), channel_id=1, source_target_pairs={{0,16},{8,24},{16,0},{24,8},{1,17},{9,25},{17,1},{25,9},{2,18},{10... | collective-permute-start | bytes 393224 | tf_op jit(solution)/shard_map/ppermute | solution.py:31
  54.9 8.1 %collective-permute-start.16 = (bf16[128,512]{1,0:T(8,128)(2,1)S(1)}, bf16[128,512]{1,0:T(8,128)(2,1)S(1)}, u32[]{:S(2)}, u32[]{:S(2)}) collective-permute-start(bf16[128,512]{1,0:T(8,128)(2,1)S(1)} %shard_map.119), channel_id=1, source_target_pairs={{0,8},{8,0},{16,24},{24,16},{1,9},{9,1},{17,25},{25,17},{2,10},{10... | collective-permute-start | bytes 393224 | tf_op jit(solution)/shard_map/ppermute | solution.py:31
  57.7 6.3 %collective-permute-start.19 = (bf16[256,256]{1,0:T(8,128)(2,1)S(1)}, bf16[256,256]{1,0:T(8,128)(2,1)S(1)}, u32[]{:S(2)}, u32[]{:S(2)}) collective-permute-start(bf16[256,256]{1,0:T(8,128)(2,1)S(1)} %get-tuple-element.86), channel_id=1, source_target_pairs={{0,16},{8,24},{16,0},{24,8},{1,17},{9,25},{17,1},{25,9},{2,18},{10... | collective-permute-start | bytes 393224 | tf_op jit(solution)/shard_map/ppermute | solution.py:31
  60.1 10.8 %collective-permute-start.27 = (bf16[160,512]{1,0:T(8,128)(2,1)S(1)}, bf16[160,512]{1,0:T(8,128)(2,1)S(1)}, u32[]{:S(2)}, u32[]{:S(2)}) collective-permute-start(bf16[160,512]{1,0:T(8,128)(2,1)S(1)} %get-tuple-element.98.refs_7_), channel_id=1, source_target_pairs={{0,4},{1,5},{2,6},{3,7},{4,0},{5,1},{6,2},{7,3},{8,12},{9,13},{10,... | collective-permute-start | bytes 491528 | tf_op jit(solution)/shard_map/ppermute | solution.py:31
  66.5 7.4 %collective-permute-start.25 = (bf16[128,768]{1,0:T(8,128)(2,1)S(1)}, bf16[128,768]{1,0:T(8,128)(2,1)S(1)}, u32[]{:S(2)}, u32[]{:S(2)}) collective-permute-start(bf16[128,768]{1,0:T(8,128)(2,1)S(1)} %get-tuple-element.101), channel_id=1, source_target_pairs={{0,16},{8,24},{16,0},{24,8},{1,17},{9,25},{17,1},{25,9},{2,18},{10... | collective-permute-start | bytes 589832 | tf_op jit(solution)/shard_map/ppermute | solution.py:31
  66.8 13.5 %collective-permute-start.24 = (bf16[128,768]{1,0:T(8,128)(2,1)S(1)}, bf16[128,768]{1,0:T(8,128)(2,1)S(1)}, u32[]{:S(2)}, u32[]{:S(2)}) collective-permute-start(bf16[128,768]{1,0:T(8,128)(2,1)S(1)} %get-tuple-element.100), channel_id=1, source_target_pairs={{0,8},{8,0},{16,24},{24,16},{1,9},{9,1},{17,25},{25,17},{2,10},{10... | collective-permute-start | bytes 589832 | tf_op jit(solution)/shard_map/ppermute | solution.py:31
  68.5 11.8 %collective-permute-start.26 = (bf16[128,768]{1,0:T(8,128)(2,1)S(1)}, bf16[128,768]{1,0:T(8,128)(2,1)S(1)}, u32[]{:S(2)}, u32[]{:S(2)}) collective-permute-start(bf16[128,768]{1,0:T(8,128)(2,1)S(1)} %get-tuple-element.102), channel_id=1, source_target_pairs={{0,24},{8,16},{16,8},{24,0},{1,25},{9,17},{17,9},{25,1},{2,26},{10... | collective-permute-start | bytes 589832 | tf_op jit(solution)/shard_map/ppermute | solution.py:31
  71.0 7.7 %collective-permute-start.28 = (bf16[64,512]{1,0:T(8,128)(2,1)S(1)}, bf16[64,512]{1,0:T(8,128)(2,1)S(1)}, u32[]{:S(2)}, u32[]{:S(2)}) collective-permute-start(bf16[64,512]{1,0:T(8,128)(2,1)S(1)} %get-tuple-element.106), channel_id=1, source_target_pairs={{0,8},{8,0},{16,24},{24,16},{1,9},{9,1},{17,25},{25,17},{2,10},{10... | collective-permute-start | bytes 196616 | tf_op jit(solution)/shard_map/ppermute | solution.py:31
  73.9 6.3 %collective-permute-start.31 = (bf16[64,512]{1,0:T(8,128)(2,1)S(1)}, bf16[64,512]{1,0:T(8,128)(2,1)S(1)}, u32[]{:S(2)}, u32[]{:S(2)}) collective-permute-start(bf16[64,512]{1,0:T(8,128)(2,1)S(1)} %shard_map.129), channel_id=1, source_target_pairs={{0,24},{8,16},{16,8},{24,0},{1,25},{9,17},{17,9},{25,1},{2,26},{10... | collective-permute-start | bytes 196616 | tf_op jit(solution)/shard_map/ppermute | solution.py:31
  (10 other events, 53.3 us)
